TPU v7x, 32 devices: a whole 2x2x4 slice. The times are simulated.
32 devices in a mesh: shard: 2 (over x), heads: 4 (over y, core), tensor: 4 (over z).
Axes of the slice: x: 2, y: 2, z: 4, core: 2. Of those that a mesh axis runs over, the one named last changes fastest.
Arguments:
- tokens: bfloat16 [12608, 768], P(('shard', 'heads', 'tensor')), may hold values from -6 to 6
- ln1_gain: bfloat16 [768], P('shard'), may hold values from 0.5 to 1.5
- ln1_bias: bfloat16 [768], P('shard'), may hold values from -2 to 2
- qkv_weight: bfloat16 [768, 2304], P('shard'), may hold values from -0.21875 to 0.21875
- out_weight: bfloat16 [768, 768], P('shard'), may hold values from -1.75 to 1.75
- ln2_gain: bfloat16 [768], P('shard'), may hold values from 0.5 to 1.5
- ln2_bias: bfloat16 [768], P('shard'), may hold values from -2 to 2
- router_weight: bfloat16 [768, 8], P('shard'), may hold values from -0.109375 to 0.109375
- expert_in: bfloat16 [8, 768, 3072], P(None, 'shard', 'tensor'), may hold values from -0.21875 to 0.21875
- expert_out: bfloat16 [8, 3072, 768], P(None, 'tensor', 'shard'), may hold values from -0.4375 to 0.4375
- route_noise: float32 [12608, 8], P(('shard', 'heads', 'tensor')), may hold values from -3 to 3
- expert_ids: int32 [12608, 2], P(('shard', 'heads', 'tensor')), may hold values from 0 to 7, all different within a row
- cotangent: bfloat16 [12608, 768], P(('shard', 'heads', 'tensor')), may hold values from -6 to 6
Outputs:
- mixed: bfloat16 [12608, 768], P(('shard', 'heads', 'tensor'))
- grad_tokens: bfloat16 [12608, 768], P(('shard', 'heads', 'tensor'))
- grad_ln1_gain: float32 [768], P('shard')
- grad_ln1_bias: float32 [768], P('shard')
- grad_qkv_weight: float32 [768, 2304], P('shard')
- grad_out_weight: float32 [768, 768], P('shard')
- grad_ln2_gain: float32 [768], P('shard')
- grad_ln2_bias: float32 [768], P('shard')
- grad_router_weight: float32 [768, 8], P('shard')
- grad_expert_in: float32 [8, 768, 3072], P(None, 'shard', 'tensor')
- grad_expert_out: float32 [8, 3072, 768], P(None, 'tensor', 'shard')
Inputs may be any that keep to these rules, and one draw needn't show every extreme that they name: `expert_ids`: each row names 2 different experts.
All inputs are finite; a program needn't handle non-finite values.
Results may differ from a plain program's by a relative error of at most 0.02.
Values may be sent and summed in bfloat16 or wider, within the bound.
A program may use at most 320 MiB of HBM per device.

v0:
```python
import jax
import jax.numpy as jnp
from jax import lax
from jax.sharding import PartitionSpec as P

HEAD_DIM = 64
SEQ = 197


EPS = 1e-06
HIGH = lax.Precision.HIGHEST


def layer_norm(values, gain, bias):
    mean = jnp.mean(values, -1, keepdims=True)
    centred = values - mean
    spread = jnp.mean(centred * centred, -1, keepdims=True)
    return centred * lax.rsqrt(spread + EPS) * gain + bias


def route_gates(normed, router, noise, chosen):
    logits = jnp.dot(normed, router, precision=HIGH) + noise
    return jax.nn.softmax(logits, -1) * chosen


def contract_rows(left, right):
    return lax.dot_general(
        left, right, (((0,), (0,)), ((), ())), preferred_element_type=jnp.float32
    )


def contract_cols(left, right):
    return lax.dot_general(
        left, right, (((1,), (1,)), ((), ())), preferred_element_type=jnp.float32
    )


def gather_weights(gain_a, bias_a, proj_qkv, proj_out, gain_b, bias_b, router, inner, outer):
    return (
        lax.all_gather(gain_a, "shard", axis=0, tiled=True),
        lax.all_gather(bias_a, "shard", axis=0, tiled=True),
        lax.all_gather(proj_qkv, "shard", axis=0, tiled=True),
        lax.all_gather(proj_out, "shard", axis=0, tiled=True),
        lax.all_gather(gain_b, "shard", axis=0, tiled=True),
        lax.all_gather(bias_b, "shard", axis=0, tiled=True),
        lax.all_gather(router, "shard", axis=0, tiled=True),
        lax.all_gather(inner, "shard", axis=1, tiled=True),
        lax.all_gather(outer, "shard", axis=2, tiled=True),
    )


def local(
    tokens,
    ln1_gain,
    ln1_bias,
    qkv_weight,
    out_weight,
    ln2_gain,
    ln2_bias,
    router_weight,
    expert_in,
    expert_out,
    route_noise,
    expert_ids,
    cotangent,
):
    groups = lax.axis_size("heads")
    rows = tokens.shape[0]
    width = tokens.shape[1]
    experts = expert_in.shape[0]
    images = rows // SEQ
    head_group = width // HEAD_DIM // groups
    scale = HEAD_DIM ** (-0.5)
    full = gather_weights(
        ln1_gain,
        ln1_bias,
        qkv_weight,
        out_weight,
        ln2_gain,
        ln2_bias,
        router_weight,
        expert_in,
        expert_out,
    )
    gain_a, bias_a, proj_qkv, proj_out, gain_b, bias_b, router, inner, outer = full
    start_x = tokens.astype(jnp.float32)
    first_norm, first_pull = jax.vjp(
        layer_norm, start_x, gain_a.astype(jnp.float32), bias_a.astype(jnp.float32)
    )
    normed_a = first_norm.astype(jnp.bfloat16)
    packed = jnp.dot(normed_a, proj_qkv, preferred_element_type=jnp.float32).astype(jnp.bfloat16)
    packed = packed.reshape(rows, groups, 3 * head_group * HEAD_DIM)
    moved = lax.all_to_all(packed, "heads", split_axis=1, concat_axis=0, tiled=True).reshape(
        groups, images, SEQ, 3, head_group, HEAD_DIM
    )
    query = moved[:, :, :, 0]
    keys = moved[:, :, :, 1]
    values = moved[:, :, :, 2]

    def scores_of():
        return (
            jnp.einsum("gnihd,gnjhd->gnhij", query, keys, preferred_element_type=jnp.float32)
            * scale
        )

    scores = scores_of()
    highest = jnp.max(scores, -1, keepdims=True)
    totals = jnp.sum(jnp.exp(scores - highest), -1, keepdims=True)
    logsum = highest + jnp.log(totals)
    probs = jnp.exp(scores - logsum)
    attended = jnp.einsum(
        "gnhij,gnjhd->gnihd", probs.astype(jnp.bfloat16), values, preferred_element_type=jnp.float32
    ).astype(jnp.bfloat16)
    attended = attended.reshape(groups, rows, head_group * HEAD_DIM)
    returned = lax.all_to_all(attended, "heads", split_axis=0, concat_axis=2, tiled=True).reshape(
        rows, width
    )
    middle = start_x + jnp.dot(returned, proj_out, preferred_element_type=jnp.float32)
    second_norm, second_pull = jax.vjp(
        layer_norm, middle, gain_b.astype(jnp.float32), bias_b.astype(jnp.float32)
    )
    normed_b = second_norm.astype(jnp.bfloat16)
    labels = jnp.arange(experts, dtype=jnp.int32)
    chosen = jnp.sum((expert_ids[:, :, None] == labels[None, None, :]).astype(jnp.float32), 1)

    def gate_function(normed, weight):
        return route_gates(normed, weight, route_noise, chosen)

    gates, gate_pull = jax.vjp(
        gate_function, normed_b.astype(jnp.float32), router.astype(jnp.float32)
    )
    rows_all, gates_all = (
        lax.all_gather(normed_b, "tensor", axis=0, tiled=True),
        lax.all_gather(gates.astype(jnp.bfloat16), "tensor", axis=0, tiled=True),
    )
    part_gates = gates_all.astype(jnp.float32)
    total = jnp.zeros((rows * lax.axis_size("tensor"), width), jnp.float32)
    for expert_expert in range(experts):
        expert_hidden = jnp.dot(rows_all, inner[expert_expert], preferred_element_type=jnp.float32)
        expert_active = (
            jax.nn.gelu(expert_hidden) * part_gates[:, expert_expert : expert_expert + 1]
        ).astype(jnp.bfloat16)
        total = total + jnp.dot(
            expert_active, outer[expert_expert], preferred_element_type=jnp.float32
        )
    moe_out = lax.psum_scatter(
        total.astype(jnp.bfloat16), "tensor", scatter_dimension=0, tiled=True
    ).astype(jnp.float32)
    mixed = (middle + moe_out).astype(jnp.bfloat16)
    full = gather_weights(
        ln1_gain,
        ln1_bias,
        qkv_weight,
        out_weight,
        ln2_gain,
        ln2_bias,
        router_weight,
        expert_in,
        expert_out,
    )
    gain_a, bias_a, proj_qkv, proj_out, gain_b, bias_b, router, inner, outer = full
    grad_out = cotangent.astype(jnp.float32)
    grad_rows = lax.all_gather(cotangent, "tensor", axis=0, tiled=True)
    gates_float = gates_all.astype(jnp.float32)
    grad_rows_in = jnp.zeros((rows_all.shape[0], width), jnp.float32)
    gate_grads = []
    inner_grads = []
    outer_grads = []
    for expert in range(experts):
        hidden = jnp.dot(rows_all, inner[expert], preferred_element_type=jnp.float32)
        activated, gelu_pull = jax.vjp(jax.nn.gelu, hidden)
        gate_column = gates_float[:, expert : expert + 1]
        active = (activated * gate_column).astype(jnp.bfloat16)
        outer_grads.append(contract_rows(active, grad_rows))
        grad_active = contract_cols(grad_rows, outer[expert])
        gate_grads.append(jnp.sum(grad_active * activated, 1))
        grad_hidden = gelu_pull(grad_active * gate_column)[0].astype(jnp.bfloat16)
        inner_grads.append(contract_rows(rows_all, grad_hidden))
        grad_rows_in = grad_rows_in + contract_cols(grad_hidden, inner[expert])
    gate_table = jnp.stack(gate_grads, 1)
    grad_normed_moe, grad_gates = (
        lax.psum_scatter(grad_rows_in, "tensor", scatter_dimension=0, tiled=True),
        lax.psum_scatter(gate_table, "tensor", scatter_dimension=0, tiled=True),
    )
    route_normed, grad_router = gate_pull(grad_gates)
    grad_mid, grad_gain_b, grad_bias_b = second_pull(grad_normed_moe + route_normed)
    grad_middle = grad_out + grad_mid
    grad_proj = grad_middle.astype(jnp.bfloat16)
    grad_proj_out = contract_rows(returned, grad_proj)
    grad_returned = contract_cols(grad_proj, proj_out).astype(jnp.bfloat16)
    grad_attended = lax.all_to_all(
        grad_returned.reshape(1, rows, width), "heads", split_axis=2, concat_axis=0, tiled=True
    )
    grad_attended = grad_attended.reshape(groups, images, SEQ, head_group, HEAD_DIM)
    probs = jnp.exp(scores_of() - logsum)
    grad_values = jnp.einsum(
        "gnhij,gnihd->gnjhd",
        probs.astype(jnp.bfloat16),
        grad_attended,
        preferred_element_type=jnp.float32,
    )
    grad_weights = jnp.einsum(
        "gnihd,gnjhd->gnhij", grad_attended, values, preferred_element_type=jnp.float32
    )
    inner_sum = jnp.sum(probs * grad_weights, -1, keepdims=True)
    grad_scores = (probs * (grad_weights - inner_sum)).astype(jnp.bfloat16)
    grad_query = (
        jnp.einsum("gnhij,gnjhd->gnihd", grad_scores, keys, preferred_element_type=jnp.float32)
        * scale
    )
    grad_keys = (
        jnp.einsum("gnhij,gnihd->gnjhd", grad_scores, query, preferred_element_type=jnp.float32)
        * scale
    )
    grad_stack = jnp.stack((grad_query, grad_keys, grad_values), 3).astype(jnp.bfloat16)
    grad_stack = grad_stack.reshape(groups * rows, 1, 3 * head_group * HEAD_DIM)
    grad_packed = lax.all_to_all(
        grad_stack, "heads", split_axis=0, concat_axis=1, tiled=True
    ).reshape(rows, 3 * width)
    grad_proj_qkv = contract_rows(normed_a, grad_packed)
    grad_normed_a = contract_cols(grad_packed, proj_qkv)
    grad_first, grad_gain_a, grad_bias_a = first_pull(grad_normed_a)
    grad_tokens = (grad_middle + grad_first).astype(jnp.bfloat16)
    shares = (
        lax.psum_scatter(
            grad_gain_a.astype(jnp.bfloat16), "shard", scatter_dimension=0, tiled=True
        ).astype(jnp.float32),
        lax.psum_scatter(
            grad_bias_a.astype(jnp.bfloat16), "shard", scatter_dimension=0, tiled=True
        ).astype(jnp.float32),
        lax.psum_scatter(
            grad_proj_qkv.astype(jnp.bfloat16), "shard", scatter_dimension=0, tiled=True
        ).astype(jnp.float32),
        lax.psum_scatter(
            grad_proj_out.astype(jnp.bfloat16), "shard", scatter_dimension=0, tiled=True
        ).astype(jnp.float32),
        lax.psum_scatter(
            grad_gain_b.astype(jnp.bfloat16), "shard", scatter_dimension=0, tiled=True
        ).astype(jnp.float32),
        lax.psum_scatter(
            grad_bias_b.astype(jnp.bfloat16), "shard", scatter_dimension=0, tiled=True
        ).astype(jnp.float32),
        lax.psum_scatter(
            grad_router.astype(jnp.bfloat16), "shard", scatter_dimension=0, tiled=True
        ).astype(jnp.float32),
        lax.psum_scatter(
            jnp.stack(inner_grads, 0).astype(jnp.bfloat16), "shard", scatter_dimension=1, tiled=True
        ).astype(jnp.float32),
        lax.psum_scatter(
            jnp.stack(outer_grads, 0).astype(jnp.bfloat16), "shard", scatter_dimension=2, tiled=True
        ).astype(jnp.float32),
    )
    dense_sums = (
        lax.psum(shares[0].astype(jnp.bfloat16), ("heads", "tensor")).astype(jnp.float32),
        lax.psum(shares[1].astype(jnp.bfloat16), ("heads", "tensor")).astype(jnp.float32),
        lax.psum(shares[2].astype(jnp.bfloat16), ("heads", "tensor")).astype(jnp.float32),
        lax.psum(shares[3].astype(jnp.bfloat16), ("heads", "tensor")).astype(jnp.float32),
        lax.psum(shares[4].astype(jnp.bfloat16), ("heads", "tensor")).astype(jnp.float32),
        lax.psum(shares[5].astype(jnp.bfloat16), ("heads", "tensor")).astype(jnp.float32),
        lax.psum(shares[6].astype(jnp.bfloat16), ("heads", "tensor")).astype(jnp.float32),
    )
    expert_sums = (
        lax.psum(shares[7].astype(jnp.bfloat16), "heads").astype(jnp.float32),
        lax.psum(shares[8].astype(jnp.bfloat16), "heads").astype(jnp.float32),
    )
    return (
        mixed,
        grad_tokens,
        dense_sums[0],
        dense_sums[1],
        dense_sums[2],
        dense_sums[3],
        dense_sums[4],
        dense_sums[5],
        dense_sums[6],
        expert_sums[0],
        expert_sums[1],
    )


def solution(mesh):
    return jax.shard_map(
        local,
        mesh=mesh,
        in_specs=(
            P(("shard", "heads", "tensor"), None),
            P("shard"),
            P("shard"),
            P("shard", None),
            P("shard", None),
            P("shard"),
            P("shard"),
            P("shard", None),
            P(None, "shard", "tensor"),
            P(None, "tensor", "shard"),
            P(("shard", "heads", "tensor"), None),
            P(("shard", "heads", "tensor"), None),
            P(("shard", "heads", "tensor"), None),
        ),
        out_specs=(
            P(("shard", "heads", "tensor"), None),
            P(("shard", "heads", "tensor"), None),
            P("shard"),
            P("shard"),
            P("shard", None),
            P("shard", None),
            P("shard"),
            P("shard"),
            P("shard", None),
            P(None, "shard", "tensor"),
            P(None, "tensor", "shard"),
        ),
        check_vma=False,
    )
```

profile of v0, /device:TPU:17, one launch (start us, length us, event | category | flops | bytes accessed | tf_op | source)
XLA Modules:
  0.0 1519.4 jit_solution(9204612092862431575)
XLA Ops:
  19.1 40.9 %all-gather.14.cloned.1.call-done = bf16[768,2304]{1,0:T(8,128)(2,1)} async-done(((bf16[384,2304]{1,0:T(8,128)(2,1)}), bf16[768,2304]{1,0:T(8,128)(2,1)}) %all-gather.14.cloned.1.call-update) | async-done | bytes 3538960 | tf_op jit(solution)/shard_map/all_gather | solution.py:42
  76.2 23.7 %all-to-all-done = bf16[394,4,576]{2,0,1:T(8,128)(2,1)S(1)} async-done(((bf16[394,4,576]{2,0,1:T(8,128)(2,1)}), bf16[394,4,576]{2,0,1:T(8,128)(2,1)S(1)}, u32[]{:S(2)}, u32[]{:S(2)}) %all-to-all-start) | async-done | bytes 1815584 | tf_op jit(solution)/shard_map/all_to_all | solution.py:93
  162.8 27.5 %all-gather.22.cloned.1.call-done = bf16[4,394,768]{2,1,0:T(8,128)(2,1)} async-done(((bf16[1,394,768]{2,1,0:T(8,128)(2,1)}), bf16[4,394,768]{2,1,0:T(8,128)(2,1)}) %all-gather.22.cloned.1.call-update) | async-done | bytes 2420752 | tf_op jit(solution)/shard_map/all_gather | solution.py:133
  192.6 117.0 %all-gather.20.cloned.1.call-done = bf16[8,768,768]{2,1,0:T(8,128)(2,1)} async-done(((bf16[8,768,384]{2,1,0:T(8,128)(2,1)}), bf16[8,768,768]{2,1,0:T(8,128)(2,1)}) %all-gather.20.cloned.1.call-update) | async-done | bytes 9437200 | tf_op jit(solution)/shard_map/all_gather | solution.py:48
  334.1 14.2 fusion.129
  357.0 72.0 %all-gather.18.cloned.1.call-done = bf16[8,768,768]{2,1,0:T(8,128)(2,1)} async-done(((bf16[8,384,768]{2,1,0:T(8,128)(2,1)}), bf16[8,768,768]{2,1,0:T(8,128)(2,1)}) %all-gather.18.cloned.1.call-update) | async-done | bytes 9437200 | tf_op jit(solution)/shard_map/all_gather | solution.py:47
  446.8 10.9 fusion.15
  529.8 14.6 add_convert_fusion
  544.4 44.3 %fusion = bf16[400,768]{1,0:T(8,128)(2,1)S(1)} fusion(bf16[1576,768]{1,0:T(8,128)(2,1)S(1)} %add_convert_fusion), kind=kCustom, calls=%all-reduce-scatter | all-reduce-scatter fusion | flops 1228801 | bytes 3035648
  590.9 13.9 all-reduce.2
  635.1 15.0 add_add_fusion
  650.2 83.1 %fusion.1 = f32[400,768]{1,0:T(8,128)S(1)} fusion(f32[1576,768]{1,0:T(8,128)} %add_add_fusion), kind=kCustom, calls=%all-reduce-scatter.1 | all-reduce-scatter fusion | flops 1228801 | bytes 6070784
  815.1 17.5 %reshape.172 = bf16[1576,1,576]{2,1,0:T(2,128)(2,1)} reshape(bf16[4,2,197,3,3,64]{5,4,3,2,1,0:T(4,128)(2,1)} %copy.93) | data formatting | bytes 3631104 | tf_op jit(solution)/shard_map/convert_element_type | solution.py:215
  832.6 14.5 reduce.26
  852.3 27.0 %all_to_all.60 = bf16[4,2,113472]{2,1,0:T(2,128)(2,1)} all-to-all(bf16[4,2,113472]{2,1,0:T(2,128)(2,1)} %reshape.203), channel_id=1, replica_groups=mesh['shard'=2,'heads'=4,'tensor'=4] {'heads'}, dimensions={0} | all-to-all | bytes 3631104 | tf_op jit(solution)/shard_map/all_to_all | solution.py:217
  888.1 13.4 reduce.12
  964.4 13.4 copy.98
  977.8 10.6 copy.109
  1021.7 77.4 %reduce-scatter.23.cloned.1.call-done = bf16[384,6144]{1,0:T(8,128)(2,1)} async-done(((bf16[768,6144]{1,0:T(8,128)(2,1)}), bf16[384,6144]{1,0:T(8,128)(2,1)}) %reduce-scatter.23.cloned.1.call-update) | async-done | bytes 4718608
  1112.0 100.3 %reduce-scatter.19.cloned.1.call-done = bf16[8,384,768]{2,1,0:T(8,128)(2,1)} async-done(((bf16[8,768,768]{2,1,0:T(8,128)(2,1)}), bf16[8,384,768]{2,1,0:T(8,128)(2,1)}) %reduce-scatter.19.cloned.1.call-update) | async-done | bytes 4718608 | tf_op jit(solution)/shard_map/reduce_scatter | solution.py:246
  1213.6 12.5 reduce-scatter.21.cloned.1.call-done
  1237.8 57.3 %all-reduce.9 = (bf16[384]{0:T(512)(128)(2,1)S(1)}, bf16[384]{0:T(512)(128)(2,1)S(1)}, bf16[384]{0:T(512)(128)(2,1)S(1)}, bf16[384]{0:T(512)(128)(2,1)S(1)}, bf16[384,8]{0,1:T(8,128)(2,1)S(1)}) all-reduce(bf16[384]{0:T(512)(128)(2,1)S(1)} %dynamic-slice.7, ...), channel_id=1, replica_groups=mesh['shard'=2,'heads'=4,'tensor'=4] {'heads','tensor'}, use_global_device_ids=true, to_apply=%region_28.0 | all-reduce | flops 4608 | bytes 18432 | tf_op jit(solution)/shard_map/psum | solution.py:254
  1300.7 26.2 %all-reduce.16.cloned.1.call-done = (bf16[384,2304]{1,0:T(8,128)(2,1)}, bf16[384,768]{1,0:T(8,128)(2,1)}) async-done(((bf16[384,2304]{1,0:T(8,128)(2,1)}, bf16[384,768]{1,0:T(8,128)(2,1)}), (bf16[384,2304]{1,0:T(8,128)(2,1)}, bf16[384,768]{1,0:T(8,128)(2,1)})) %all-reduce.16.cloned.1.call-update) | async-done | bytes 2359312 | tf_op jit(solution)/shard_map/psum | solution.py:256
  1331.5 169.4 %all-reduce.18.cloned.1.call-done = (bf16[8,384,768]{2,1,0:T(8,128)(2,1)}, bf16[8,768,384]{2,1,0:T(8,128)(2,1)}) async-done(((bf16[8,384,768]{2,1,0:T(8,128)(2,1)}, bf16[8,768,384]{2,1,0:T(8,128)(2,1)}), (bf16[8,384,768]{2,1,0:T(8,128)(2,1)}, bf16[8,768,384]{2,1,0:T(8,128)(2,1)})) %all-reduce.18.cloned.1.call-update) | async-done | bytes 9437200 | tf_op jit(solution)/shard_map/psum | solution.py:263
  (488 shorter events, 484.8 us)
Async XLA Ops:
  7.2 52.8 %all-gather.14.cloned.1.call-start = ((), (), s32[]{:S(2)}) async-start(), calls=%async_computation.9 | async-start | bytes 5308416 | tf_op jit(solution)/shard_map/all_gather | solution.py:42
  7.9 123.8 %all-gather.16.cloned.1.call-start = ((), (), s32[]{:S(2)}) async-start(), calls=%async_computation.10 | async-start | bytes 1769472 | tf_op jit(solution)/shard_map/all_gather | solution.py:43
  71.2 28.7 %all-to-all-start = ((bf16[394,4,576]{2,0,1:T(8,128)(2,1)}), bf16[394,4,576]{2,0,1:T(8,128)(2,1)S(1)}, u32[]{:S(2)}, u32[]{:S(2)}) async-start(bf16[394,4,576]{2,0,1:T(8,128)(2,1)} %copy.68), calls=%async_computation | async-start | bytes 4096000 | tf_op jit(solution)/shard_map/all_to_all | solution.py:93
  75.5 70.4 %all-gather.24.cloned.1.call-start = ((), (), s32[]{:S(2)}) async-start(), calls=%async_computation.17 | async-start | bytes 3072000 | tf_op jit(solution)/shard_map/all_gather | solution.py:163
  120.5 15.1 all-to-all-start.1
  124.7 65.6 %all-gather.22.cloned.1.call-start = ((), (), s32[]{:S(2)}) async-start(), calls=%async_computation.16 | async-start | bytes 3072000 | tf_op jit(solution)/shard_map/all_gather | solution.py:133
  139.5 170.2 %all-gather.20.cloned.1.call-start = ((), (), s32[]{:S(2)}) async-start(), calls=%async_computation.12 | async-start | bytes 14155776 | tf_op jit(solution)/shard_map/all_gather | solution.py:48
  140.1 289.0 %all-gather.18.cloned.1.call-start = ((), (), s32[]{:S(2)}) async-start(), calls=%async_computation.11 | async-start | bytes 14155776 | tf_op jit(solution)/shard_map/all_gather | solution.py:47
  162.2 277.2 %copy-start.74 = (f32[1576]{0:T(1024)}, f32[1576]{0:T(1024)S(1)}, u32[]{:S(2)}) copy-start(f32[1576]{0:T(1024)S(1)} %get-tuple-element.25) | copy-start | bytes 18916
  162.2 295.5 %copy-start.72 = (f32[1576]{0:T(1024)}, f32[1576]{0:T(1024)S(1)}, u32[]{:S(2)}) copy-start(f32[1576]{0:T(1024)S(1)} %get-tuple-element.24) | copy-start | bytes 18916
  162.2 307.3 %copy-start.70 = (f32[1576]{0:T(1024)}, f32[1576]{0:T(1024)S(1)}, u32[]{:S(2)}) copy-start(f32[1576]{0:T(1024)S(1)} %get-tuple-element.23) | copy-start | bytes 18916
  162.2 318.8 %copy-start.68 = (f32[1576]{0:T(1024)}, f32[1576]{0:T(1024)S(1)}, u32[]{:S(2)}) copy-start(f32[1576]{0:T(1024)S(1)} %get-tuple-element.22) | copy-start | bytes 18916
  162.2 330.7 %copy-start.66 = (f32[1576]{0:T(1024)}, f32[1576]{0:T(1024)S(1)}, u32[]{:S(2)}) copy-start(f32[1576]{0:T(1024)S(1)} %get-tuple-element.21) | copy-start | bytes 18916
  192.6 328.7 %copy-start.20 = (bf16[1576,768]{1,0:T(8,128)(2,1)}, bf16[1576,768]{1,0:T(8,128)(2,1)S(1)}, u32[]{:S(2)}) copy-start(bf16[1576,768]{1,0:T(8,128)(2,1)S(1)} %reshape.162) | copy-start | bytes 7262212
  588.8 146.7 %collective-permute-start = (bf16[18,768]{1,0:T(8,128)(2,1)S(1)}, bf16[18,768]{1,0:T(8,128)(2,1)S(1)}, u32[]{:S(2)}, u32[]{:S(2)}) collective-permute-start(bf16[18,768]{1,0:T(8,128)(2,1)S(1)} %slice.167), channel_id=1, source_target_pairs={{0,1},{1,2},{2,3},{4,5},{5,6},{6,7},{8,9},{9,10},{10,11},{12,13},{... | collective-permute-start | bytes 82952
  733.3 6.4 collective-permute-start.1
  761.9 17.6 %all-to-all-start.2 = ((bf16[4,2,37824]{2,1,0:T(2,128)(2,1)}), bf16[4,2,37824]{2,1,0:T(2,128)(2,1)S(1)}, u32[]{:S(2)}, u32[]{:S(2)}) async-start(bf16[4,2,37824]{2,1,0:T(2,128)(2,1)} %reshape.201), calls=%async_computation.2 | async-start | bytes 1212416 | tf_op jit(solution)/shard_map/all_to_all | solution.py:191
  770.7 250.4 %reduce-scatter.17.cloned.1.call-start = ((), (), s32[]{:S(2)}) async-start(), calls=%async_computation.14 | async-start | bytes 1769472 | tf_op jit(solution)/shard_map/reduce_scatter | solution.py:234
  773.6 247.5 %reduce-scatter.15.cloned.1.call-start = ((), (), s32[]{:S(2)}) async-start(), calls=%async_computation.13 | async-start | bytes 5308416 | tf_op jit(solution)/shard_map/reduce_scatter | solution.py:231
  918.9 180.1 %reduce-scatter.23.cloned.1.call-start = ((), (), s32[]{:S(2)}) async-start(), calls=%async_computation.19 | async-start | bytes 14155776
  988.4 223.9 %reduce-scatter.19.cloned.1.call-start = ((), (), s32[]{:S(2)}) async-start(), calls=%async_computation.15 | async-start | bytes 14155776 | tf_op jit(solution)/shard_map/reduce_scatter | solution.py:246
  1018.8 207.3 %reduce-scatter.21.cloned.1.call-start = ((), (), s32[]{:S(2)}) async-start(), calls=%async_computation.18 | async-start | bytes 294912
  1021.0 305.8 %all-reduce.16.cloned.1.call-start = ((), (), s32[]{:S(2)}) async-start(), calls=%async_computation.20 | async-start | bytes 4718592 | tf_op jit(solution)/shard_map/psum | solution.py:256
  1021.6 479.3 %all-reduce.18.cloned.1.call-start = ((), (), s32[]{:S(2)}) async-start(), calls=%async_computation.21 | async-start | bytes 18874368 | tf_op jit(solution)/shard_map/psum | solution.py:263
  (128 other events, 2216.3 us)
Sparse Core Ops, SparseCore 0:
  9.6 50.4 all-gather.13
  61.6 22.7 all-gather.15
  86.0 50.9 all-gather.23
  139.6 50.6 all-gather.21
  191.7 117.9 all-gather.19
  311.1 117.9 all-gather.17
  774.4 21.5 reduce-scatter.16
  919.0 46.9 reduce-scatter.14
  988.5 110.4 reduce-scatter.22
  1101.7 110.5 reduce-scatter.18
  1215.2 10.9 reduce-scatter.20
  1229.6 97.1 all-reduce.15
  1329.4 171.4 all-reduce.17
where the time goes:
time: 1530 us; the launch traced here: 1520 us
  waiting for transfers between devices  681 us (45%)
  matrix products  315 us (21%)
  blocking collectives  256 us (17%)
  local copies, waits for them, and re-layouts  160 us (10%)
  other arithmetic  67.8 us (4%)
  starting transfers between devices  21.8 us (1%)
  between operations  17.9 us (1%)
    psum x1, waiting for transfers between devices, local(): lax.psum(shares[7].astype(jnp.bfloat16), 'heads').astype(jnp.float32)  169 us
    unnamed x4, blocking collectives  146 us
    all_gather x1, waiting for transfers between devices, gather_weights(): lax.all_gather(outer, 'shard', axis=2, tiled=True)  117 us
    reduce_scatter x1, waiting for transfers between devices, local(): lax.psum_scatter(jnp.stack(inner_grads, 0).astype(jnp.bfloat16), 'shard',...  100 us
    dot_general x18, matrix products, contract_cols(): lax.dot_general(left, right, (((1,), (1,)), ((), ())), preferred_element_...  97.4 us
    unnamed x17, waiting for transfers between devices  93.6 us
    unnamed x298, local copies, waits for them, and re-layouts  87.6 us
    dot_general x18, matrix products, contract_rows(): lax.dot_general(left, right, (((0,), (0,)), ((), ())), preferred_element_...  83.7 us
  transfers between devices with their start and end apart: 18, of which 12 were waited for; matrix products, arithmetic and copies ran while one was open for 31% of the time, Pallas kernels for 0%

commit v1 on v0

v1 whole, which is shorter than its diff:
```python
import jax
import jax.numpy as jnp
from jax import lax
from jax.sharding import PartitionSpec as P

HEAD_DIM = 64
SEQ = 197
EPS = 1e-06
HIGH = lax.Precision.HIGHEST
AXES = ("shard", "heads", "tensor")
BF = jnp.bfloat16
F32 = jnp.float32


def layer_norm(values, gain, bias):
    mean = jnp.mean(values, -1, keepdims=True)
    centred = values - mean
    spread = jnp.mean(centred * centred, -1, keepdims=True)
    return centred * lax.rsqrt(spread + EPS) * gain + bias


def route_gates(normed, router, noise, chosen):
    logits = jnp.dot(normed, router, precision=HIGH) + noise
    return jax.nn.softmax(logits, -1) * chosen


def contract_rows(left, right):
    return lax.dot_general(left, right, (((0,), (0,)), ((), ())), preferred_element_type=F32)


def contract_cols(left, right):
    return lax.dot_general(left, right, (((1,), (1,)), ((), ())), preferred_element_type=F32)


class Comm:
    def __init__(self):
        self.sizes = tuple(lax.axis_size(axis) for axis in AXES)
        self.shard = lax.axis_index("shard")
        self.head = lax.axis_index("heads")
        self.tensor = lax.axis_index("tensor")
        self.pair = self.head % 2

    def move(self, value, step):
        shards, heads, tensors = self.sizes
        pairs = []
        for s in range(shards):
            for h in range(heads):
                for t in range(tensors):
                    to = step(s, h, t)
                    if 0 <= to[2] < tensors:
                        source = (s * heads + h) * tensors + t
                        pairs.append((source, (to[0] * heads + to[1]) * tensors + to[2]))
        return lax.ppermute(value, AXES, pairs)

    def over_core(self, value):
        return self.move(value, lambda s, h, t: (s, h ^ 1, t))

    def over_heads(self, value):
        return self.move(value, lambda s, h, t: (s, (h + 2) % 4, t))

    def over_shard(self, value):
        return self.move(value, lambda s, h, t: (1 - s, h, t))

    def up(self, value):
        return self.move(value, lambda s, h, t: (s, h, t + 1))

    def down(self, value):
        return self.move(value, lambda s, h, t: (s, h, t - 1))

    def halves(self, value, index, axis):
        size = value.shape[axis] // 2
        mine = lax.dynamic_slice_in_dim(value, index * size, size, axis)
        other = lax.dynamic_slice_in_dim(value, (1 - index) * size, size, axis)
        return mine, other

    def join(self, mine, other, index, axis):
        first = jnp.where(index == 0, mine, other)
        second = jnp.where(index == 0, other, mine)
        return jnp.concatenate((first, second), axis)

    def gather_shard(self, value, axis):
        if self.sizes[0] != 2:
            return lax.all_gather(value, "shard", axis=axis, tiled=True)
        return self.join(value, self.over_shard(value), self.shard, axis)

    def gather_shard_split(self, value, axis, cut):
        if self.sizes[0] != 2:
            return lax.all_gather(value, "shard", axis=axis, tiled=True)
        mine, _ = self.halves(value, self.pair, cut)
        got = self.over_shard(mine)
        both = self.join(got, self.over_core(got), self.pair, cut)
        return self.join(value, both, self.shard, axis)

    def scatter_shard(self, value, axis):
        if self.sizes[0] != 2:
            return lax.psum_scatter(value.astype(BF), "shard", scatter_dimension=axis, tiled=True).astype(F32)
        mine, other = self.halves(value, self.shard, axis)
        return mine.astype(F32) + self.over_shard(other.astype(BF)).astype(F32)

    def scatter_core(self, value, axis):
        mine, other = self.halves(value, self.pair, axis)
        return mine.astype(F32) + self.over_core(other.astype(BF)).astype(F32)

    def scatter_heads(self, value, axis):
        mine, other = self.halves(value, self.head // 2, axis)
        return mine.astype(F32) + self.over_heads(other.astype(BF)).astype(F32)

    def line_gather(self, value):
        ups, downs = [value], [value]
        for _ in range(3):
            ups.append(self.up(ups[-1]))
            downs.append(self.down(downs[-1]))
        out = [value]
        for back in (1, 2, 3):
            out.append(jnp.where(self.tensor >= back, ups[back], downs[4 - back]))
        return out

    def line_scatter(self, parts):
        high, low = parts[1].astype(BF), parts[3].astype(BF)
        high = (parts[2].astype(F32) + self.up(high).astype(F32)).astype(BF)
        low = (parts[2].astype(F32) + self.down(low).astype(F32)).astype(BF)
        high = (parts[3].astype(F32) + self.up(high).astype(F32)).astype(BF)
        low = (parts[1].astype(F32) + self.down(low).astype(F32)).astype(BF)
        return parts[0].astype(F32) + self.up(high).astype(F32) + self.down(low).astype(F32)


def local(
    tokens,
    ln1_gain,
    ln1_bias,
    qkv_weight,
    out_weight,
    ln2_gain,
    ln2_bias,
    router_weight,
    expert_in,
    expert_out,
    route_noise,
    expert_ids,
    cotangent,
):
    comm = Comm()
    rows, width = tokens.shape
    experts = expert_in.shape[0]
    images = rows // SEQ
    heads = width // HEAD_DIM
    scale = HEAD_DIM ** (-0.5)
    half = experts // 2
    depth = ln1_gain.shape[0]

    smalls = jnp.concatenate(
        (ln1_gain[None], ln1_bias[None], ln2_gain[None], ln2_bias[None], router_weight.T), 0
    )
    smalls = comm.gather_shard(smalls, 1)
    gain_a, bias_a, gain_b, bias_b = (smalls[i].astype(F32) for i in range(4))
    router = smalls[4:].T
    dense = jnp.concatenate((qkv_weight, out_weight), 1)
    dense = comm.gather_shard_split(dense, 0, 1)
    proj_qkv, proj_out = dense[:, : 3 * width], dense[:, 3 * width :]
    own_in = lax.dynamic_slice_in_dim(expert_in, comm.pair * half, half, 0)
    own_out = lax.dynamic_slice_in_dim(expert_out, comm.pair * half, half, 0)
    inner = comm.gather_shard(own_in, 1)
    outer = comm.gather_shard(own_out, 2)
    grad_rows = jnp.concatenate(comm.line_gather(cotangent), 0)
    grad_rows = jnp.concatenate((grad_rows, comm.over_core(grad_rows)), 0)

    start_x = tokens.astype(F32)
    first_norm, first_pull = jax.vjp(layer_norm, start_x, gain_a, bias_a)
    normed_a = first_norm.astype(BF)
    packed = jnp.dot(normed_a, proj_qkv, preferred_element_type=F32).astype(BF)
    groups = heads // 3
    split = packed.reshape(images, SEQ, groups, 3, 3, HEAD_DIM)
    split = split.transpose(3, 0, 2, 4, 1, 5).reshape(3, images, heads, SEQ, HEAD_DIM)
    query, keys, values = split[0], split[1], split[2]
    scores = jnp.einsum("nhid,nhjd->nhij", query, keys, preferred_element_type=F32) * scale
    probs = jax.nn.softmax(scores, -1)
    weights = probs.astype(BF)
    attended = jnp.einsum("nhij,nhjd->nhid", weights, values, preferred_element_type=F32).astype(BF)
    returned = attended.transpose(0, 2, 1, 3).reshape(rows, width)
    middle = start_x + jnp.dot(returned, proj_out, preferred_element_type=F32)
    second_norm, second_pull = jax.vjp(layer_norm, middle, gain_b, bias_b)
    normed_b = second_norm.astype(BF)
    labels = jnp.arange(experts, dtype=jnp.int32)
    chosen = jnp.sum((expert_ids[:, :, None] == labels[None, None, :]).astype(F32), 1)

    def gate_function(normed, weight):
        return route_gates(normed, weight, route_noise, chosen)

    gates, gate_pull = jax.vjp(gate_function, normed_b.astype(F32), router.astype(F32))
    sent = jnp.concatenate((normed_b, jnp.pad(gates.astype(BF), ((0, 0), (0, 128 - experts)))), 1)
    rows_all = jnp.concatenate(comm.line_gather(sent), 0)
    rows_all = jnp.concatenate((rows_all, comm.over_core(rows_all)), 0)
    part_gates = lax.dynamic_slice_in_dim(rows_all[:, width:], comm.pair * half, half, 1).astype(F32)
    rows_all = rows_all[:, :width]

    total = jnp.zeros((rows_all.shape[0], width), F32)
    grad_rows_in = jnp.zeros((rows_all.shape[0], width), F32)
    gate_grads, inner_grads, outer_grads = [], [], []

    def reduce_expert(grad, axis, other):
        part = comm.scatter_shard(grad, axis)
        part = comm.scatter_heads(part, other).astype(BF)
        return comm.join(part, comm.over_heads(part), comm.head // 2, other)

    for expert in range(half):
        hidden = jnp.dot(rows_all, inner[expert], preferred_element_type=F32)
        activated, gelu_pull = jax.vjp(jax.nn.gelu, hidden)
        gate_column = part_gates[:, expert : expert + 1]
        active = (activated * gate_column).astype(BF)
        total = total + jnp.dot(active, outer[expert], preferred_element_type=F32)
        grad_active = contract_cols(grad_rows, outer[expert])
        gate_grads.append(jnp.sum(grad_active * activated, 1))
        grad_hidden = gelu_pull(grad_active * gate_column)[0].astype(BF)
        grad_rows_in = grad_rows_in + contract_cols(grad_hidden, inner[expert])
        outer_grads.append(reduce_expert(contract_rows(active, grad_rows), 1, 0))
        inner_grads.append(reduce_expert(contract_rows(rows_all, grad_hidden), 0, 1))

    count = rows * 4
    gate_table = jnp.stack(gate_grads, 1)
    spread = jnp.zeros((2 * count, 128), F32)
    spread = lax.dynamic_update_slice_in_dim(spread, gate_table, comm.pair * half, 1)
    back = jnp.concatenate((grad_rows_in, spread), 1).astype(BF)
    back = back[:count].astype(F32) + comm.over_core(back[count:]).astype(F32)
    back = comm.line_scatter([back[k * rows : (k + 1) * rows] for k in range(4)])
    grad_normed_moe, grad_gates = back[:, :width], back[:, width : width + experts]
    moe = total.astype(BF)
    moe = moe[:count].astype(F32) + comm.over_core(moe[count:]).astype(F32)
    moe = comm.line_scatter([moe[k * rows : (k + 1) * rows] for k in range(4)])
    mixed = (middle + moe).astype(BF)

    grad_out = cotangent.astype(F32)
    route_normed, grad_router = gate_pull(grad_gates)
    grad_mid, grad_gain_b, grad_bias_b = second_pull(grad_normed_moe + route_normed)
    grad_middle = grad_out + grad_mid
    grad_proj = grad_middle.astype(BF)
    grad_proj_out = contract_rows(returned, grad_proj)
    grad_returned = contract_cols(grad_proj, proj_out).astype(BF)
    grad_attended = grad_returned.reshape(images, SEQ, heads, HEAD_DIM).transpose(0, 2, 1, 3)
    grad_values = jnp.einsum("nhij,nhid->nhjd", weights, grad_attended, preferred_element_type=F32)
    grad_weights = jnp.einsum("nhid,nhjd->nhij", grad_attended, values, preferred_element_type=F32)
    inner_sum = jnp.sum(probs * grad_weights, -1, keepdims=True)
    grad_scores = (probs * (grad_weights - inner_sum)).astype(BF)
    grad_query = jnp.einsum("nhij,nhjd->nhid", grad_scores, keys, preferred_element_type=F32) * scale
    grad_keys = jnp.einsum("nhij,nhid->nhjd", grad_scores, query, preferred_element_type=F32) * scale
    stack = jnp.stack((grad_query, grad_keys, grad_values), 0).astype(BF)
    stack = stack.reshape(3, images, groups, 3, SEQ, HEAD_DIM).transpose(1, 4, 2, 0, 3, 5)
    grad_packed = stack.reshape(rows, 3 * width)
    grad_proj_qkv = contract_rows(normed_a, grad_packed)
    grad_normed_a = contract_cols(grad_packed, proj_qkv)
    grad_first, grad_gain_a, grad_bias_a = first_pull(grad_normed_a)
    grad_tokens = (grad_middle + grad_first).astype(BF)

    small = jnp.concatenate(
        (grad_gain_a[:, None], grad_bias_a[:, None], grad_gain_b[:, None], grad_bias_b[:, None], grad_router), 1
    )
    small = jnp.pad(small, ((0, 0), (0, 128 - small.shape[1])))
    shares = jnp.concatenate((grad_proj_qkv, grad_proj_out, small, jnp.zeros_like(small)), 1)
    shares = comm.scatter_core(shares, 1)
    shares = comm.scatter_shard(shares, 0)
    shares = comm.scatter_heads(shares, 1)
    cut = shares.shape[0] // 4
    rolled = [
        lax.dynamic_slice_in_dim(shares, ((comm.tensor + 4 - k) % 4) * cut, cut, 0) for k in range(4)
    ]
    summed = comm.line_scatter(rolled).astype(BF)
    pieces = comm.line_gather(summed)
    whole = jnp.zeros(shares.shape, BF)
    for k in range(4):
        whole = lax.dynamic_update_slice_in_dim(whole, pieces[k], ((comm.tensor + 4 - k) % 4) * cut, 0)
    whole = comm.join(whole, comm.over_heads(whole), comm.head // 2, 1)
    whole = comm.join(whole, comm.over_core(whole), comm.pair, 1).astype(F32)
    small = whole[:, 4 * width : 4 * width + 128]

    grad_in, grad_outer = jnp.stack(inner_grads, 0), jnp.stack(outer_grads, 0)
    grad_in = comm.join(grad_in, comm.over_core(grad_in), comm.pair, 0).astype(F32)
    grad_outer = comm.join(grad_outer, comm.over_core(grad_outer), comm.pair, 0).astype(F32)
    return (
        mixed,
        grad_tokens,
        small[:, 0],
        small[:, 1],
        whole[:, : 3 * width],
        whole[:, 3 * width : 4 * width],
        small[:, 2],
        small[:, 3],
        small[:, 4 : 4 + experts],
        grad_in,
        grad_outer,
    )


def solution(mesh):
    split = P(AXES, None)
    vector, matrix = P("shard"), P("shard", None)
    inner, outer = P(None, "shard", "tensor"), P(None, "tensor", "shard")
    return jax.shard_map(
        local,
        mesh=mesh,
        in_specs=(
            split, vector, vector, matrix, matrix, vector, vector, matrix, inner, outer, split, split, split,
        ),
        out_specs=(
            split, split, vector, vector, matrix, matrix, vector, vector, matrix, inner, outer,
        ),
        check_vma=False,
    )
```

time: 1530 us -> 1000 us (0.65)
  waiting for transfers between devices: 681 us -> 170 us
  blocking collectives: 256 us -> 0 us
  starting transfers between devices: 21.8 us -> 150 us
  local copies, waits for them, and re-layouts: 160 us -> 280 us
  other arithmetic: 67.8 us -> 118 us
  matrix products: 315 us -> 266 us
    all_gather x6 -> x0, waiting for transfers between devices: 257 us -> none  [the longest x1 117 us: gather_weights(): lax.all_gather(outer, 'shard', axis=2, tiled=True)]
    psum x2 -> x0, waiting for transfers between devices: 196 us -> none  [the longest x1 169 us: local(): lax.psum(shares[7].astype(jnp.bfloat16), 'heads').astype(jnp.float32)]
    ppermute x0 -> x76, waiting for transfers between devices: none -> 170 us  [move(): return lax.ppermute(value, AXES, pairs)]
    ppermute x0 -> x76, starting transfers between devices: none -> 150 us  [move(): return lax.ppermute(value, AXES, pairs)]
    unnamed x4 -> x0, blocking collectives: 146 us -> none
    reduce_scatter x3 -> x0, waiting for transfers between devices: 100 us -> none  [the longest x1 100 us: local(): lax.psum_scatter(jnp.stack(inner_grads, 0).astype(jnp.bfloat16), 'shard',...]
    unnamed x17 -> x0, waiting for transfers between devices: 93.6 us -> none
    concatenate x0 -> x10, local copies, waits for them, and re-layouts: none -> 83.7 us  [the longest x1 30.6 us: local(): rows_all = jnp.concatenate((rows_all, comm.over_core(rows_all)), 0)]
  transfers between devices with their start and end apart: 18 -> 76, of which waited for: 12 -> 29; matrix products, arithmetic and copies ran while one was open for 31% -> 47% of each run, Pallas kernels for 0% -> 0%
where the time goes in v1:
time: 1000 us; the launch traced here: 988 us
  local copies, waits for them, and re-layouts  280 us (28%)
  matrix products  266 us (27%)
  waiting for transfers between devices  170 us (17%)
  starting transfers between devices  150 us (15%)
  other arithmetic  118 us (12%)
    ppermute x76, waiting for transfers between devices, move(): return lax.ppermute(value, AXES, pairs)  170 us
    ppermute x76, starting transfers between devices, move(): return lax.ppermute(value, AXES, pairs)  150 us
    dot_general x10, matrix products, contract_cols(): lax.dot_general(left, right, (((1,), (1,)), ((), ())), preferred_element_...  77.2 us
    dot_general x10, matrix products, contract_rows(): lax.dot_general(left, right, (((0,), (0,)), ((), ())), preferred_element_...  74 us
    dot_general x4, matrix products, local(): hidden = jnp.dot(rows_all, inner[expert], preferred_element_type=F32)  57.8 us
    unnamed x311, local copies, waits for them, and re-layouts  54.7 us
    dot_general x4, matrix products, local(): total = total + jnp.dot(active, outer[expert], preferred_element_type=F32)  38.5 us
    ppermute x20, local copies, waits for them, and re-layouts, move(): return lax.ppermute(value, AXES, pairs)  35.7 us
  transfers between devices with their start and end apart: 76, of which 29 were waited for; matrix products, arithmetic and copies ran while one was open for 47% of the time, Pallas kernels for 0%

profile of v1, /device:TPU:17, one launch (start us, length us, event | category | flops | bytes accessed | tf_op | source)
XLA Modules:
  0.0 988.4 jit_solution(16324271357102187112)
XLA Ops:
  49.6 8.4 collective-permute-done.24
  63.0 16.7 %concatenate.96 = bf16[1576,768]{1,0:T(8,128)(2,1)} concatenate(bf16[394,768]{1,0:T(8,128)(2,1)} %param.25, bf16[394,768]{1,0:T(8,128)(2,1)} %broadcast_select_fusion.21, bf16[394,768]{1,0:T(8,128)(2,1)} %broadcast_select_fusion.20, bf16[394,768]{1,0:T(8,128)(2,1)} %broadcast_select_fusion.19), dimensions={0} | concatenate | bytes 4841472 | tf_op jit(solution)/shard_map/concatenate | solution.py:164
  120.3 11.0 %collective-permute-done.3 = bf16[394,896]{1,0:T(8,128)(2,1)S(1)} collective-permute-done((bf16[394,896]{1,0:T(8,128)(2,1)S(1)}, bf16[394,896]{1,0:T(8,128)(2,1)S(1)}, u32[]{:S(2)}, u32[]{:S(2)}) %collective-permute-start.3) | collective-permute-done | bytes 706080 | tf_op jit(solution)/shard_map/ppermute | solution.py:53
  169.5 25.7 %concatenate.97 = bf16[3152,768]{1,0:T(8,128)(2,1)} concatenate(bf16[394,768]{1,0:T(8,128)(2,1)} %param.25, bf16[394,768]{1,0:T(8,128)(2,1)S(1)} %copy-done.38, bf16[394,768]{1,0:T(8,128)(2,1)S(1)} %copy-done.36, bf16[394,768]{1,0:T(8,128)(2,1)S(1)} %copy-done.37, bf16[1576,768]{1,0:T(8,128)(2,1)} %collective-permute-done.25), dimensions={0} | concatenate | bytes 9682944 | tf_op jit(solution)/shard_map/concatenate | solution.py:165
  212.9 10.5 %fusion.120 = f32[3152,768]{1,0:T(8,128)} fusion(bf16[3152,768]{1,0:T(8,128)(2,1)} %concatenate.97, bf16[4,768,384]{2,1,0:T(8,128)(2,1)} %copy-done.16, bf16[4,768,384]{2,1,0:T(8,128)(2,1)} %copy-done.14), kind=kOutput, calls=%fused_computation.334 | convolution fusion | flops 3720609792 | bytes 19243008 | tf_op jit(solution)/shard_map/dot_general | solution.py:32
  223.4 9.0 fusion.124
  248.8 30.6 %concatenate.93 = bf16[3152,896]{1,0:T(8,128)(2,1)} concatenate(bf16[394,896]{1,0:T(8,128)(2,1)} %copy-done.66, bf16[394,896]{1,0:T(8,128)(2,1)S(1)} %copy.239, bf16[394,896]{1,0:T(8,128)(2,1)} %copy.240, bf16[394,896]{1,0:T(8,128)(2,1)} %copy.241, bf16[1576,896]{1,0:T(8,128)(2,1)} %collective-permute-done.9), dimensions={0} | concatenate | bytes 11296768 | tf_op jit(solution)/shard_map/concatenate | solution.py:192
  284.0 14.9 %fusion.9 = (bf16[3152,768]{1,0:T(8,128)(2,1)}, bf16[3152]{0:T(1024)(128)(2,1)}, bf16[3152,768]{1,0:T(8,128)(2,1)}) fusion(f32[3152,768]{1,0:T(8,128)} %fusion.124, f32[3152]{0:T(1024)S(1)} %get-tuple-element.88, bf16[4,384,768]{2,1,0:T(8,128)(2,1)S(1)} %copy-done.13, bf16[4,384,768]{2,1,0:T(8,128)(2,1)S(1)} %copy-done.11, bf16[3152,896]{1,0:T(8,128)(2,1)S(1)} %copy-done.26), kind=kOutput, calls=%fused_computation.22 | convolution fusion | flops 3783545856 | bytes 28948640 | tf_op jit(solution)/shard_map/dot_general | solution.py:206
  298.9 9.6 fusion.143
  315.3 14.7 %fusion.16 = (bf16[3152,768]{1,0:T(8,128)(2,1)}, bf16[3152]{0:T(1024)(128)(2,1)}, bf16[3152,768]{1,0:T(8,128)(2,1)}) fusion(f32[3152,768]{1,0:T(8,128)} %fusion.120, f32[3152]{0:T(1024)S(1)} %get-tuple-element.87, bf16[4,384,768]{2,1,0:T(8,128)(2,1)S(1)} %copy-done.13, bf16[4,384,768]{2,1,0:T(8,128)(2,1)S(1)} %copy-done.11, bf16[3152,896]{1,0:T(8,128)(2,1)S(1)} %copy-done.26), kind=kOutput, calls=%fused_computation.29 | convolution fusion | flops 3783545856 | bytes 28948640 | tf_op jit(solution)/shard_map/dot_general | solution.py:206
  345.2 14.2 %fusion.23 = (bf16[3152,768]{1,0:T(8,128)(2,1)}, bf16[3152]{0:T(1024)(128)(2,1)S(1)}, bf16[3152,768]{1,0:T(8,128)(2,1)}) fusion(f32[3152,768]{1,0:T(8,128)} %fusion.128, f32[3152]{0:T(1024)S(1)} %get-tuple-element.86, bf16[4,384,768]{2,1,0:T(8,128)(2,1)S(1)} %copy-done.13, bf16[4,384,768]{2,1,0:T(8,128)(2,1)S(1)} %copy-done.11, ...), kind=kOutput, calls=%fused_computation.36 | convolution fusion | flops 3783545856 | bytes 28948640 | tf_op jit(solution)/shard_map/dot_general | solution.py:206
  359.5 9.6 fusion.145
  369.1 9.2 fusion.130
  391.5 8.3 fusion.76
  411.7 14.1 %fusion.30 = (bf16[3152,768]{1,0:T(8,128)(2,1)}, bf16[3152]{0:T(1024)(128)(2,1)S(1)}, bf16[3152,768]{1,0:T(8,128)(2,1)S(1)}) fusion(f32[3152,768]{1,0:T(8,128)} %fusion.141, f32[3152]{0:T(1024)S(1)} %copy-done.122, bf16[768,768]{1,0:T(8,128)(2,1)S(1)} %copy-done.50, bf16[3152,896]{1,0:T(8,128)(2,1)S(1)} %copy-done.26), kind=kOutput, calls=%fused_computation.43 | convolution fusion | flops 3781186560 | bytes 25409696 | tf_op jit(solution)/shard_map/dot_general | solution.py:206
  434.0 15.3 %add_convert_fusion.1 = bf16[3152,768]{0,1:T(8,128)(2,1)} fusion(f32[3152,768]{0,1:T(8,128)} %fusion.130, f32[3152,768]{0,1:T(8,128)} %fusion.126, f32[3152,768]{0,1:T(8,128)} %fusion.122, bf16[3152,768]{1,0:T(8,128)(2,1)} %copy-done.49, bf16[768,768]{1,0:T(8,128)(2,1)S(1)} %copy-done.52), kind=kOutput, calls=%fused_computation.15 | convolution fusion | flops 3727933440 | bytes 39911424 | tf_op jit(solution)/shard_map/dot_general | solution.py:210
  455.5 10.6 %fusion.117 = f32[3152,768]{0,1:T(8,128)} fusion(bf16[3152,768]{1,0:T(8,128)(2,1)} %get-tuple-element.102, bf16[4,384,768]{2,1,0:T(8,128)(2,1)} %copy-done.12, bf16[4,384,768]{2,1,0:T(8,128)(2,1)} %copy-done.10), kind=kOutput, calls=%fused_computation.333 | convolution fusion | flops 3720609792 | bytes 19243008 | tf_op jit(solution)/shard_map/dot_general | solution.py:32
  466.1 15.3 %add_convert_fusion = bf16[3152,768]{0,1:T(8,128)(2,1)S(1)} fusion(f32[3152,768]{0,1:T(8,128)} %fusion.117, f32[3152,768]{0,1:T(8,128)} %fusion.114, f32[3152,768]{0,1:T(8,128)} %fusion.111, bf16[3152,768]{1,0:T(8,128)(2,1)} %get-tuple-element.96, bf16[768,768]{1,0:T(8,128)(2,1)} %fusion.69), kind=kOutput, calls=%fused_computation.14 | convolution fusion | flops 3727933440 | bytes 39911424 | tf_op jit(solution)/shard_map/dot_general | solution.py:32
  495.4 9.6 fusion.72
  593.7 12.9 %collective-permute-done.14 = bf16[394,768]{1,0:T(8,128)(2,1)S(1)} collective-permute-done((bf16[394,768]{1,0:T(8,128)(2,1)}, bf16[394,768]{1,0:T(8,128)(2,1)S(1)}, u32[]{:S(2)}, u32[]{:S(2)}) %collective-permute-start.14) | collective-permute-done | bytes 605216 | tf_op jit(solution)/shard_map/ppermute | solution.py:53
  670.3 12.9 %collective-permute-done.18 = bf16[394,768]{1,0:T(8,128)(2,1)S(1)} collective-permute-done((bf16[394,768]{1,0:T(8,128)(2,1)}, bf16[394,768]{1,0:T(8,128)(2,1)S(1)}, u32[]{:S(2)}, u32[]{:S(2)}) %collective-permute-start.18) | collective-permute-done | bytes 605216 | tf_op jit(solution)/shard_map/ppermute | solution.py:53
  823.3 27.4 %collective-permute-done.35 = bf16[384,832]{0,1:T(8,128)(2,1)S(1)} collective-permute-done((bf16[384,832]{0,1:T(8,128)(2,1)S(1)}, bf16[384,832]{0,1:T(8,128)(2,1)S(1)}, u32[]{:S(2)}, u32[]{:S(2)}) %collective-permute-start.35) | collective-permute-done | bytes 639008 | tf_op jit(solution)/shard_map/ppermute | solution.py:53
  936.7 9.6 copy.305
  957.5 9.7 copy.304
  (700 shorter events, 655.0 us)
Async XLA Ops:
  14.1 119.2 %collective-permute-start.11 = (bf16[4,768,384]{2,1,0:T(8,128)(2,1)}, bf16[4,768,384]{2,1,0:T(8,128)(2,1)}, u32[]{:S(2)}, u32[]{:S(2)}) collective-permute-start(bf16[4,768,384]{2,1,0:T(8,128)(2,1)} %constant_dynamic-slice_fusion), channel_id=1, source_target_pairs={{0,16},{1,17},{2,18},{3,19},{4,20},{5,21},{6,22},{7,23},{8,24},{9,... | collective-permute-start | bytes 7077896 | tf_op jit(solution)/shard_map/ppermute | solution.py:53
  33.8 46.9 %collective-permute-start.2 = (bf16[384,1536]{1,0:T(8,128)(2,1)}, bf16[384,1536]{1,0:T(8,128)(2,1)}, u32[]{:S(2)}, u32[]{:S(2)}) collective-permute-start(bf16[384,1536]{1,0:T(8,128)(2,1)} %collective-permute-done.1), channel_id=1, source_target_pairs={{0,4},{1,5},{2,6},{3,7},{4,0},{5,1},{6,2},{7,3},{8,12},{9,13},{10,... | collective-permute-start | bytes 3538952 | tf_op jit(solution)/shard_map/ppermute | solution.py:53
  42.4 97.1 %collective-permute-start.10 = (bf16[4,384,768]{2,1,0:T(8,128)(2,1)}, bf16[4,384,768]{2,1,0:T(8,128)(2,1)}, u32[]{:S(2)}, u32[]{:S(2)}) collective-permute-start(bf16[4,384,768]{2,1,0:T(8,128)(2,1)} %constant_dynamic-slice_fusion.1), channel_id=1, source_target_pairs={{0,16},{1,17},{2,18},{3,19},{4,20},{5,21},{6,22},{7,23},{8,24},{9,... | collective-permute-start | bytes 7077896 | tf_op jit(solution)/shard_map/ppermute | solution.py:53
  79.7 89.8 %collective-permute-start.25 = (bf16[1576,768]{1,0:T(8,128)(2,1)}, bf16[1576,768]{1,0:T(8,128)(2,1)}, u32[]{:S(2)}, u32[]{:S(2)}) collective-permute-start(bf16[1576,768]{1,0:T(8,128)(2,1)} %concatenate.96), channel_id=1, source_target_pairs={{0,4},{1,5},{2,6},{3,7},{4,0},{5,1},{6,2},{7,3},{8,12},{9,13},{10,... | collective-permute-start | bytes 7262216 | tf_op jit(solution)/shard_map/ppermute | solution.py:53
  150.2 45.0 %collective-permute-start.8 = (bf16[394,896]{1,0:T(8,128)(2,1)}, bf16[394,896]{1,0:T(8,128)(2,1)}, u32[]{:S(2)}, u32[]{:S(2)}) collective-permute-start(bf16[394,896]{1,0:T(8,128)(2,1)} %collective-permute-done.7), channel_id=1, source_target_pairs={{0,1},{1,2},{2,3},{4,5},{5,6},{6,7},{8,9},{9,10},{10,11},{12,13},{... | collective-permute-start | bytes 2118152 | tf_op jit(solution)/shard_map/ppermute | solution.py:53
  155.1 44.0 %collective-permute-start.6 = (bf16[394,896]{1,0:T(8,128)(2,1)}, bf16[394,896]{1,0:T(8,128)(2,1)}, u32[]{:S(2)}, u32[]{:S(2)}) collective-permute-start(bf16[394,896]{1,0:T(8,128)(2,1)} %collective-permute-done.5), channel_id=1, source_target_pairs={{1,0},{2,1},{3,2},{5,4},{6,5},{7,6},{9,8},{10,9},{11,10},{13,12},{... | collective-permute-start | bytes 2118152 | tf_op jit(solution)/shard_map/ppermute | solution.py:53
  408.1 173.4 %collective-permute-start.66 = (bf16[768,384]{0,1:T(8,128)(2,1)}, bf16[768,384]{0,1:T(8,128)(2,1)}, u32[]{:S(2)}, u32[]{:S(2)}) collective-permute-start(bf16[768,384]{0,1:T(8,128)(2,1)} %dynamic-slice_convert_fusion.5), channel_id=1, source_target_pairs={{0,16},{1,17},{2,18},{3,19},{4,20},{5,21},{6,22},{7,23},{8,24},{9,... | collective-permute-start | bytes 1769480 | tf_op jit(solution)/shard_map/ppermute | solution.py:53
  410.5 176.2 %collective-permute-start.63 = (bf16[768,384]{0,1:T(8,128)(2,1)}, bf16[768,384]{0,1:T(8,128)(2,1)}, u32[]{:S(2)}, u32[]{:S(2)}) collective-permute-start(bf16[768,384]{0,1:T(8,128)(2,1)} %dynamic-slice_convert_fusion.6), channel_id=1, source_target_pairs={{0,16},{1,17},{2,18},{3,19},{4,20},{5,21},{6,22},{7,23},{8,24},{9,... | collective-permute-start | bytes 1769480 | tf_op jit(solution)/shard_map/ppermute | solution.py:53
  454.9 58.0 %collective-permute-start.12 = (bf16[1576,768]{1,0:T(8,128)(2,1)}, bf16[1576,768]{1,0:T(8,128)(2,1)}, u32[]{:S(2)}, u32[]{:S(2)}) collective-permute-start(bf16[1576,768]{1,0:T(8,128)(2,1)} %copy.246), channel_id=1, source_target_pairs={{0,4},{1,5},{2,6},{3,7},{4,0},{5,1},{6,2},{7,3},{8,12},{9,13},{10,... | collective-permute-start | bytes 7262216 | tf_op jit(solution)/shard_map/ppermute | solution.py:53
  531.4 38.7 %collective-permute-start.27 = (bf16[394,896]{1,0:T(8,128)(2,1)S(1)}, bf16[394,896]{1,0:T(8,128)(2,1)}, u32[]{:S(2)}, u32[]{:S(2)}) collective-permute-start(bf16[394,896]{1,0:T(8,128)(2,1)S(1)} %copy.267), channel_id=1, source_target_pairs={{0,1},{1,2},{2,3},{4,5},{5,6},{6,7},{8,9},{9,10},{10,11},{12,13},{... | collective-permute-start | bytes 2118152 | tf_op jit(solution)/shard_map/ppermute | solution.py:53
  586.7 39.3 %collective-permute-start.72 = (bf16[768,384]{0,1:T(8,128)(2,1)}, bf16[768,384]{0,1:T(8,128)(2,1)}, u32[]{:S(2)}, u32[]{:S(2)}) collective-permute-start(bf16[768,384]{0,1:T(8,128)(2,1)} %dynamic-slice_convert_fusion.3), channel_id=1, source_target_pairs={{0,16},{1,17},{2,18},{3,19},{4,20},{5,21},{6,22},{7,23},{8,24},{9,... | collective-permute-start | bytes 1769480 | tf_op jit(solution)/shard_map/ppermute | solution.py:53
  589.2 39.4 %collective-permute-start.69 = (bf16[768,384]{0,1:T(8,128)(2,1)}, bf16[768,384]{0,1:T(8,128)(2,1)}, u32[]{:S(2)}, u32[]{:S(2)}) collective-permute-start(bf16[768,384]{0,1:T(8,128)(2,1)} %dynamic-slice_convert_fusion.4), channel_id=1, source_target_pairs={{0,16},{1,17},{2,18},{3,19},{4,20},{5,21},{6,22},{7,23},{8,24},{9,... | collective-permute-start | bytes 1769480 | tf_op jit(solution)/shard_map/ppermute | solution.py:53
  591.7 72.4 %collective-permute-start.53 = (bf16[384,768]{0,1:T(8,128)(2,1)}, bf16[384,768]{0,1:T(8,128)(2,1)}, u32[]{:S(2)}, u32[]{:S(2)}) collective-permute-start(bf16[384,768]{0,1:T(8,128)(2,1)} %dynamic-slice_convert_fusion.9), channel_id=1, source_target_pairs={{0,16},{1,17},{2,18},{3,19},{4,20},{5,21},{6,22},{7,23},{8,24},{9,... | collective-permute-start | bytes 1769480 | tf_op jit(solution)/shard_map/ppermute | solution.py:53
  636.5 47.2 %collective-permute-start.29 = (bf16[394,896]{1,0:T(8,128)(2,1)}, bf16[394,896]{1,0:T(8,128)(2,1)}, u32[]{:S(2)}, u32[]{:S(2)}) collective-permute-start(bf16[394,896]{1,0:T(8,128)(2,1)} %copy.271), channel_id=1, source_target_pairs={{0,1},{1,2},{2,3},{4,5},{5,6},{6,7},{8,9},{9,10},{10,11},{12,13},{... | collective-permute-start | bytes 2118152 | tf_op jit(solution)/shard_map/ppermute | solution.py:53
  664.2 77.7 %collective-permute-start.50 = (bf16[384,768]{0,1:T(8,128)(2,1)}, bf16[384,768]{0,1:T(8,128)(2,1)}, u32[]{:S(2)}, u32[]{:S(2)}) collective-permute-start(bf16[384,768]{0,1:T(8,128)(2,1)} %dynamic-slice_convert_fusion.10), channel_id=1, source_target_pairs={{0,16},{1,17},{2,18},{3,19},{4,20},{5,21},{6,22},{7,23},{8,24},{9,... | collective-permute-start | bytes 1769480 | tf_op jit(solution)/shard_map/ppermute | solution.py:53
  667.8 80.3 %collective-permute-start.59 = (bf16[384,768]{0,1:T(8,128)(2,1)}, bf16[384,768]{0,1:T(8,128)(2,1)}, u32[]{:S(2)}, u32[]{:S(2)}) collective-permute-start(bf16[384,768]{0,1:T(8,128)(2,1)} %dynamic-slice_convert_fusion.7), channel_id=1, source_target_pairs={{0,16},{1,17},{2,18},{3,19},{4,20},{5,21},{6,22},{7,23},{8,24},{9,... | collective-permute-start | bytes 1769480 | tf_op jit(solution)/shard_map/ppermute | solution.py:53
  683.2 67.4 %collective-permute-start.56 = (bf16[384,768]{0,1:T(8,128)(2,1)}, bf16[384,768]{0,1:T(8,128)(2,1)}, u32[]{:S(2)}, u32[]{:S(2)}) collective-permute-start(bf16[384,768]{0,1:T(8,128)(2,1)} %dynamic-slice_convert_fusion.8), channel_id=1, source_target_pairs={{0,16},{1,17},{2,18},{3,19},{4,20},{5,21},{6,22},{7,23},{8,24},{9,... | collective-permute-start | bytes 1769480 | tf_op jit(solution)/shard_map/ppermute | solution.py:53
  683.7 68.8 %collective-permute-start.67 = (bf16[384,384]{0,1:T(8,128)(2,1)}, bf16[384,384]{0,1:T(8,128)(2,1)}, u32[]{:S(2)}, u32[]{:S(2)}) collective-permute-start(bf16[384,384]{0,1:T(8,128)(2,1)} %dynamic-slice_convert_fusion.14), channel_id=1, source_target_pairs={{0,8},{1,9},{2,10},{3,11},{4,12},{5,13},{6,14},{7,15},{8,0},{9,1},... | collective-permute-start | bytes 884744 | tf_op jit(solution)/shard_map/ppermute | solution.py:53
  687.7 67.0 %collective-permute-start.64 = (bf16[384,384]{0,1:T(8,128)(2,1)}, bf16[384,384]{0,1:T(8,128)(2,1)}, u32[]{:S(2)}, u32[]{:S(2)}) collective-permute-start(bf16[384,384]{0,1:T(8,128)(2,1)} %dynamic-slice_convert_fusion.15), channel_id=1, source_target_pairs={{0,8},{1,9},{2,10},{3,11},{4,12},{5,13},{6,14},{7,15},{8,0},{9,1},... | collective-permute-start | bytes 884744 | tf_op jit(solution)/shard_map/ppermute | solution.py:53
  799.0 53.9 %collective-permute-start.52 = (bf16[384,384]{0,1:T(8,128)(2,1)S(1)}, bf16[384,384]{0,1:T(8,128)(2,1)S(1)}, u32[]{:S(2)}, u32[]{:S(2)}) collective-permute-start(bf16[384,384]{0,1:T(8,128)(2,1)S(1)} %add_convert_fusion.19), channel_id=1, source_target_pairs={{0,8},{1,9},{2,10},{3,11},{4,12},{5,13},{6,14},{7,15},{8,0},{9,1},... | collective-permute-start | bytes 884744 | tf_op jit(solution)/shard_map/ppermute | solution.py:53
  805.4 54.3 %collective-permute-start.61 = (bf16[384,384]{0,1:T(8,128)(2,1)S(1)}, bf16[384,384]{0,1:T(8,128)(2,1)S(1)}, u32[]{:S(2)}, u32[]{:S(2)}) collective-permute-start(bf16[384,384]{0,1:T(8,128)(2,1)S(1)} %add_convert_fusion.16), channel_id=1, source_target_pairs={{0,8},{1,9},{2,10},{3,11},{4,12},{5,13},{6,14},{7,15},{8,0},{9,1},... | collective-permute-start | bytes 884744 | tf_op jit(solution)/shard_map/ppermute | solution.py:53
  811.7 55.5 %collective-permute-start.58 = (bf16[384,384]{0,1:T(8,128)(2,1)S(1)}, bf16[384,384]{0,1:T(8,128)(2,1)S(1)}, u32[]{:S(2)}, u32[]{:S(2)}) collective-permute-start(bf16[384,384]{0,1:T(8,128)(2,1)S(1)} %add_convert_fusion.17), channel_id=1, source_target_pairs={{0,8},{1,9},{2,10},{3,11},{4,12},{5,13},{6,14},{7,15},{8,0},{9,1},... | collective-permute-start | bytes 884744 | tf_op jit(solution)/shard_map/ppermute | solution.py:53
  818.0 112.2 %collective-permute-start.75 = (bf16[4,768,384]{1,2,0:T(8,128)(2,1)}, bf16[4,768,384]{1,2,0:T(8,128)(2,1)}, u32[]{:S(2)}, u32[]{:S(2)}) collective-permute-start(bf16[4,768,384]{1,2,0:T(8,128)(2,1)} %pad_maximum_fusion.3), channel_id=1, source_target_pairs={{0,4},{1,5},{2,6},{3,7},{4,0},{5,1},{6,2},{7,3},{8,12},{9,13},{10,... | collective-permute-start | bytes 7077896 | tf_op jit(solution)/shard_map/ppermute | solution.py:53
  886.7 64.6 %collective-permute-start.62 = (bf16[4,384,768]{1,2,0:T(8,128)(2,1)}, bf16[4,384,768]{1,2,0:T(8,128)(2,1)}, u32[]{:S(2)}, u32[]{:S(2)}) collective-permute-start(bf16[4,384,768]{1,2,0:T(8,128)(2,1)} %pad_maximum_fusion.2), channel_id=1, source_target_pairs={{0,4},{1,5},{2,6},{3,7},{4,0},{5,1},{6,2},{7,3},{8,12},{9,13},{10,... | collective-permute-start | bytes 7077896 | tf_op jit(solution)/shard_map/ppermute | solution.py:53
  (204 other events, 2489.9 us)

commit v2 on v1

v2 whole, which is shorter than its diff:
```python
import jax
import jax.numpy as jnp
from jax import lax
from jax.experimental import pallas as pl
from jax.experimental.pallas import tpu as pltpu
from jax.sharding import PartitionSpec as P

HEAD_DIM = 64
SEQ = 197
EPS = 1e-06
AXES = ("shard", "heads", "tensor")
BF = jnp.bfloat16
F32 = jnp.float32


def contract_rows(left, right):
    return lax.dot_general(left, right, (((0,), (0,)), ((), ())), preferred_element_type=F32)


def contract_cols(left, right):
    return lax.dot_general(left, right, (((1,), (1,)), ((), ())), preferred_element_type=F32)


PAD = 208
TILE = 128
CHUNK = 256
FAR = 512.0
EXTRA = 128
MASKED = -1e30
CUBIC = 0.044715
ROOT = (2.0 / 3.141592653589793) ** 0.5
BIG = 60 * 1024 * 1024


def dot(left, right):
    return jnp.dot(left, right, preferred_element_type=F32)


def norm_parts(values):
    centred = values - jnp.mean(values, -1, keepdims=True)
    inverse = lax.rsqrt(jnp.mean(centred * centred, -1, keepdims=True) + EPS)
    return centred * inverse, inverse


def norm_back(grad, unit, inverse, gain):
    scaled = grad * gain
    along = jnp.mean(scaled * unit, -1, keepdims=True)
    return inverse * (scaled - jnp.mean(scaled, -1, keepdims=True) - unit * along)


def head_probs(query, keys, scale):
    scores = contract_cols(query, keys) * scale
    column = lax.broadcasted_iota(jnp.int32, scores.shape, 1)
    scores = jnp.where(column < SEQ, scores, MASKED)
    raised = jnp.exp(scores - jnp.max(scores, -1, keepdims=True))
    return raised / jnp.sum(raised, -1, keepdims=True)


def front_kernel(
    x_ref, small_ref, qkv_ref, out_ref, router_ref, noise_ref, ids_ref,
    normed_ref, packed_ref, attended_ref, middle_ref, sent_ref, prob_ref,
):
    width = x_ref.shape[1]
    images = x_ref.shape[0] // PAD
    group = 3 * HEAD_DIM
    groups = width // group
    scale = HEAD_DIM ** (-0.5)
    experts = 8
    for image in range(images):
        at = pl.ds(image * PAD, PAD)
        x = x_ref[at, :].astype(F32)
        unit, _ = norm_parts(x)
        normed = (unit * small_ref[0:1, :] + small_ref[1:2, :]).astype(BF)
        normed_ref[at, :] = normed
        lane = lax.broadcasted_iota(jnp.int32, (PAD, group), 1) // HEAD_DIM
        outs = []
        for double in range(groups // 2):
            cols = pl.ds(double * 6 * group, 6 * group)
            packed = dot(normed, qkv_ref[:, cols])
            packed_ref[at, cols] = packed.astype(BF)
            for side in range(2):
                query, keys, values = (
                    packed[:, (3 * side + k) * group : (3 * side + k + 1) * group].astype(BF)
                    for k in range(3)
                )
                total = jnp.zeros((PAD, group), F32)
                for head in range(3):
                    mask = lane == head
                    probs = head_probs(jnp.where(mask, query, jnp.zeros_like(query)), keys, scale)
                    total = jnp.where(mask, dot(probs.astype(BF), values), total)
                outs.append(total)
        attended = jnp.concatenate(outs, 1).astype(BF)
        attended_ref[at, :] = attended
        middle = x + dot(attended, out_ref[...])
        middle_ref[at, :] = middle
        unit, _ = norm_parts(middle)
        normed = (unit * small_ref[2:3, :] + small_ref[3:4, :]).astype(BF)
        lane = lax.broadcasted_iota(jnp.int32, (PAD, EXTRA), 1)
        logits = dot(normed, router_ref[...]) + noise_ref[at, :]
        logits = jnp.where(lane < experts, logits, MASKED)
        raised = jnp.exp(logits - jnp.max(logits, -1, keepdims=True))
        probs = raised / jnp.sum(raised, -1, keepdims=True)
        prob_ref[at, :] = probs
        first, second = ids_ref[at, 0:1], ids_ref[at, 1:2]
        chosen = ((lane == first) | (lane == second)).astype(F32)
        first, second = first + experts, second + experts
        flags = (((lane == first) | (lane == second)) & (lane >= experts)).astype(F32)
        sent_ref[at, 0:width] = normed
        sent_ref[at, width : width + EXTRA] = (probs * chosen + flags).astype(BF)


def front(x, small, qkv, out, router, noise, ids):
    rows, width = x.shape
    shape = jax.ShapeDtypeStruct
    return pl.pallas_call(
        front_kernel,
        out_shape=(
            shape((rows, width), BF),
            shape((rows, 3 * width), BF),
            shape((rows, width), BF),
            shape((rows, width), F32),
            shape((rows, width + EXTRA), BF),
            shape((rows, EXTRA), F32),
        ),
        compiler_params=pltpu.CompilerParams(vmem_limit_bytes=BIG),
        cost_estimate=pl.CostEstimate(flops=8 * 10**9, bytes_accessed=10**7, transcendentals=10**6),
        name="front",
    )(x, small, qkv, out, router, noise, ids)


def expert_kernel(
    place_ref, rows_ref, cot_ref, own_in, got_in, own_out, got_out,
    total_ref, back_ref, grad_in, grad_out,
    inner, outer, picked, grads, gate, active, hidden_grad, made, made_back, ranks, sum_in, sum_out, stage_in, stage_out,
    load_sem, store_sem,
):
    blocks, length, width = cot_ref.shape
    count = got_in.shape[0]
    depth = got_in.shape[1]
    pair, shard = place_ref[0], place_ref[1]
    experts = 2 * count
    capacity = blocks * TILE

    def loads(expert, slot):
        mine = pl.ds(pl.multiple_of(shard * depth, EXTRA), depth)
        other = pl.ds(pl.multiple_of((1 - shard) * depth, EXTRA), depth)
        index = pair * count + expert
        return (
            pltpu.make_async_copy(own_in.at[index], inner.at[slot, mine, :], load_sem.at[slot, 0]),
            pltpu.make_async_copy(got_in.at[expert], inner.at[slot, other, :], load_sem.at[slot, 1]),
            pltpu.make_async_copy(own_out.at[index], outer.at[slot, :, mine], load_sem.at[slot, 2]),
            pltpu.make_async_copy(got_out.at[expert], outer.at[slot, :, other], load_sem.at[slot, 3]),
        )

    def stores(expert, slot):
        return (
            pltpu.make_async_copy(stage_in.at[slot], grad_in.at[expert], store_sem.at[slot, 0]),
            pltpu.make_async_copy(stage_out.at[slot], grad_out.at[expert], store_sem.at[slot, 1]),
        )

    for copy in loads(0, 0):
        copy.start()
    ahead = lax.broadcasted_iota(jnp.int32, (length, length), 0)
    behind = lax.broadcasted_iota(jnp.int32, (length, length), 1)
    order = jnp.where(behind < ahead, 1.0, jnp.where(behind == ahead, FAR, 0.0)).astype(BF)

    def rank(block, carry):
        flags = rows_ref[block, :, width : width + EXTRA]
        place = lax.dot_general(flags, order, (((0,), (1,)), ((), ())), preferred_element_type=F32)
        ranks[block] = place[0:16, :] - FAR
        total_ref[block] = jnp.zeros(total_ref.shape[1:], BF)
        back_ref[block] = jnp.zeros(back_ref.shape[1:], BF)
        return carry

    lax.fori_loop(0, blocks, rank, 0)

    for expert in range(count):
        slot = expert % 2
        if expert + 1 < count:
            for copy in loads(expert + 1, 1 - slot):
                copy.start()
        line = pl.ds(experts + pair * count + expert, 1)
        highest = ranks[0, line, :]
        for block in range(1, blocks):
            highest = jnp.maximum(highest, ranks[block, line, :])
        passes = (jnp.maximum(jnp.max(highest), -1.0).astype(jnp.int32) + TILE) // TILE
        sum_in[...] = jnp.zeros(sum_in.shape, F32)
        sum_out[...] = jnp.zeros(sum_out.shape, F32)
        for copy in loads(expert, slot):
            copy.wait()

        def one_pass(step, carry):
            base = (step * TILE).astype(F32)
            slots = lax.broadcasted_iota(jnp.int32, (TILE, length), 0).astype(F32) + base

            def take(block, carry):
                choose = (ranks[block, line, :] == slots).astype(BF)
                at = pl.ds(pl.multiple_of(block * TILE, TILE), TILE)
                both = dot(choose, rows_ref[block])
                picked[at, :] = both[:, :width].astype(BF)
                lane = lax.broadcasted_iota(jnp.int32, (TILE, EXTRA), 1)
                column = jnp.where(lane == pair * count + expert, both[:, width:], 0.0)
                gate[at, :] = jnp.broadcast_to(jnp.sum(column, -1, keepdims=True), (TILE, EXTRA))
                grads[at, :] = dot(choose, cot_ref[block]).astype(BF)
                return carry

            lax.fori_loop(0, blocks, take, 0, unroll=2)

            def chunk(index, carry):
                at = pl.ds(pl.multiple_of(index * CHUNK, CHUNK), CHUNK)
                value = dot(picked[at, :], inner[slot])
                grad_active = contract_cols(grads[at, :], outer[slot])
                gate_column = gate[at, 0:1]
                square = value * value
                bent = jnp.tanh(ROOT * value * (1.0 + CUBIC * square))
                plus = 0.5 * (1.0 + bent)
                bowed = value * plus
                slope = plus + (0.5 * ROOT) * value * (1.0 - bent * bent) * (1.0 + (3.0 * CUBIC) * square)
                active[at, :] = (bowed * gate_column).astype(BF)
                back = (grad_active * gate_column * slope).astype(BF)
                hidden_grad[at, :] = back
                lane = lax.broadcasted_iota(jnp.int32, (CHUNK, EXTRA), 1)
                gate_grad = jnp.sum(grad_active * bowed, -1, keepdims=True)
                made_back[at, width : width + EXTRA] = jnp.where(
                    lane == pair * count + expert, gate_grad, 0.0
                ).astype(BF)
                made[at, :] = dot(active[at, :], outer[slot]).astype(BF)
                made_back[at, 0:width] = contract_cols(back, inner[slot]).astype(BF)
                return carry

            lax.fori_loop(0, capacity // CHUNK, chunk, 0)
            for third in range(3):
                at = pl.ds(third * CHUNK, CHUNK)
                sum_out[at, :] += contract_rows(active[:, at], grads[...])
                sum_in[at, :] += contract_rows(picked[:, at], hidden_grad[...])

            def give(block, carry):
                choose = (ranks[block, line, :] == slots).astype(BF)
                at = pl.ds(pl.multiple_of(block * TILE, TILE), TILE)
                total_ref[block] = (total_ref[block].astype(F32) + contract_rows(choose, made[at, :])).astype(BF)
                back_ref[block] = (back_ref[block].astype(F32) + contract_rows(choose, made_back[at, :])).astype(BF)
                return carry

            lax.fori_loop(0, blocks, give, 0, unroll=2)
            return carry

        lax.fori_loop(0, passes, one_pass, 0)
        if expert >= 2:
            for copy in stores(expert - 2, slot):
                copy.wait()
        stage_in[slot] = sum_in[...].astype(BF)
        stage_out[slot] = sum_out[...].astype(BF)
        for copy in stores(expert, slot):
            copy.start()
    for expert in range(max(count - 2, 0), count):
        for copy in stores(expert, expert % 2):
            copy.wait()


def expert_pass(place, rows, cot, own_in, got_in, own_out, got_out):
    blocks, length, width = cot.shape
    count, _, hidden = got_in.shape
    capacity = blocks * TILE
    shape = jax.ShapeDtypeStruct
    anywhere = pl.BlockSpec(memory_space=pl.ANY)
    vmem = pl.BlockSpec(memory_space=pltpu.VMEM)
    return pl.pallas_call(
        expert_kernel,
        out_shape=(
            shape((blocks, length, width), BF),
            shape((blocks, length, width + EXTRA), BF),
            shape((count, width, hidden), BF),
            shape((count, hidden, width), BF),
        ),
        in_specs=[pl.BlockSpec(memory_space=pltpu.SMEM), vmem, vmem] + [anywhere] * 4,
        out_specs=(vmem, vmem, anywhere, anywhere),
        scratch_shapes=[
            pltpu.VMEM((2, width, hidden), BF),
            pltpu.VMEM((2, hidden, width), BF),
            pltpu.VMEM((capacity, width), BF),
            pltpu.VMEM((capacity, width), BF),
            pltpu.VMEM((capacity, EXTRA), F32),
            pltpu.VMEM((capacity, hidden), BF),
            pltpu.VMEM((capacity, hidden), BF),
            pltpu.VMEM((capacity, width), BF),
            pltpu.VMEM((capacity, width + EXTRA), BF),
            pltpu.VMEM((blocks, 16, length), F32),
            pltpu.VMEM((width, hidden), F32),
            pltpu.VMEM((hidden, width), F32),
            pltpu.VMEM((2, width, hidden), BF),
            pltpu.VMEM((2, hidden, width), BF),
            pltpu.SemaphoreType.DMA((2, 4)),
            pltpu.SemaphoreType.DMA((2, 2)),
        ],
        compiler_params=pltpu.CompilerParams(vmem_limit_bytes=BIG),
        cost_estimate=pl.CostEstimate(flops=50 * 10**9, bytes_accessed=5 * 10**7, transcendentals=10**6),
        name="experts",
    )(place, rows, cot, own_in, got_in, own_out, got_out)


def back_kernel(
    moe_ref, cot_ref, x_ref, middle_ref, sent_ref, prob_ref, attended_ref, packed_ref, normed_ref,
    small_ref, qkv_ref, out_ref, router_ref,
    tokens_ref, grad_qkv, grad_out, grad_small, grad_router,
    stacked, projected,
):
    rows, width = x_ref.shape
    images = rows // PAD
    group = 3 * HEAD_DIM
    groups = width // group
    scale = HEAD_DIM ** (-0.5)
    experts = 8
    lane = lax.broadcasted_iota(jnp.int32, (PAD, EXTRA), 1)
    sums = [jnp.zeros((1, width), F32) for _ in range(4)]
    router_sum = jnp.zeros((EXTRA, width), F32)
    lanes = lax.broadcasted_iota(jnp.int32, (PAD, group), 1) // HEAD_DIM
    for image in range(images):
        at = pl.ds(image * PAD, PAD)
        moe = moe_ref[at, :].astype(F32)
        first_flags = sent_ref[at, width : width + EXTRA].astype(F32)
        chosen = jnp.where(lane < experts, pltpu.roll(first_flags, EXTRA - experts, 1), 0.0)
        probs = prob_ref[at, :]
        asked = moe[:, width:] * chosen
        grad_logits = probs * (asked - jnp.sum(probs * asked, -1, keepdims=True))
        coarse = grad_logits.astype(BF)
        fine = (grad_logits - coarse.astype(F32)).astype(BF)
        normed_b = sent_ref[at, 0:width]
        router_sum = router_sum + contract_rows(coarse, normed_b) + contract_rows(fine, normed_b)
        routed = contract_cols(coarse, router_ref[...]) + contract_cols(fine, router_ref[...])
        grad = moe[:, :width] + routed
        unit, inverse = norm_parts(middle_ref[at, :])
        sums[2] = sums[2] + jnp.sum(grad * unit, 0, keepdims=True)
        sums[3] = sums[3] + jnp.sum(grad, 0, keepdims=True)
        grad_middle = cot_ref[at, :].astype(F32) + norm_back(grad, unit, inverse, small_ref[2:3, :])
        grad_proj = grad_middle.astype(BF)
        projected[at, :] = grad_proj
        for double in range(groups // 2):
            made = []
            packed = packed_ref[at, pl.ds(double * 6 * group, 6 * group)]
            for side in range(2):
                query, keys, values = (
                    packed[:, (3 * side + k) * group : (3 * side + k + 1) * group] for k in range(3)
                )
                index = double * 2 + side
                grad_att = contract_cols(grad_proj, out_ref[pl.ds(index * group, group), :]).astype(BF)
                outs = [jnp.zeros((PAD, group), F32) for _ in range(3)]
                for head in range(3):
                    mask = lanes == head
                    probs = head_probs(jnp.where(mask, query, jnp.zeros_like(query)), keys, scale)
                    part = jnp.where(mask, grad_att, jnp.zeros_like(grad_att))
                    grad_weights = contract_cols(part, values)
                    inner_sum = jnp.sum(probs * grad_weights, -1, keepdims=True)
                    grad_scores = (probs * (grad_weights - inner_sum)).astype(BF)
                    outs[0] = jnp.where(mask, dot(grad_scores, keys), outs[0])
                    outs[1] = jnp.where(mask, contract_rows(grad_scores, query), outs[1])
                    outs[2] = jnp.where(mask, contract_rows(probs.astype(BF), grad_att), outs[2])
                made += [outs[0] * scale, outs[1] * scale, outs[2]]
            stacked[at, pl.ds(double * 6 * group, 6 * group)] = jnp.concatenate(made, 1).astype(BF)
        grad = contract_cols(stacked[at, :], qkv_ref[...])
        unit, inverse = norm_parts(x_ref[at, :].astype(F32))
        sums[0] = sums[0] + jnp.sum(grad * unit, 0, keepdims=True)
        sums[1] = sums[1] + jnp.sum(grad, 0, keepdims=True)
        tokens_ref[at, :] = (grad_middle + norm_back(grad, unit, inverse, small_ref[0:1, :])).astype(BF)
    grad_router[...] = router_sum[0:experts, :]
    for index in range(4):
        grad_small[index : index + 1, :] = sums[index]
    grad_out[...] = contract_rows(attended_ref[...], projected[...]).astype(BF)
    for third in range(3):
        cols = pl.ds(third * width, width)
        grad_qkv[:, cols] = contract_rows(normed_ref[...], stacked[:, cols]).astype(BF)


def back(moe, cot, x, middle, sent, prob, attended, packed, normed, small, qkv, out, router):
    rows, width = x.shape
    shape = jax.ShapeDtypeStruct
    return pl.pallas_call(
        back_kernel,
        out_shape=(
            shape((rows, width), BF),
            shape((width, 3 * width), BF),
            shape((width, width), BF),
            shape((4, width), F32),
            shape((8, width), F32),
        ),
        scratch_shapes=[pltpu.VMEM((rows, 3 * width), BF), pltpu.VMEM((rows, width), BF)],
        compiler_params=pltpu.CompilerParams(vmem_limit_bytes=BIG),
        cost_estimate=pl.CostEstimate(flops=16 * 10**9, bytes_accessed=2 * 10**7, transcendentals=10**6),
        name="back",
    )(moe, cot, x, middle, sent, prob, attended, packed, normed, small, qkv, out, router)


class Comm:
    def __init__(self):
        self.sizes = tuple(lax.axis_size(axis) for axis in AXES)
        self.shard = lax.axis_index("shard")
        self.head = lax.axis_index("heads")
        self.tensor = lax.axis_index("tensor")
        self.pair = self.head % 2

    def move(self, value, step):
        shards, heads, tensors = self.sizes
        pairs = []
        for s in range(shards):
            for h in range(heads):
                for t in range(tensors):
                    to = step(s, h, t)
                    if 0 <= to[2] < tensors:
                        source = (s * heads + h) * tensors + t
                        pairs.append((source, (to[0] * heads + to[1]) * tensors + to[2]))
        return lax.ppermute(value, AXES, pairs)

    def over_core(self, value):
        return self.move(value, lambda s, h, t: (s, h ^ 1, t))

    def over_heads(self, value):
        return self.move(value, lambda s, h, t: (s, (h + 2) % 4, t))

    def over_shard(self, value):
        return self.move(value, lambda s, h, t: (1 - s, h, t))

    def up(self, value):
        return self.move(value, lambda s, h, t: (s, h, t + 1))

    def down(self, value):
        return self.move(value, lambda s, h, t: (s, h, t - 1))

    def halves(self, value, index, axis):
        size = value.shape[axis] // 2
        mine = lax.dynamic_slice_in_dim(value, index * size, size, axis)
        other = lax.dynamic_slice_in_dim(value, (1 - index) * size, size, axis)
        return mine, other

    def join(self, mine, other, index, axis):
        first = jnp.where(index == 0, mine, other)
        second = jnp.where(index == 0, other, mine)
        return jnp.concatenate((first, second), axis)

    def gather_shard(self, value, axis):
        if self.sizes[0] != 2:
            return lax.all_gather(value, "shard", axis=axis, tiled=True)
        return self.join(value, self.over_shard(value), self.shard, axis)

    def gather_shard_split(self, value, axis, cut):
        if self.sizes[0] != 2:
            return lax.all_gather(value, "shard", axis=axis, tiled=True)
        mine, _ = self.halves(value, self.pair, cut)
        got = self.over_shard(mine)
        both = self.join(got, self.over_core(got), self.pair, cut)
        return self.join(value, both, self.shard, axis)

    def scatter_shard(self, value, axis):
        if self.sizes[0] != 2:
            return lax.psum_scatter(value.astype(BF), "shard", scatter_dimension=axis, tiled=True).astype(F32)
        mine, other = self.halves(value, self.shard, axis)
        return mine.astype(F32) + self.over_shard(other.astype(BF)).astype(F32)

    def scatter_core(self, value, axis):
        mine, other = self.halves(value, self.pair, axis)
        return mine.astype(F32) + self.over_core(other.astype(BF)).astype(F32)

    def scatter_heads(self, value, axis):
        mine, other = self.halves(value, self.head // 2, axis)
        return mine.astype(F32) + self.over_heads(other.astype(BF)).astype(F32)

    def line_gather(self, value):
        ups, downs = [value], [value]
        for _ in range(3):
            ups.append(self.up(ups[-1]))
            downs.append(self.down(downs[-1]))
        out = [value]
        for back in (1, 2, 3):
            out.append(jnp.where(self.tensor >= back, ups[back], downs[4 - back]))
        return out

    def line_scatter(self, parts):
        high, low = parts[1].astype(BF), parts[3].astype(BF)
        high = (parts[2].astype(F32) + self.up(high).astype(F32)).astype(BF)
        low = (parts[2].astype(F32) + self.down(low).astype(F32)).astype(BF)
        high = (parts[3].astype(F32) + self.up(high).astype(F32)).astype(BF)
        low = (parts[1].astype(F32) + self.down(low).astype(F32)).astype(BF)
        return parts[0].astype(F32) + self.up(high).astype(F32) + self.down(low).astype(F32)


def local(
    tokens, ln1_gain, ln1_bias, qkv_weight, out_weight, ln2_gain, ln2_bias, router_weight,
    expert_in, expert_out, route_noise, expert_ids, cotangent,
):
    comm = Comm()
    rows, width = tokens.shape
    experts = expert_in.shape[0]
    images = rows // SEQ
    half = experts // 2
    padded = images * PAD

    def pad(value, lanes=0, fill=0):
        value = value.reshape(images, SEQ, value.shape[1])
        value = jnp.pad(value, ((0, 0), (0, PAD - SEQ), (0, lanes)), constant_values=fill)
        return value.reshape(padded, value.shape[2])

    def unpad(value):
        return value.reshape(images, PAD, value.shape[1])[:, :SEQ].reshape(rows, value.shape[1])

    smalls = jnp.concatenate(
        (ln1_gain[None], ln1_bias[None], ln2_gain[None], ln2_bias[None], router_weight.T), 0
    )
    smalls = comm.gather_shard(smalls, 1)
    gains = smalls[:4].astype(F32)
    router = jnp.pad(smalls[4:].T, ((0, 0), (0, EXTRA - experts)))
    dense = jnp.concatenate((qkv_weight, out_weight), 1)
    dense = comm.gather_shard_split(dense, 0, 1)
    proj_qkv, proj_out = dense[:, : 3 * width], dense[:, 3 * width :]
    own_in = lax.dynamic_slice_in_dim(expert_in, comm.pair * half, half, 0)
    own_out = lax.dynamic_slice_in_dim(expert_out, comm.pair * half, half, 0)
    cot = pad(cotangent)
    grad_rows = jnp.stack(comm.line_gather(cot), 0)
    grad_rows = jnp.concatenate((grad_rows, comm.over_core(grad_rows)), 0)
    if comm.sizes[0] == 2:
        place = jnp.stack((comm.pair, comm.shard)).astype(jnp.int32)
        weights = (expert_in, comm.over_shard(own_in), expert_out, comm.over_shard(own_out))
    else:
        place = jnp.stack((0 * comm.pair, 0 * comm.shard)).astype(jnp.int32)
        place = place.at[0].set(comm.pair)
        inner = lax.all_gather(own_in, "shard", axis=1, tiled=True)
        outer = lax.all_gather(own_out, "shard", axis=2, tiled=True)
        inner = jnp.concatenate((inner, inner), 0)
        outer = jnp.concatenate((outer, outer), 0)
        middle_cut = width // 2
        weights = (
            inner[:, :middle_cut], inner[:half, middle_cut:], outer[:, :, :middle_cut], outer[:half, :, middle_cut:]
        )

    x = pad(tokens)
    normed_a, packed, attended, middle, sent, prob = front(
        x, gains, proj_qkv, proj_out, router, pad(route_noise, EXTRA - experts), pad(expert_ids, 0, -1)
    )
    rows_all = jnp.stack(comm.line_gather(sent), 0)
    rows_all = jnp.concatenate((rows_all, comm.over_core(rows_all)), 0)
    total, back_all, grads_in, grads_out = expert_pass(place, rows_all, grad_rows, *weights)

    def reduce_expert(grad, axis, other):
        part = comm.scatter_shard(grad, axis)
        part = comm.scatter_heads(part, other).astype(BF)
        return comm.join(part, comm.over_heads(part), comm.head // 2, other)

    inner_grads = [reduce_expert(grads_in[e], 0, 1) for e in range(half)]
    outer_grads = [reduce_expert(grads_out[e], 1, 0) for e in range(half)]

    def collect(value):
        value = value[:4].astype(F32) + comm.over_core(value[4:]).astype(F32)
        return comm.line_scatter([value[k] for k in range(4)])

    moe_grad = collect(back_all)
    moe = collect(total)
    mixed = (unpad(middle) + unpad(moe)).astype(BF)
    grad_tokens, grad_qkv, grad_out, grad_small, grad_router = back(
        moe_grad, cot, x, middle, sent, prob, attended, packed, normed_a, gains, proj_qkv, proj_out, router
    )
    grad_tokens = unpad(grad_tokens)

    small = jnp.concatenate((grad_small, grad_router), 0).T.astype(BF)
    small = jnp.pad(small, ((0, 0), (0, 128 - small.shape[1])))
    shares = jnp.concatenate((grad_qkv, grad_out, small, jnp.zeros_like(small)), 1)
    shares = comm.scatter_core(shares, 1)
    shares = comm.scatter_shard(shares, 0)
    shares = comm.scatter_heads(shares, 1)
    cut = shares.shape[0] // 4
    rolled = [
        lax.dynamic_slice_in_dim(shares, ((comm.tensor + 4 - k) % 4) * cut, cut, 0) for k in range(4)
    ]
    summed = comm.line_scatter(rolled).astype(BF)
    pieces = comm.line_gather(summed)
    whole = jnp.zeros(shares.shape, BF)
    for k in range(4):
        whole = lax.dynamic_update_slice_in_dim(whole, pieces[k], ((comm.tensor + 4 - k) % 4) * cut, 0)
    whole = comm.join(whole, comm.over_heads(whole), comm.head // 2, 1)
    whole = comm.join(whole, comm.over_core(whole), comm.pair, 1).astype(F32)
    small = whole[:, 4 * width : 4 * width + 128]

    grad_in, grad_outer = jnp.stack(inner_grads, 0), jnp.stack(outer_grads, 0)
    grad_in = comm.join(grad_in, comm.over_core(grad_in), comm.pair, 0).astype(F32)
    grad_outer = comm.join(grad_outer, comm.over_core(grad_outer), comm.pair, 0).astype(F32)
    return (
        mixed,
        grad_tokens,
        small[:, 0],
        small[:, 1],
        whole[:, : 3 * width],
        whole[:, 3 * width : 4 * width],
        small[:, 2],
        small[:, 3],
        small[:, 4 : 4 + experts],
        grad_in,
        grad_outer,
    )


def solution(mesh):
    split = P(AXES, None)
    vector, matrix = P("shard"), P("shard", None)
    inner, outer = P(None, "shard", "tensor"), P(None, "tensor", "shard")
    return jax.shard_map(
        local,
        mesh=mesh,
        in_specs=(
            split, vector, vector, matrix, matrix, vector, vector, matrix, inner, outer, split, split, split,
        ),
        out_specs=(
            split, split, vector, vector, matrix, matrix, vector, vector, matrix, inner, outer,
        ),
        check_vma=False,
    )
```

time: 1000 us -> 766 us (0.77)
  matrix products: 266 us -> 0 us
  local copies, waits for them, and re-layouts: 280 us -> 74.4 us
  waiting for transfers between devices: 170 us -> 349 us
  Pallas kernels: 0 us -> 113 us
  other arithmetic: 118 us -> 74.8 us
    dot_general x38 -> x0, matrix products: 262 us -> none  [the longest x10 77.2 us: contract_cols(): lax.dot_general(left, right, (((1,), (1,)), ((), ())), preferred_element_...]
    ppermute x76, waiting for transfers between devices: 170 us -> 349 us  [move(): return lax.ppermute(value, AXES, pairs)]
    pallas_call x0 -> x3, Pallas kernels: none -> 113 us  [the longest x1 75 us: expert_pass(): pl.pallas_call(expert_kernel, out_shape=(shape((blocks, length, width), B...]
    unnamed x311 -> x112, local copies, waits for them, and re-layouts: 54.7 us -> 17.1 us
    ppermute x20 -> x1, local copies, waits for them, and re-layouts: 35.7 us -> 1.14 us  [move(): return lax.ppermute(value, AXES, pairs)]
    concatenate x6 -> x1, local copies, waits for them, and re-layouts: 27.2 us -> 0.01 us  [local(): jnp.concatenate((grad_qkv, grad_out, small, jnp.zeros_like(small)), 1)]
    concatenate x1, local copies, waits for them, and re-layouts: 30.6 us -> 4.13 us  [local(): rows_all = jnp.concatenate((rows_all, comm.over_core(rows_all)), 0)]
    concatenate x1, local copies, waits for them, and re-layouts: 25.7 us -> 0.17 us  [local(): grad_rows = jnp.concatenate((grad_rows, comm.over_core(grad_rows)), 0)]
  transfers between devices with their start and end apart: 76 -> 76, of which waited for: 29 -> 37; matrix products, arithmetic and copies ran while one was open for 47% -> 16% of each run, Pallas kernels for 0% -> 5%
where the time goes in v2:
time: 766 us; the launch traced here: 756 us
  waiting for transfers between devices  349 us (46%)
  starting transfers between devices  141 us (18%)
  Pallas kernels  113 us (15%)
  other arithmetic  74.8 us (10%)
  local copies, waits for them, and re-layouts  74.4 us (10%)
    ppermute x76, waiting for transfers between devices, move(): return lax.ppermute(value, AXES, pairs)  349 us
    ppermute x76, starting transfers between devices, move(): return lax.ppermute(value, AXES, pairs)  141 us
    pallas_call x1, Pallas kernels, expert_pass(): pl.pallas_call(expert_kernel, out_shape=(shape((blocks, length, width), B...  75 us
    pallas_call x1, Pallas kernels, back(): pl.pallas_call(back_kernel, out_shape=(shape((rows, width), BF), shape((w...  26.8 us
    unnamed x112, local copies, waits for them, and re-layouts  17.1 us
  transfers between devices with their start and end apart: 76, of which 37 were waited for; matrix products, arithmetic and copies ran while one was open for 16% of the time, Pallas kernels for 5%

profile of v2, /device:TPU:17, one launch (start us, length us, event | category | flops | bytes accessed | tf_op | source)
XLA Modules:
  0.0 755.5 jit_solution(10235379935192943536)
XLA Ops:
  5.0 25.7 %collective-permute-done.1 = bf16[384,1536]{1,0:T(8,128)(2,1)} collective-permute-done((bf16[384,1536]{1,0:T(8,128)(2,1)S(1)}, bf16[384,1536]{1,0:T(8,128)(2,1)}, u32[]{:S(2)}, u32[]{:S(2)}) %collective-permute-start.1) | collective-permute-done | bytes 1179680 | tf_op jit(solution)/shard_map/ppermute | solution.py:410
  51.4 11.0 %front.1 = (bf16[416,768]{1,0:T(8,128)(2,1)}, bf16[416,2304]{1,0:T(8,128)(2,1)}, bf16[416,768]{1,0:T(8,128)(2,1)}, f32[416,768]{1,0:T(8,128)}, bf16[416,896]{1,0:T(8,128)(2,1)}, /*index=5*/f32[416,128]{1,0:T(8,128)}) custom-call(bf16[416,768]{1,0:T(8,128)(2,1)} %bitcast.157, f32[4,768]{1,0:T(4,128)} %maximum_convert_fusion.4.small_ref, ...), custom_call_target="tpu_custom_call" | custom-call | flops 8000000000 | bytes 10000000 | tf_op jit(solution)/shard_map/front/pallas_call | solution.py:115
  73.9 8.4 %collective-permute-done.4 = bf16[416,896]{1,0:T(8,128)(2,1)S(1)} collective-permute-done((bf16[416,896]{1,0:T(8,128)(2,1)}, bf16[416,896]{1,0:T(8,128)(2,1)S(1)}, u32[]{:S(2)}, u32[]{:S(2)}) %collective-permute-start.4) | collective-permute-done | bytes 745504 | tf_op jit(solution)/shard_map/ppermute | solution.py:410
  87.7 8.4 %collective-permute-done.12 = bf16[416,768]{1,0:T(8,128)(2,1)} collective-permute-done((bf16[416,768]{1,0:T(8,128)(2,1)}, bf16[416,768]{1,0:T(8,128)(2,1)}, u32[]{:S(2)}, u32[]{:S(2)}) %collective-permute-start.12) | collective-permute-done | bytes 639008 | tf_op jit(solution)/shard_map/ppermute | solution.py:410
  102.3 8.9 %collective-permute-done.14 = bf16[416,768]{1,0:T(8,128)(2,1)} collective-permute-done((bf16[416,768]{1,0:T(8,128)(2,1)}, bf16[416,768]{1,0:T(8,128)(2,1)}, u32[]{:S(2)}, u32[]{:S(2)}) %collective-permute-start.14) | collective-permute-done | bytes 639008 | tf_op jit(solution)/shard_map/ppermute | solution.py:410
  116.5 9.2 %collective-permute-done.13 = bf16[416,768]{1,0:T(8,128)(2,1)} collective-permute-done((bf16[416,768]{1,0:T(8,128)(2,1)}, bf16[416,768]{1,0:T(8,128)(2,1)}, u32[]{:S(2)}, u32[]{:S(2)}) %collective-permute-start.13) | collective-permute-done | bytes 639008 | tf_op jit(solution)/shard_map/ppermute | solution.py:410
  130.8 10.8 %collective-permute-done.6 = bf16[416,896]{1,0:T(8,128)(2,1)S(1)} collective-permute-done((bf16[416,896]{1,0:T(8,128)(2,1)S(1)}, bf16[416,896]{1,0:T(8,128)(2,1)S(1)}, u32[]{:S(2)}, u32[]{:S(2)}) %collective-permute-start.6) | collective-permute-done | bytes 745504 | tf_op jit(solution)/shard_map/ppermute | solution.py:410
  143.2 13.5 %collective-permute-done.8 = bf16[416,896]{1,0:T(8,128)(2,1)S(1)} collective-permute-done((bf16[416,896]{1,0:T(8,128)(2,1)}, bf16[416,896]{1,0:T(8,128)(2,1)S(1)}, u32[]{:S(2)}, u32[]{:S(2)}) %collective-permute-start.8) | collective-permute-done | bytes 745504 | tf_op jit(solution)/shard_map/ppermute | solution.py:410
  177.6 44.0 %collective-permute-done.17.got_in = bf16[4,384,768]{2,1,0:T(8,128)(2,1)S(1)} collective-permute-done((bf16[4,384,768]{2,1,0:T(8,128)(2,1)S(1)}, bf16[4,384,768]{2,1,0:T(8,128)(2,1)S(1)}, u32[]{:S(2)}, u32[]{:S(2)}) %collective-permute-start.17) | collective-permute-done | bytes 2359328 | tf_op jit(solution)/shard_map/ppermute | solution.py:410
  223.0 49.2 %collective-permute-done.18.got_out = bf16[4,768,384]{2,1,0:T(8,128)(2,1)} collective-permute-done((bf16[4,768,384]{2,1,0:T(8,128)(2,1)S(1)}, bf16[4,768,384]{2,1,0:T(8,128)(2,1)}, u32[]{:S(2)}, u32[]{:S(2)}) %collective-permute-start.18) | collective-permute-done | bytes 2359328 | tf_op jit(solution)/shard_map/ppermute | solution.py:410
  272.2 75.0 %experts.1 = (bf16[8,416,768]{2,1,0:T(8,128)(2,1)}, bf16[8,416,896]{2,1,0:T(8,128)(2,1)}, bf16[4,768,768]{2,1,0:T(8,128)(2,1)}, bf16[4,768,768]{2,1,0:T(8,128)(2,1)}) custom-call(s32[2]{0:T(128)} %pad_add_fusion.place_ref, bf16[8,416,896]{2,1,0:T(8,128)(2,1)} %copy-done.35, bf16[8,416,768]{2,1,0:T(8,128)(2,1)} %copy-done.38, bf16[8,384,768]{2,1,0:T(8,128)(2,1)} %own_in.1, ...), custom_call_target="tpu_custom_call" | custom-call | flops 49999998976 | bytes 50000000 | tf_op jit(solution)/shard_map/experts/pallas_call | solution.py:267
  360.4 12.2 %collective-permute-done.59 = bf16[384,768]{1,0:T(8,128)(2,1)S(1)} collective-permute-done((bf16[384,768]{1,0:T(8,128)(2,1)S(1)}, bf16[384,768]{1,0:T(8,128)(2,1)S(1)}, u32[]{:S(2)}, u32[]{:S(2)}) %collective-permute-start.59) | collective-permute-done | bytes 589856 | tf_op jit(solution)/shard_map/ppermute | solution.py:410
  372.9 12.3 %collective-permute-done.56 = bf16[384,768]{1,0:T(8,128)(2,1)S(1)} collective-permute-done((bf16[384,768]{1,0:T(8,128)(2,1)S(1)}, bf16[384,768]{1,0:T(8,128)(2,1)S(1)}, u32[]{:S(2)}, u32[]{:S(2)}) %collective-permute-start.56) | collective-permute-done | bytes 589856 | tf_op jit(solution)/shard_map/ppermute | solution.py:410
  385.5 12.4 %collective-permute-done.53 = bf16[384,768]{1,0:T(8,128)(2,1)S(1)} collective-permute-done((bf16[384,768]{1,0:T(8,128)(2,1)S(1)}, bf16[384,768]{1,0:T(8,128)(2,1)S(1)}, u32[]{:S(2)}, u32[]{:S(2)}) %collective-permute-start.53) | collective-permute-done | bytes 589856 | tf_op jit(solution)/shard_map/ppermute | solution.py:410
  398.2 12.4 %collective-permute-done.50 = bf16[384,768]{1,0:T(8,128)(2,1)S(1)} collective-permute-done((bf16[384,768]{1,0:T(8,128)(2,1)S(1)}, bf16[384,768]{1,0:T(8,128)(2,1)S(1)}, u32[]{:S(2)}, u32[]{:S(2)}) %collective-permute-start.50) | collective-permute-done | bytes 589856 | tf_op jit(solution)/shard_map/ppermute | solution.py:410
  425.7 5.3 collective-permute-done.27
  438.7 9.8 %collective-permute-done.66 = bf16[768,384]{1,0:T(8,128)(2,1)S(1)} collective-permute-done((bf16[768,384]{1,0:T(8,128)(2,1)S(1)}, bf16[768,384]{1,0:T(8,128)(2,1)S(1)}, u32[]{:S(2)}, u32[]{:S(2)}) %collective-permute-start.66) | collective-permute-done | bytes 589856 | tf_op jit(solution)/shard_map/ppermute | solution.py:410
  449.8 11.3 %collective-permute-done.63 = bf16[768,384]{1,0:T(8,128)(2,1)S(1)} collective-permute-done((bf16[768,384]{1,0:T(8,128)(2,1)S(1)}, bf16[768,384]{1,0:T(8,128)(2,1)S(1)}, u32[]{:S(2)}, u32[]{:S(2)}) %collective-permute-start.63) | collective-permute-done | bytes 589856 | tf_op jit(solution)/shard_map/ppermute | solution.py:410
  473.6 7.7 %collective-permute-done.32 = bf16[416,896]{1,0:T(8,128)(2,1)S(1)} collective-permute-done((bf16[416,896]{1,0:T(8,128)(2,1)S(1)}, bf16[416,896]{1,0:T(8,128)(2,1)S(1)}, u32[]{:S(2)}, u32[]{:S(2)}) %collective-permute-start.32) | collective-permute-done | bytes 745504 | tf_op jit(solution)/shard_map/ppermute | solution.py:410
  484.6 26.8 %back.1 = (bf16[416,768]{1,0:T(8,128)(2,1)}, bf16[768,2304]{1,0:T(8,128)(2,1)}, bf16[768,768]{1,0:T(8,128)(2,1)}, f32[4,768]{1,0:T(4,128)}, f32[8,768]{1,0:T(8,128)}) custom-call(f32[416,896]{1,0:T(8,128)} %fusion.6.moe_ref, bf16[416,768]{1,0:T(8,128)(2,1)} %bitcast.152, bf16[416,768]{1,0:T(8,128)(2,1)} %bitcast.158, ...), custom_call_target="tpu_custom_call" | custom-call | flops 16000000000 | bytes 20000000 | tf_op jit(solution)/shard_map/back/pallas_call | solution.py:376
  582.8 10.0 %collective-permute-done.34 = bf16[384,1664]{1,0:T(8,128)(2,1)S(1)} collective-permute-done((bf16[384,1664]{1,0:T(8,128)(2,1)S(1)}, bf16[384,1664]{1,0:T(8,128)(2,1)S(1)}, u32[]{:S(2)}, u32[]{:S(2)}) %collective-permute-start.34) | collective-permute-done | bytes 1277984 | tf_op jit(solution)/shard_map/ppermute | solution.py:410
  599.7 9.5 %collective-permute-done.35 = bf16[384,832]{0,1:T(8,128)(2,1)S(1)} collective-permute-done((bf16[384,832]{0,1:T(8,128)(2,1)}, bf16[384,832]{0,1:T(8,128)(2,1)S(1)}, u32[]{:S(2)}, u32[]{:S(2)}) %collective-permute-start.35) | collective-permute-done | bytes 639008 | tf_op jit(solution)/shard_map/ppermute | solution.py:410
  643.0 10.7 %collective-permute-done.38 = bf16[96,832]{1,0:T(8,128)(2,1)S(1)} collective-permute-done((bf16[96,832]{1,0:T(8,128)(2,1)S(1)}, bf16[96,832]{1,0:T(8,128)(2,1)S(1)}, u32[]{:S(2)}, u32[]{:S(2)}) %collective-permute-start.38) | collective-permute-done | bytes 159776 | tf_op jit(solution)/shard_map/ppermute | solution.py:410
  722.9 6.5 collective-permute-start.49
  (396 shorter events, 341.3 us)
Async XLA Ops:
  35.9 31.9 %collective-permute-start.11 = (bf16[416,768]{1,0:T(8,128)(2,1)S(1)}, bf16[416,768]{1,0:T(8,128)(2,1)}, u32[]{:S(2)}, u32[]{:S(2)}) collective-permute-start(bf16[416,768]{1,0:T(8,128)(2,1)S(1)} %bitcast.148), channel_id=1, source_target_pairs={{1,0},{2,1},{3,2},{5,4},{6,5},{7,6},{9,8},{10,9},{11,10},{13,12},{... | collective-permute-start | bytes 1916936 | tf_op jit(solution)/shard_map/ppermute | solution.py:410
  82.4 32.2 %collective-permute-start.5 = (bf16[416,896]{1,0:T(8,128)(2,1)S(1)}, bf16[416,896]{1,0:T(8,128)(2,1)S(1)}, u32[]{:S(2)}, u32[]{:S(2)}) collective-permute-start(bf16[416,896]{1,0:T(8,128)(2,1)S(1)} %collective-permute-done.4), channel_id=1, source_target_pairs={{1,0},{2,1},{3,2},{5,4},{6,5},{7,6},{9,8},{10,9},{11,10},{13,12},{... | collective-permute-start | bytes 2236424 | tf_op jit(solution)/shard_map/ppermute | solution.py:410
  96.0 29.7 %collective-permute-start.13 = (bf16[416,768]{1,0:T(8,128)(2,1)}, bf16[416,768]{1,0:T(8,128)(2,1)}, u32[]{:S(2)}, u32[]{:S(2)}) collective-permute-start(bf16[416,768]{1,0:T(8,128)(2,1)} %collective-permute-done.12), channel_id=1, source_target_pairs={{1,0},{2,1},{3,2},{5,4},{6,5},{7,6},{9,8},{10,9},{11,10},{13,12},{... | collective-permute-start | bytes 1916936 | tf_op jit(solution)/shard_map/ppermute | solution.py:410
  98.0 30.2 %collective-permute-start.7 = (bf16[416,896]{1,0:T(8,128)(2,1)S(1)}, bf16[416,896]{1,0:T(8,128)(2,1)}, u32[]{:S(2)}, u32[]{:S(2)}) collective-permute-start(bf16[416,896]{1,0:T(8,128)(2,1)S(1)} %collective-permute-done.3), channel_id=1, source_target_pairs={{0,1},{1,2},{2,3},{4,5},{5,6},{6,7},{8,9},{9,10},{10,11},{12,13},{... | collective-permute-start | bytes 2236424 | tf_op jit(solution)/shard_map/ppermute | solution.py:410
  111.2 49.7 %collective-permute-start.15 = (bf16[416,768]{1,0:T(8,128)(2,1)}, bf16[416,768]{1,0:T(8,128)(2,1)S(1)}, u32[]{:S(2)}, u32[]{:S(2)}) collective-permute-start(bf16[416,768]{1,0:T(8,128)(2,1)} %collective-permute-done.14), channel_id=1, source_target_pairs={{0,1},{1,2},{2,3},{4,5},{5,6},{6,7},{8,9},{9,10},{10,11},{12,13},{... | collective-permute-start | bytes 1916936 | tf_op jit(solution)/shard_map/ppermute | solution.py:410
  168.6 52.9 %collective-permute-start.17 = (bf16[4,384,768]{2,1,0:T(8,128)(2,1)S(1)}, bf16[4,384,768]{2,1,0:T(8,128)(2,1)S(1)}, u32[]{:S(2)}, u32[]{:S(2)}) collective-permute-start(bf16[4,384,768]{2,1,0:T(8,128)(2,1)S(1)} %constant_dynamic-slice_fusion.2), channel_id=1, source_target_pairs={{0,16},{1,17},{2,18},{3,19},{4,20},{5,21},{6,22},{7,23},{8,24},{9,... | collective-permute-start | bytes 7077896 | tf_op jit(solution)/shard_map/ppermute | solution.py:410
  171.4 100.8 %collective-permute-start.18 = (bf16[4,768,384]{2,1,0:T(8,128)(2,1)S(1)}, bf16[4,768,384]{2,1,0:T(8,128)(2,1)}, u32[]{:S(2)}, u32[]{:S(2)}) collective-permute-start(bf16[4,768,384]{2,1,0:T(8,128)(2,1)S(1)} %constant_dynamic-slice_fusion.1), channel_id=1, source_target_pairs={{0,16},{1,17},{2,18},{3,19},{4,20},{5,21},{6,22},{7,23},{8,24},{9,... | collective-permute-start | bytes 7077896 | tf_op jit(solution)/shard_map/ppermute | solution.py:410
  350.9 59.7 %collective-permute-start.26 = (bf16[4,416,896]{2,1,0:T(8,128)(2,1)}, bf16[4,416,896]{2,1,0:T(8,128)(2,1)}, u32[]{:S(2)}, u32[]{:S(2)}) collective-permute-start(bf16[4,416,896]{2,1,0:T(8,128)(2,1)} %slice.121), channel_id=1, source_target_pairs={{0,4},{1,5},{2,6},{3,7},{4,0},{5,1},{6,2},{7,3},{8,12},{9,13},{10,... | collective-permute-start | bytes 8945672 | tf_op jit(solution)/shard_map/ppermute | solution.py:410
  355.3 272.0 %collective-permute-start.19 = (bf16[4,416,768]{2,1,0:T(8,128)(2,1)}, bf16[4,416,768]{2,1,0:T(8,128)(2,1)}, u32[]{:S(2)}, u32[]{:S(2)}) collective-permute-start(bf16[4,416,768]{2,1,0:T(8,128)(2,1)} %slice.114), channel_id=1, source_target_pairs={{0,4},{1,5},{2,6},{3,7},{4,0},{5,1},{6,2},{7,3},{8,12},{9,13},{10,... | collective-permute-start | bytes 7667720 | tf_op jit(solution)/shard_map/ppermute | solution.py:410
  359.9 38.1 %collective-permute-start.53 = (bf16[384,768]{1,0:T(8,128)(2,1)S(1)}, bf16[384,768]{1,0:T(8,128)(2,1)S(1)}, u32[]{:S(2)}, u32[]{:S(2)}) collective-permute-start(bf16[384,768]{1,0:T(8,128)(2,1)S(1)} %dynamic-slice_bitcast_fusion.6), channel_id=1, source_target_pairs={{0,16},{1,17},{2,18},{3,19},{4,20},{5,21},{6,22},{7,23},{8,24},{9,... | collective-permute-start | bytes 1769480 | tf_op jit(solution)/shard_map/ppermute | solution.py:410
  372.6 37.9 %collective-permute-start.50 = (bf16[384,768]{1,0:T(8,128)(2,1)S(1)}, bf16[384,768]{1,0:T(8,128)(2,1)S(1)}, u32[]{:S(2)}, u32[]{:S(2)}) collective-permute-start(bf16[384,768]{1,0:T(8,128)(2,1)S(1)} %dynamic-slice_bitcast_fusion.7), channel_id=1, source_target_pairs={{0,16},{1,17},{2,18},{3,19},{4,20},{5,21},{6,22},{7,23},{8,24},{9,... | collective-permute-start | bytes 1769480 | tf_op jit(solution)/shard_map/ppermute | solution.py:410
  385.3 37.9 %collective-permute-start.72 = (bf16[768,384]{1,0:T(8,128)(2,1)S(1)}, bf16[768,384]{1,0:T(8,128)(2,1)S(1)}, u32[]{:S(2)}, u32[]{:S(2)}) collective-permute-start(bf16[768,384]{1,0:T(8,128)(2,1)S(1)} %dynamic-slice_bitcast_fusion), channel_id=1, source_target_pairs={{0,16},{1,17},{2,18},{3,19},{4,20},{5,21},{6,22},{7,23},{8,24},{9,... | collective-permute-start | bytes 1769480 | tf_op jit(solution)/shard_map/ppermute | solution.py:410
  397.9 37.9 %collective-permute-start.69 = (bf16[768,384]{1,0:T(8,128)(2,1)S(1)}, bf16[768,384]{1,0:T(8,128)(2,1)S(1)}, u32[]{:S(2)}, u32[]{:S(2)}) collective-permute-start(bf16[768,384]{1,0:T(8,128)(2,1)S(1)} %dynamic-slice_bitcast_fusion.1), channel_id=1, source_target_pairs={{0,16},{1,17},{2,18},{3,19},{4,20},{5,21},{6,22},{7,23},{8,24},{9,... | collective-permute-start | bytes 1769480 | tf_op jit(solution)/shard_map/ppermute | solution.py:410
  431.0 30.1 %collective-permute-start.63 = (bf16[768,384]{1,0:T(8,128)(2,1)S(1)}, bf16[768,384]{1,0:T(8,128)(2,1)S(1)}, u32[]{:S(2)}, u32[]{:S(2)}) collective-permute-start(bf16[768,384]{1,0:T(8,128)(2,1)S(1)} %dynamic-slice_bitcast_fusion.3), channel_id=1, source_target_pairs={{0,16},{1,17},{2,18},{3,19},{4,20},{5,21},{6,22},{7,23},{8,24},{9,... | collective-permute-start | bytes 1769480 | tf_op jit(solution)/shard_map/ppermute | solution.py:410
  433.2 29.2 %collective-permute-start.28 = (bf16[416,896]{1,0:T(8,128)(2,1)S(1)}, bf16[416,896]{1,0:T(8,128)(2,1)S(1)}, u32[]{:S(2)}, u32[]{:S(2)}) collective-permute-start(bf16[416,896]{1,0:T(8,128)(2,1)S(1)} %get-tuple-element.103), channel_id=1, source_target_pairs={{0,1},{1,2},{2,3},{4,5},{5,6},{6,7},{8,9},{9,10},{10,11},{12,13},{... | collective-permute-start | bytes 2236424 | tf_op jit(solution)/shard_map/ppermute | solution.py:410
  470.6 48.2 %collective-permute-start.54 = (bf16[384,384]{1,0:T(8,128)(2,1)}, bf16[384,384]{1,0:T(8,128)(2,1)}, u32[]{:S(2)}, u32[]{:S(2)}) collective-permute-start(bf16[384,384]{1,0:T(8,128)(2,1)} %dynamic-slice_convert_fusion.8), channel_id=1, source_target_pairs={{0,8},{1,9},{2,10},{3,11},{4,12},{5,13},{6,14},{7,15},{8,0},{9,1},... | collective-permute-start | bytes 884744 | tf_op jit(solution)/shard_map/ppermute | solution.py:410
  471.6 51.3 %collective-permute-start.51 = (bf16[384,384]{1,0:T(8,128)(2,1)}, bf16[384,384]{1,0:T(8,128)(2,1)}, u32[]{:S(2)}, u32[]{:S(2)}) collective-permute-start(bf16[384,384]{1,0:T(8,128)(2,1)} %dynamic-slice_convert_fusion.9), channel_id=1, source_target_pairs={{0,8},{1,9},{2,10},{3,11},{4,12},{5,13},{6,14},{7,15},{8,0},{9,1},... | collective-permute-start | bytes 884744 | tf_op jit(solution)/shard_map/ppermute | solution.py:410
  481.3 43.9 %collective-permute-start.73 = (bf16[384,384]{1,0:T(8,128)(2,1)}, bf16[384,384]{1,0:T(8,128)(2,1)}, u32[]{:S(2)}, u32[]{:S(2)}) collective-permute-start(bf16[384,384]{1,0:T(8,128)(2,1)} %dynamic-slice_convert_fusion.2), channel_id=1, source_target_pairs={{0,8},{1,9},{2,10},{3,11},{4,12},{5,13},{6,14},{7,15},{8,0},{9,1},... | collective-permute-start | bytes 884744 | tf_op jit(solution)/shard_map/ppermute | solution.py:410
  483.0 43.7 %collective-permute-start.70 = (bf16[384,384]{1,0:T(8,128)(2,1)}, bf16[384,384]{1,0:T(8,128)(2,1)}, u32[]{:S(2)}, u32[]{:S(2)}) collective-permute-start(bf16[384,384]{1,0:T(8,128)(2,1)} %dynamic-slice_convert_fusion.3), channel_id=1, source_target_pairs={{0,8},{1,9},{2,10},{3,11},{4,12},{5,13},{6,14},{7,15},{8,0},{9,1},... | collective-permute-start | bytes 884744 | tf_op jit(solution)/shard_map/ppermute | solution.py:410
  518.8 45.6 %collective-permute-start.33 = (bf16[768,1664]{1,0:T(8,128)(2,1)S(1)}, bf16[768,1664]{1,0:T(8,128)(2,1)S(1)}, u32[]{:S(2)}, u32[]{:S(2)}) collective-permute-start(bf16[768,1664]{1,0:T(8,128)(2,1)S(1)} %constant_dynamic-slice_fusion), channel_id=1, source_target_pairs={{0,4},{1,5},{2,6},{3,7},{4,0},{5,1},{6,2},{7,3},{8,12},{9,13},{10,... | collective-permute-start | bytes 7667720 | tf_op jit(solution)/shard_map/ppermute | solution.py:410
  575.7 94.4 %collective-permute-start.62 = (bf16[4,384,768]{2,1,0:T(8,128)(2,1)}, bf16[4,384,768]{2,1,0:T(8,128)(2,1)}, u32[]{:S(2)}, u32[]{:S(2)}) collective-permute-start(bf16[4,384,768]{2,1,0:T(8,128)(2,1)} %pad_maximum_fusion.3), channel_id=1, source_target_pairs={{0,4},{1,5},{2,6},{3,7},{4,0},{5,1},{6,2},{7,3},{8,12},{9,13},{10,... | collective-permute-start | bytes 7077896 | tf_op jit(solution)/shard_map/ppermute | solution.py:410
  617.8 92.1 %collective-permute-start.75 = (bf16[4,768,384]{2,1,0:T(8,128)(2,1)}, bf16[4,768,384]{2,1,0:T(8,128)(2,1)}, u32[]{:S(2)}, u32[]{:S(2)}) collective-permute-start(bf16[4,768,384]{2,1,0:T(8,128)(2,1)} %pad_maximum_fusion.4), channel_id=1, source_target_pairs={{0,4},{1,5},{2,6},{3,7},{4,0},{5,1},{6,2},{7,3},{8,12},{9,13},{10,... | collective-permute-start | bytes 7077896 | tf_op jit(solution)/shard_map/ppermute | solution.py:410
  668.2 44.6 %collective-permute-start.21 = (bf16[416,768]{1,0:T(8,128)(2,1)}, bf16[416,768]{1,0:T(8,128)(2,1)}, u32[]{:S(2)}, u32[]{:S(2)}) collective-permute-start(bf16[416,768]{1,0:T(8,128)(2,1)} %get-tuple-element.109), channel_id=1, source_target_pairs={{0,1},{1,2},{2,3},{4,5},{5,6},{6,7},{8,9},{9,10},{10,11},{12,13},{... | collective-permute-start | bytes 1916936 | tf_op jit(solution)/shard_map/ppermute | solution.py:410
  670.1 42.6 %collective-permute-start.24 = (bf16[416,768]{1,0:T(8,128)(2,1)}, bf16[416,768]{1,0:T(8,128)(2,1)}, u32[]{:S(2)}, u32[]{:S(2)}) collective-permute-start(bf16[416,768]{1,0:T(8,128)(2,1)} %get-tuple-element.110), channel_id=1, source_target_pairs={{1,0},{2,1},{3,2},{5,4},{6,5},{7,6},{9,8},{10,9},{11,10},{13,12},{... | collective-permute-start | bytes 1916936 | tf_op jit(solution)/shard_map/ppermute | solution.py:410
  (106 other events, 1775.1 us)

commit v3 on v2

v3 whole, which is shorter than its diff:
```python
import jax
import jax.numpy as jnp
from jax import lax
from jax.experimental import pallas as pl
from jax.experimental.pallas import tpu as pltpu
from jax.sharding import PartitionSpec as P

HEAD_DIM = 64
SEQ = 197
EPS = 1e-06
AXES = ("shard", "heads", "tensor")
BF = jnp.bfloat16
F32 = jnp.float32


def contract_rows(left, right):
    return lax.dot_general(left, right, (((0,), (0,)), ((), ())), preferred_element_type=F32)


def contract_cols(left, right):
    return lax.dot_general(left, right, (((1,), (1,)), ((), ())), preferred_element_type=F32)


PAD = 208
TILE = 128
CHUNK = 256
FAR = 512.0
TALL = 16
LANES = 128
MASKED = -1e30
CUBIC = 0.044715
ROOT = (2.0 / 3.141592653589793) ** 0.5
BIG = 60 * 1024 * 1024
MESH = pl.DeviceIdType.MESH


def dot(left, right):
    return jnp.dot(left, right, preferred_element_type=F32)


def norm_parts(values):
    centred = values - jnp.mean(values, -1, keepdims=True)
    inverse = lax.rsqrt(jnp.mean(centred * centred, -1, keepdims=True) + EPS)
    return centred * inverse, inverse


def norm_back(grad, unit, inverse, gain):
    scaled = grad * gain
    along = jnp.mean(scaled * unit, -1, keepdims=True)
    return inverse * (scaled - jnp.mean(scaled, -1, keepdims=True) - unit * along)


def head_probs(query, keys, scale):
    scores = contract_cols(query, keys) * scale
    column = lax.broadcasted_iota(jnp.int32, scores.shape, 1)
    scores = jnp.where(column < SEQ, scores, MASKED)
    raised = jnp.exp(scores - jnp.max(scores, -1, keepdims=True))
    return raised / jnp.sum(raised, -1, keepdims=True)


def gain_row(small_ref, experts, index):
    row = slice(experts + index, experts + index + 1)
    return jnp.concatenate((small_ref[0, row, :], small_ref[1, row, :]), 1).astype(F32)


def router_rows(small_ref):
    return jnp.concatenate((small_ref[0], small_ref[1]), 1)


def attend(normed, at, qkv_ref, packed_ref):
    width = normed.shape[1]
    group = 3 * HEAD_DIM
    scale = HEAD_DIM ** (-0.5)
    lane = lax.broadcasted_iota(jnp.int32, (PAD, group), 1) // HEAD_DIM
    outs = []
    for double in range(width // group // 2):
        cols = pl.ds(double * 6 * group, 6 * group)
        packed = dot(normed, qkv_ref[:, cols])
        packed_ref[at, cols] = packed.astype(BF)
        for side in range(2):
            query, keys, values = (
                packed[:, (3 * side + k) * group : (3 * side + k + 1) * group].astype(BF)
                for k in range(3)
            )
            total = jnp.zeros((PAD, group), F32)
            for head in range(3):
                mask = lane == head
                probs = head_probs(jnp.where(mask, query, jnp.zeros_like(query)), keys, scale)
                total = jnp.where(mask, dot(probs.astype(BF), values), total)
            outs.append(total)
    return jnp.concatenate(outs, 1).astype(BF)


def route(normed, small_ref, noise, ids, experts):
    logits = contract_cols(router_rows(small_ref), normed) + noise
    row = lax.broadcasted_iota(jnp.int32, logits.shape, 0)
    logits = jnp.where(row < experts, logits, MASKED)
    raised = jnp.exp(logits - jnp.max(logits, 0, keepdims=True))
    probs = raised / jnp.sum(raised, 0, keepdims=True)
    chosen = ((row == ids[0:1]) | (row == ids[1:2])).astype(F32)
    shifted = row - experts
    flags = (((shifted == ids[0:1]) | (shifted == ids[1:2])) & (shifted >= 0)).astype(F32)
    return probs, probs * chosen + flags


def front_image(image, experts, x_ref, small_ref, qkv_ref, out_ref, noise_ref, ids_ref, keep):
    normed_ref, packed_ref, attended_ref, middle_ref = keep
    at = pl.ds(image * PAD, PAD)
    x = x_ref[at, :].astype(F32)
    unit, _ = norm_parts(x)
    normed = (unit * gain_row(small_ref, experts, 0) + gain_row(small_ref, experts, 1)).astype(BF)
    normed_ref[at, :] = normed
    attended = attend(normed, at, qkv_ref, packed_ref)
    attended_ref[at, :] = attended
    middle = x + dot(attended, out_ref[...])
    middle_ref[at, :] = middle
    unit, _ = norm_parts(middle)
    normed = (unit * gain_row(small_ref, experts, 2) + gain_row(small_ref, experts, 3)).astype(BF)
    cols = slice(image * PAD, (image + 1) * PAD)
    probs, flags = route(normed, small_ref, noise_ref[:, cols], ids_ref[:, cols], experts)
    return normed, probs, flags


def front_kernel(
    x_ref, small_ref, qkv_ref, out_ref, noise_ref, ids_ref,
    normed_ref, packed_ref, attended_ref, middle_ref, rows_ref, flag_ref, prob_ref,
):
    keep = (normed_ref, packed_ref, attended_ref, middle_ref)
    probs, flags = [], []
    for image in range(x_ref.shape[0] // PAD):
        normed, prob, flag = front_image(
            image, TALL // 2, x_ref, small_ref, qkv_ref, out_ref, noise_ref, ids_ref, keep
        )
        rows_ref[pl.ds(image * PAD, PAD), :] = normed
        probs.append(prob)
        flags.append(flag)
    prob_ref[...] = jnp.concatenate(probs, 1)
    flag_ref[...] = jnp.concatenate(flags, 1).astype(BF)


def front(x, small, qkv, out, noise, ids):
    rows, width = x.shape
    shape = jax.ShapeDtypeStruct
    return pl.pallas_call(
        front_kernel,
        out_shape=(
            shape((rows, width), BF),
            shape((rows, 3 * width), BF),
            shape((rows, width), BF),
            shape((rows, width), F32),
            shape((rows, width), BF),
            shape((TALL, rows), BF),
            shape((TALL, rows), F32),
        ),
        compiler_params=pltpu.CompilerParams(vmem_limit_bytes=BIG),
        cost_estimate=pl.CostEstimate(flops=8 * 10**9, bytes_accessed=10**7, transcendentals=10**6),
        name="front",
    )(x, small, qkv, out, noise, ids)


class Place:
    def __init__(self):
        shard, head, tensor = (lax.axis_index(axis) for axis in AXES)
        self.shard, self.head, self.tensor = shard, head, tensor
        self.pair, self.side = lax.rem(head, 2), lax.div(head, 2)
        self.across = (1 - shard, head, tensor)
        self.beside = (shard, lax.rem(head + 2, 4), tensor)
        self.twin = (shard, head + 1 - 2 * self.pair, tensor)
        self.above = (shard, head, lax.rem(tensor + 1, 4))
        self.below = (shard, head, lax.rem(tensor + 3, 4))

    def greet(self):
        barrier = pltpu.get_barrier_semaphore()
        for device in (self.across, self.beside, self.twin, self.above, self.below):
            pl.semaphore_signal(barrier, inc=1, device_id=device, device_id_type=MESH)
        pl.semaphore_wait(barrier, 5)


class Links:
    def __init__(self, send, recv):
        self.send, self.recv, self.used = send, recv, 0
        self.sent = []

    def copy(self, source, target, device):
        index = self.used
        self.used += 1
        return pltpu.make_async_remote_copy(
            src_ref=source, dst_ref=target, send_sem=self.send.at[index], recv_sem=self.recv.at[index],
            device_id=device, device_id_type=MESH,
        )

    def start(self, source, target, device):
        copy = self.copy(source, target, device)
        copy.start()
        self.sent.append((None, copy))
        return copy

    def finish(self):
        for when, copy in self.sent:
            if when is None:
                copy.wait_send()
            else:
                pl.when(when)(copy.wait_send)


class LineGather:
    def __init__(self, links, place, view, own, parts):
        self.links, self.place, self.view, self.own = links, place, view, own
        self.copies = {}
        self.parts = parts

    def start(self, part, step):
        t = self.place.tensor
        for name, slot, device, sends in (
            ("up", t - step, self.place.above, (t >= step) & (t < 3)),
            ("down", t + step, self.place.below, (t + step <= 3) & (t > 0)),
        ):
            slot = jnp.clip(slot, 0, 3)
            source = self.own(part) if step == 0 else self.view(slot, part)
            copy = self.links.copy(source, self.view(slot, part), device)
            pl.when(sends)(copy.start)
            self.links.sent.append((sends, copy))
            self.copies[name, part, step] = copy

    def wait(self, part, step, then=None):
        t = self.place.tensor
        for name, slot, comes in (("up", t - 1 - step, t >= step + 1), ("down", t + 1 + step, t + 1 + step <= 3)):
            copy = self.copies[name, part, step]

            @pl.when(comes)
            def _():
                copy.wait_recv()

    def arrived(self, step):
        t = self.place.tensor
        return (
            (jnp.clip(t - 1 - step, 0, 3), t >= step + 1),
            (jnp.clip(t + 1 + step, 0, 3), t + 1 + step <= 3),
        )


def head_kernel(
    x_ref, cot_ref, small_own, qkv_own, out_own, expert_in, expert_out, noise_ref, ids_ref,
    small_ref, qkv_ref, out_ref, normed_ref, packed_ref, attended_ref, middle_ref, prob_ref,
    rows_all, flags_all, cot_all, got_in, got_out,
    sent_rows, sent_flags, send, recv, local_sem,
):
    place = Place()
    links = Links(send, recv)
    width = x_ref.shape[1]
    experts = expert_in.shape[0]
    depth = qkv_own.shape[0]
    quarter = depth // 4
    shard, pair, side, tensor = place.shard, place.pair, place.side, place.tensor
    mine = pair * 4 + tensor
    place.greet()

    def dense_rows(owner, across_side, across_pair, start, size):
        return pl.ds(pl.multiple_of(owner * depth + (across_side * 2 + across_pair) * quarter + start, TALL), size)

    pieces = ((qkv_own, qkv_ref, 0, quarter // 2), (qkv_own, qkv_ref, quarter // 2, quarter // 2), (out_own, out_ref, 0, quarter))
    smalls = links.start(small_own, small_ref.at[shard], place.across)
    cross = []
    for own, full, start, size in pieces:
        source = own.at[pl.ds(pl.multiple_of((side * 2 + pair) * quarter + start, TALL), size), :]
        cross.append(links.start(source, full.at[dense_rows(shard, side, pair, start, size), :], place.across))
    here = pl.ds(pl.multiple_of(shard * depth, TALL), depth)
    locals_ = [
        pltpu.make_async_copy(qkv_own, qkv_ref.at[here, :], local_sem.at[0]),
        pltpu.make_async_copy(out_own, out_ref.at[here, :], local_sem.at[1]),
        pltpu.make_async_copy(small_own, small_ref.at[shard], local_sem.at[2]),
        pltpu.make_async_copy(cot_ref, cot_all.at[mine], local_sem.at[3]),
    ]
    for copy in locals_:
        copy.start()

    def slots(array):
        def view(slot, part):
            return array.at[pair * 4 + slot, pl.ds(part * PAD, PAD), :]

        return view

    cot_line = LineGather(links, place, slots(cot_all), lambda part: cot_ref.at[pl.ds(part * PAD, PAD), :], 2)
    for part in range(2):
        cot_line.start(part, 0)

    beside, twins = [], []
    for index, (own, full, start, size) in enumerate(pieces):
        cross[index].wait_recv()
        rows = full.at[dense_rows(1 - shard, side, pair, start, size), :]
        beside.append(links.start(rows, rows, place.beside))
        twins.append(links.start(rows, rows, place.twin))
    for index, (own, full, start, size) in enumerate(pieces):
        beside[index].wait_recv()
        rows = full.at[dense_rows(1 - shard, 1 - side, pair, start, size), :]
        twins.append(links.start(rows, rows, place.twin))

    def expert_item(item):
        index = side * 2 + item // 2
        source, target = (expert_in, got_in) if item % 2 == 0 else (expert_out, got_out)
        return source.at[pair * (experts // 2) + index], target.at[index]

    fetched = [links.start(*expert_item(item), place.across) for item in range(4)]
    for part in range(2):
        cot_line.wait(part, 0)
        cot_line.start(part, 1)
    smalls.wait_recv()
    for copy in twins:
        copy.wait_recv()
    for copy in locals_:
        copy.wait()

    keep = (normed_ref, packed_ref, attended_ref, middle_ref)
    row_line = LineGather(links, place, slots(rows_all), lambda part: sent_rows.at[pl.ds(part * PAD, PAD), :], 2)
    flag_line = LineGather(links, place, lambda slot, part: flags_all.at[pair * 4 + slot], lambda part: sent_flags, 1)
    probs, flags = [], []
    twin_rows = []
    forwarded = []

    def forward_expert(item):
        fetched[item].wait_recv()
        _, target = expert_item(item)
        forwarded.append(links.start(target, target, place.beside))

    for image in range(2):
        normed, prob, flag = front_image(
            image, experts, x_ref, small_ref, qkv_ref, out_ref, noise_ref, ids_ref, keep
        )
        at = pl.ds(image * PAD, PAD)
        sent_rows[at, :] = normed
        row_line.start(image, 0)
        twin_rows.append(links.start(sent_rows.at[at, :], rows_all.at[mine, at, :], place.twin))
        probs.append(prob)
        flags.append(flag)
        if image == 0:
            for part in range(2):
                cot_line.wait(part, 1)
                cot_line.start(part, 2)
    prob_ref[...] = jnp.concatenate(probs, 1)
    sent_flags[...] = jnp.concatenate(flags, 1).astype(BF)
    flag_line.start(0, 0)
    twin_flags = [links.start(sent_flags, flags_all.at[mine], place.twin)]
    keep_own = [
        pltpu.make_async_copy(sent_rows, rows_all.at[mine], local_sem.at[0]),
        pltpu.make_async_copy(sent_flags, flags_all.at[mine], local_sem.at[1]),
    ]
    for copy in keep_own:
        copy.start()

    def share(line, array, part, step, copies, whole):
        for slot, comes in line.arrived(step):
            index = pair * 4 + slot
            ref = array.at[index] if whole else array.at[index, pl.ds(part * PAD, PAD), :]
            copy = links.copy(ref, ref, place.twin)
            pl.when(comes)(copy.start)
            links.sent.append((comes, copy))
            copies.append((comes, copy))

    twin_steps = []
    forward_expert(0)
    for step in range(3):
        for part in range(2):
            row_line.wait(part, step)
            if step < 2:
                row_line.start(part, step + 1)
            share(row_line, rows_all, part, step, twin_steps, False)
        flag_line.wait(0, step)
        if step < 2:
            flag_line.start(0, step + 1)
        share(flag_line, flags_all, 0, step, twin_steps, True)
        if step == 0:
            for part in range(2):
                cot_line.wait(part, 2)
            ours = cot_all.at[pl.ds(pair * 4, 4)]
            twin_cot = links.start(ours, ours, place.twin)
        forward_expert(step + 1)

    for copy in twin_rows + twin_flags + [twin_cot] + forwarded:
        copy.wait_recv()
    for comes, copy in twin_steps:
        pl.when(comes)(copy.wait_recv)
    for copy in keep_own:
        copy.wait()
    links.finish()


def head(x, cot, small, qkv, out, expert_in, expert_out, noise, ids):
    rows, width = x.shape
    depth = qkv.shape[0]
    count = expert_in.shape[0] // 2
    shape = jax.ShapeDtypeStruct
    anywhere = pl.BlockSpec(memory_space=pl.ANY)
    vmem = pl.BlockSpec(memory_space=pltpu.VMEM)
    return pl.pallas_call(
        head_kernel,
        out_shape=(
            shape((2, TALL, depth), BF),
            shape((width, 3 * width), BF),
            shape((width, width), BF),
            shape((rows, width), BF),
            shape((rows, 3 * width), BF),
            shape((rows, width), BF),
            shape((rows, width), F32),
            shape((TALL, rows), F32),
            shape((8, rows, width), BF),
            shape((8, TALL, rows), BF),
            shape((8, rows, width), BF),
            shape((count,) + expert_in.shape[1:], BF),
            shape((count,) + expert_out.shape[1:], BF),
        ),
        in_specs=[vmem] * 3 + [anywhere] * 4 + [vmem] * 2,
        out_specs=(vmem,) * 8 + (anywhere,) * 5,
        scratch_shapes=[
            pltpu.VMEM((rows, width), BF),
            pltpu.VMEM((TALL, rows), BF),
            pltpu.SemaphoreType.DMA((96,)),
            pltpu.SemaphoreType.DMA((96,)),
            pltpu.SemaphoreType.DMA((4,)),
        ],
        compiler_params=pltpu.CompilerParams(vmem_limit_bytes=BIG, collective_id=1, has_side_effects=True),
        cost_estimate=pl.CostEstimate(flops=8 * 10**9, bytes_accessed=3 * 10**7, transcendentals=10**6),
        name="head",
    )(x, cot, small, qkv, out, expert_in, expert_out, noise, ids)


def expert_kernel(
    place_ref, rows_ref, flag_ref, cot_ref, own_in, got_in, own_out, got_out,
    total_ref, back_ref, gate_ref, grad_in, grad_out,
    inner, outer, picked, grads, gate, active, hidden_grad, made, made_back, made_gate, ranks, sum_in, sum_out,
    stage_in, stage_out, load_sem, store_sem,
):
    blocks, length, width = cot_ref.shape
    count = got_in.shape[0]
    depth = got_in.shape[1]
    pair, shard = place_ref[0], place_ref[1]
    experts = 2 * count
    capacity = blocks * TILE

    def loads(expert, slot):
        mine = pl.ds(pl.multiple_of(shard * depth, LANES), depth)
        other = pl.ds(pl.multiple_of((1 - shard) * depth, LANES), depth)
        index = pair * count + expert
        return (
            pltpu.make_async_copy(own_in.at[index], inner.at[slot, mine, :], load_sem.at[slot, 0]),
            pltpu.make_async_copy(got_in.at[expert], inner.at[slot, other, :], load_sem.at[slot, 1]),
            pltpu.make_async_copy(own_out.at[index], outer.at[slot, :, mine], load_sem.at[slot, 2]),
            pltpu.make_async_copy(got_out.at[expert], outer.at[slot, :, other], load_sem.at[slot, 3]),
        )

    def stores(expert, slot):
        return (
            pltpu.make_async_copy(stage_in.at[slot], grad_in.at[expert], store_sem.at[slot, 0]),
            pltpu.make_async_copy(stage_out.at[slot], grad_out.at[expert], store_sem.at[slot, 1]),
        )

    for copy in loads(0, 0):
        copy.start()
    ahead = lax.broadcasted_iota(jnp.int32, (length, length), 0)
    behind = lax.broadcasted_iota(jnp.int32, (length, length), 1)
    order = jnp.where(behind < ahead, 1.0, jnp.where(behind == ahead, FAR, 0.0)).astype(BF)

    def rank(block, carry):
        ranks[block] = contract_cols(flag_ref[block], order) - FAR
        total_ref[block] = jnp.zeros(total_ref.shape[1:], BF)
        back_ref[block] = jnp.zeros(back_ref.shape[1:], BF)
        gate_ref[block] = jnp.zeros(gate_ref.shape[1:], BF)
        return carry

    lax.fori_loop(0, blocks, rank, 0)

    for expert in range(count):
        slot = expert % 2
        if expert + 1 < count:
            for copy in loads(expert + 1, 1 - slot):
                copy.start()
        line = pl.ds(experts + pair * count + expert, 1)
        highest = ranks[0, line, :]
        for block in range(1, blocks):
            highest = jnp.maximum(highest, ranks[block, line, :])
        passes = (jnp.maximum(jnp.max(highest), -1.0).astype(jnp.int32) + TILE) // TILE
        sum_in[...] = jnp.zeros(sum_in.shape, F32)
        sum_out[...] = jnp.zeros(sum_out.shape, F32)
        for copy in loads(expert, slot):
            copy.wait()

        def one_pass(step, carry):
            base = (step * TILE).astype(F32)
            slots = lax.broadcasted_iota(jnp.int32, (TILE, length), 0).astype(F32) + base

            def take(block, carry):
                choose = (ranks[block, line, :] == slots).astype(BF)
                at = pl.ds(pl.multiple_of(block * TILE, TILE), TILE)
                picked[at, :] = dot(choose, rows_ref[block]).astype(BF)
                grads[at, :] = dot(choose, cot_ref[block]).astype(BF)
                columns = contract_cols(choose, flag_ref[block])
                lane = lax.broadcasted_iota(jnp.int32, (TILE, TALL), 1)
                column = jnp.where(lane == pair * count + expert, columns, 0.0)
                gate[at, :] = jnp.broadcast_to(jnp.sum(column, -1, keepdims=True), (TILE, LANES))
                return carry

            lax.fori_loop(0, blocks, take, 0, unroll=2)

            def chunk(index, carry):
                at = pl.ds(pl.multiple_of(index * CHUNK, CHUNK), CHUNK)
                value = dot(picked[at, :], inner[slot])
                grad_active = contract_cols(grads[at, :], outer[slot])
                gate_column = gate[at, 0:1]
                square = value * value
                bent = jnp.tanh(ROOT * value * (1.0 + CUBIC * square))
                plus = 0.5 * (1.0 + bent)
                bowed = value * plus
                slope = plus + (0.5 * ROOT) * value * (1.0 - bent * bent) * (1.0 + (3.0 * CUBIC) * square)
                active[at, :] = (bowed * gate_column).astype(BF)
                back = (grad_active * gate_column * slope).astype(BF)
                hidden_grad[at, :] = back
                lane = lax.broadcasted_iota(jnp.int32, (CHUNK, TALL), 1)
                gate_grad = jnp.sum(grad_active * bowed, -1, keepdims=True)
                made_gate[at, :] = jnp.where(lane == pair * count + expert, gate_grad, 0.0).astype(BF)
                made[at, :] = dot(active[at, :], outer[slot]).astype(BF)
                made_back[at, :] = contract_cols(back, inner[slot]).astype(BF)
                return carry

            lax.fori_loop(0, capacity // CHUNK, chunk, 0)
            hidden = sum_in.shape[1]
            for start in range(0, hidden, CHUNK):
                at = pl.ds(start, CHUNK)
                sum_out[at, :] += contract_rows(active[:, at], grads[...])
            for start in range(0, width, CHUNK):
                at = pl.ds(start, CHUNK)
                sum_in[at, :] += contract_rows(picked[:, at], hidden_grad[...])

            def give(block, carry):
                choose = (ranks[block, line, :] == slots).astype(BF)
                at = pl.ds(pl.multiple_of(block * TILE, TILE), TILE)
                total_ref[block] = (total_ref[block].astype(F32) + contract_rows(choose, made[at, :])).astype(BF)
                back_ref[block] = (back_ref[block].astype(F32) + contract_rows(choose, made_back[at, :])).astype(BF)
                gate_ref[block] = (gate_ref[block].astype(F32) + contract_rows(made_gate[at, :], choose)).astype(BF)
                return carry

            lax.fori_loop(0, blocks, give, 0, unroll=2)
            return carry

        lax.fori_loop(0, passes, one_pass, 0)
        if expert >= 2:
            for copy in stores(expert - 2, slot):
                copy.wait()
        stage_in[slot] = sum_in[...].astype(BF)
        stage_out[slot] = sum_out[...].astype(BF)
        for copy in stores(expert, slot):
            copy.start()
    for expert in range(max(count - 2, 0), count):
        for copy in stores(expert, expert % 2):
            copy.wait()


def expert_pass(place, rows, flags, cot, own_in, got_in, own_out, got_out):
    blocks, length, width = cot.shape
    count, _, hidden = got_in.shape
    capacity = blocks * TILE
    shape = jax.ShapeDtypeStruct
    anywhere = pl.BlockSpec(memory_space=pl.ANY)
    vmem = pl.BlockSpec(memory_space=pltpu.VMEM)
    return pl.pallas_call(
        expert_kernel,
        out_shape=(
            shape((blocks, length, width), BF),
            shape((blocks, length, width), BF),
            shape((blocks, TALL, length), BF),
            shape((count, width, hidden), BF),
            shape((count, hidden, width), BF),
        ),
        in_specs=[pl.BlockSpec(memory_space=pltpu.SMEM), vmem, vmem, vmem] + [anywhere] * 4,
        out_specs=(vmem, vmem, vmem, anywhere, anywhere),
        scratch_shapes=[
            pltpu.VMEM((2, width, hidden), BF),
            pltpu.VMEM((2, hidden, width), BF),
            pltpu.VMEM((capacity, width), BF),
            pltpu.VMEM((capacity, width), BF),
            pltpu.VMEM((capacity, LANES), F32),
            pltpu.VMEM((capacity, hidden), BF),
            pltpu.VMEM((capacity, hidden), BF),
            pltpu.VMEM((capacity, width), BF),
            pltpu.VMEM((capacity, width), BF),
            pltpu.VMEM((capacity, TALL), BF),
            pltpu.VMEM((blocks, TALL, length), F32),
            pltpu.VMEM((width, hidden), F32),
            pltpu.VMEM((hidden, width), F32),
            pltpu.VMEM((2, width, hidden), BF),
            pltpu.VMEM((2, hidden, width), BF),
            pltpu.SemaphoreType.DMA((2, 4)),
            pltpu.SemaphoreType.DMA((2, 2)),
        ],
        compiler_params=pltpu.CompilerParams(vmem_limit_bytes=BIG),
        cost_estimate=pl.CostEstimate(flops=50 * 10**9, bytes_accessed=5 * 10**7, transcendentals=10**6),
        name="experts",
    )(place, rows, flags, cot, own_in, got_in, own_out, got_out)


def back_attention(at, grad_proj, packed_ref, out_ref, stacked):
    width = grad_proj.shape[1]
    group = 3 * HEAD_DIM
    scale = HEAD_DIM ** (-0.5)
    lanes = lax.broadcasted_iota(jnp.int32, (PAD, group), 1) // HEAD_DIM
    for double in range(width // group // 2):
        made = []
        packed = packed_ref[at, pl.ds(double * 6 * group, 6 * group)]
        for side in range(2):
            query, keys, values = (
                packed[:, (3 * side + k) * group : (3 * side + k + 1) * group] for k in range(3)
            )
            index = double * 2 + side
            grad_att = contract_cols(grad_proj, out_ref[pl.ds(index * group, group), :]).astype(BF)
            outs = [jnp.zeros((PAD, group), F32) for _ in range(3)]
            for head in range(3):
                mask = lanes == head
                probs = head_probs(jnp.where(mask, query, jnp.zeros_like(query)), keys, scale)
                part = jnp.where(mask, grad_att, jnp.zeros_like(grad_att))
                grad_weights = contract_cols(part, values)
                inner_sum = jnp.sum(probs * grad_weights, -1, keepdims=True)
                grad_scores = (probs * (grad_weights - inner_sum)).astype(BF)
                outs[0] = jnp.where(mask, dot(grad_scores, keys), outs[0])
                outs[1] = jnp.where(mask, contract_rows(grad_scores, query), outs[1])
                outs[2] = jnp.where(mask, contract_rows(probs.astype(BF), grad_att), outs[2])
            made += [outs[0] * scale, outs[1] * scale, outs[2]]
        stacked[at, pl.ds(double * 6 * group, 6 * group)] = jnp.concatenate(made, 1).astype(BF)


def back_middle(at, moe, gates, cot, middle, rows, probs, flags, small_ref, sums):
    experts = TALL // 2
    row = lax.broadcasted_iota(jnp.int32, flags.shape, 0)
    chosen = jnp.where(row < experts, pltpu.roll(flags, experts, 0), 0.0)
    asked = gates * chosen
    grad_logits = probs * (asked - jnp.sum(probs * asked, 0, keepdims=True))
    coarse = grad_logits.astype(BF)
    fine = (grad_logits - coarse.astype(F32)).astype(BF)
    router = router_rows(small_ref)
    sums[4] = sums[4] + dot(coarse, rows) + dot(fine, rows)
    grad = moe + contract_rows(coarse, router) + contract_rows(fine, router)
    unit, inverse = norm_parts(middle)
    sums[2] = sums[2] + jnp.sum(grad * unit, 0, keepdims=True)
    sums[3] = sums[3] + jnp.sum(grad, 0, keepdims=True)
    return cot + norm_back(grad, unit, inverse, gain_row(small_ref, experts, 2))


def back_kernel(
    moe_ref, gate_ref, cot_ref, x_ref, middle_ref, rows_ref, flag_ref, prob_ref, attended_ref, packed_ref, normed_ref,
    small_ref, qkv_ref, out_ref,
    tokens_ref, grad_qkv, grad_out, grad_small,
    stacked, projected,
):
    rows, width = x_ref.shape
    experts = TALL // 2
    sums = [jnp.zeros((1, width), F32) for _ in range(4)] + [jnp.zeros((TALL, width), F32)]
    for image in range(rows // PAD):
        at = pl.ds(image * PAD, PAD)
        cols = slice(image * PAD, (image + 1) * PAD)
        grad_middle = back_middle(
            at, moe_ref[at, :].astype(F32), gate_ref[:, cols].astype(F32), cot_ref[at, :].astype(F32),
            middle_ref[at, :], rows_ref[at, :], prob_ref[:, cols], flag_ref[:, cols].astype(F32), small_ref, sums,
        )
        grad_proj = grad_middle.astype(BF)
        projected[at, :] = grad_proj
        back_attention(at, grad_proj, packed_ref, out_ref, stacked)
        grad = contract_cols(stacked[at, :], qkv_ref[...])
        unit, inverse = norm_parts(x_ref[at, :].astype(F32))
        sums[0] = sums[0] + jnp.sum(grad * unit, 0, keepdims=True)
        sums[1] = sums[1] + jnp.sum(grad, 0, keepdims=True)
        tokens_ref[at, :] = (grad_middle + norm_back(grad, unit, inverse, gain_row(small_ref, experts, 0))).astype(BF)
    grad_small[...] = jnp.concatenate([sums[4][0:experts]] + sums[:4] + [jnp.zeros((4, width), F32)], 0).astype(BF)
    grad_out[...] = contract_rows(attended_ref[...], projected[...]).astype(BF)
    for third in range(3):
        cols = pl.ds(third * width, width)
        grad_qkv[:, cols] = contract_rows(normed_ref[...], stacked[:, cols]).astype(BF)


def back(moe, gates, cot, x, middle, sent, flags, prob, attended, packed, normed, small, qkv, out):
    rows, width = x.shape
    shape = jax.ShapeDtypeStruct
    return pl.pallas_call(
        back_kernel,
        out_shape=(
            shape((rows, width), BF),
            shape((width, 3 * width), BF),
            shape((width, width), BF),
            shape((TALL, width), BF),
        ),
        scratch_shapes=[pltpu.VMEM((rows, 3 * width), BF), pltpu.VMEM((rows, width), BF)],
        compiler_params=pltpu.CompilerParams(vmem_limit_bytes=BIG),
        cost_estimate=pl.CostEstimate(flops=16 * 10**9, bytes_accessed=2 * 10**7, transcendentals=10**6),
        name="back",
    )(moe, gates, cot, x, middle, sent, flags, prob, attended, packed, normed, small, qkv, out)


class Comm:
    def __init__(self):
        self.sizes = tuple(lax.axis_size(axis) for axis in AXES)
        self.shard = lax.axis_index("shard")
        self.head = lax.axis_index("heads")
        self.tensor = lax.axis_index("tensor")
        self.pair = self.head % 2

    def move(self, value, step):
        shards, heads, tensors = self.sizes
        pairs = []
        for s in range(shards):
            for h in range(heads):
                for t in range(tensors):
                    to = step(s, h, t)
                    if 0 <= to[2] < tensors:
                        source = (s * heads + h) * tensors + t
                        pairs.append((source, (to[0] * heads + to[1]) * tensors + to[2]))
        return lax.ppermute(value, AXES, pairs)

    def over_core(self, value):
        return self.move(value, lambda s, h, t: (s, h ^ 1, t))

    def over_heads(self, value):
        return self.move(value, lambda s, h, t: (s, (h + 2) % 4, t))

    def over_shard(self, value):
        return self.move(value, lambda s, h, t: (1 - s, h, t))

    def up(self, value):
        return self.move(value, lambda s, h, t: (s, h, t + 1))

    def down(self, value):
        return self.move(value, lambda s, h, t: (s, h, t - 1))

    def halves(self, value, index, axis):
        size = value.shape[axis] // 2
        mine = lax.dynamic_slice_in_dim(value, index * size, size, axis)
        other = lax.dynamic_slice_in_dim(value, (1 - index) * size, size, axis)
        return mine, other

    def join(self, mine, other, index, axis):
        first = jnp.where(index == 0, mine, other)
        second = jnp.where(index == 0, other, mine)
        return jnp.concatenate((first, second), axis)

    def gather_shard(self, value, axis):
        if self.sizes[0] != 2:
            return lax.all_gather(value, "shard", axis=axis, tiled=True)
        return self.join(value, self.over_shard(value), self.shard, axis)

    def gather_shard_split(self, value, axis, cut):
        if self.sizes[0] != 2:
            return lax.all_gather(value, "shard", axis=axis, tiled=True)
        mine, _ = self.halves(value, self.pair, cut)
        got = self.over_shard(mine)
        both = self.join(got, self.over_core(got), self.pair, cut)
        return self.join(value, both, self.shard, axis)

    def scatter_shard(self, value, axis):
        if self.sizes[0] != 2:
            return lax.psum_scatter(value.astype(BF), "shard", scatter_dimension=axis, tiled=True).astype(F32)
        mine, other = self.halves(value, self.shard, axis)
        return mine.astype(F32) + self.over_shard(other.astype(BF)).astype(F32)

    def scatter_core(self, value, axis):
        mine, other = self.halves(value, self.pair, axis)
        return mine.astype(F32) + self.over_core(other.astype(BF)).astype(F32)

    def scatter_heads(self, value, axis):
        mine, other = self.halves(value, self.head // 2, axis)
        return mine.astype(F32) + self.over_heads(other.astype(BF)).astype(F32)

    def line_gather(self, value):
        ups, downs = [value], [value]
        for _ in range(3):
            ups.append(self.up(ups[-1]))
            downs.append(self.down(downs[-1]))
        out = [value]
        for back in (1, 2, 3):
            out.append(jnp.where(self.tensor >= back, ups[back], downs[4 - back]))
        return out

    def line_scatter(self, parts):
        high, low = parts[1].astype(BF), parts[3].astype(BF)
        high = (parts[2].astype(F32) + self.up(high).astype(F32)).astype(BF)
        low = (parts[2].astype(F32) + self.down(low).astype(F32)).astype(BF)
        high = (parts[3].astype(F32) + self.up(high).astype(F32)).astype(BF)
        low = (parts[1].astype(F32) + self.down(low).astype(F32)).astype(BF)
        return parts[0].astype(F32) + self.up(high).astype(F32) + self.down(low).astype(F32)

    def join_slots(self, values):
        own = jnp.zeros((4,) + values[0].shape, values[0].dtype)
        for back, value in enumerate(values):
            own = lax.dynamic_update_index_in_dim(own, value, (self.tensor + 4 - back) % 4, 0)
        return self.join(own, self.over_core(own), self.pair, 0)

    def collect(self, value):
        mine, other = self.halves(value, self.pair, 0)
        mine = mine.astype(F32) + self.over_core(other).astype(F32)
        return self.line_scatter(
            [lax.dynamic_index_in_dim(mine, (self.tensor + 4 - k) % 4, 0, False) for k in range(4)]
        )


def local(
    tokens, ln1_gain, ln1_bias, qkv_weight, out_weight, ln2_gain, ln2_bias, router_weight,
    expert_in, expert_out, route_noise, expert_ids, cotangent,
):
    comm = Comm()
    rows, width = tokens.shape
    experts = expert_in.shape[0]
    images = rows // SEQ
    half = experts // 2
    padded = images * PAD

    def pad(value):
        value = value.reshape(images, SEQ, value.shape[1])
        return jnp.pad(value, ((0, 0), (0, PAD - SEQ), (0, 0))).reshape(padded, value.shape[2])

    def pad_turned(value, tall, fill):
        value = value.reshape(images, SEQ, value.shape[1]).transpose(2, 0, 1)
        value = jnp.pad(value, ((0, tall - value.shape[0]), (0, 0), (0, PAD - SEQ)), constant_values=fill)
        return value.reshape(tall, padded)

    def unpad(value):
        return value.reshape(images, PAD, value.shape[1])[:, :SEQ].reshape(rows, value.shape[1])

    small = jnp.concatenate(
        (router_weight.T, ln1_gain[None], ln1_bias[None], ln2_gain[None], ln2_bias[None]), 0
    )
    small = jnp.pad(small, ((0, TALL - small.shape[0]), (0, 0)))
    cot, x = pad(cotangent), pad(tokens)
    noise, ids = pad_turned(route_noise, TALL, 0), pad_turned(expert_ids, 8, -1)
    place = jnp.stack((comm.pair, comm.shard if comm.sizes[0] == 2 else 0 * comm.shard)).astype(jnp.int32)
    if comm.sizes[0] == 2:
        (
            small, proj_qkv, proj_out, normed_a, packed, attended, middle, prob,
            rows_all, flags_all, grad_rows, got_in, got_out,
        ) = head(x, cot, small, qkv_weight, out_weight, expert_in, expert_out, noise, ids)
        weights = (expert_in, got_in, expert_out, got_out)
        mine = comm.pair * 4 + comm.tensor
        sent = lax.dynamic_index_in_dim(rows_all, mine, 0, False)
        flags = lax.dynamic_index_in_dim(flags_all, mine, 0, False)
    else:
        small = lax.all_gather(small, "shard", axis=1, tiled=True)
        small = small.reshape(TALL, 2, width // 2).transpose(1, 0, 2)
        proj_qkv = lax.all_gather(qkv_weight, "shard", axis=0, tiled=True)
        proj_out = lax.all_gather(out_weight, "shard", axis=0, tiled=True)
        inner = lax.all_gather(lax.dynamic_slice_in_dim(expert_in, comm.pair * half, half, 0), "shard", axis=1, tiled=True)
        outer = lax.all_gather(lax.dynamic_slice_in_dim(expert_out, comm.pair * half, half, 0), "shard", axis=2, tiled=True)
        cut = width // 2
        weights = (
            jnp.concatenate((inner[:, :cut], inner[:, :cut]), 0), inner[:, cut:],
            jnp.concatenate((outer[:, :, :cut], outer[:, :, :cut]), 0), outer[:, :, cut:],
        )
        normed_a, packed, attended, middle, sent, flags, prob = front(x, small, proj_qkv, proj_out, noise, ids)

        def gather(value):
            return comm.join_slots(comm.line_gather(value))

        grad_rows, rows_all, flags_all = gather(cot), gather(sent), gather(flags)
    total, back_all, gate_all, grads_in, grads_out = expert_pass(place, rows_all, flags_all, grad_rows, *weights)

    def reduce_expert(grad, axis, other):
        part = comm.scatter_shard(grad, axis)
        part = comm.scatter_heads(part, other).astype(BF)
        return comm.join(part, comm.over_heads(part), comm.head // 2, other)

    inner_grads = [reduce_expert(grads_in[e], 0, 1) for e in range(half)]
    outer_grads = [reduce_expert(grads_out[e], 1, 0) for e in range(half)]

    moe_grad = comm.collect(back_all)
    gate_grad = comm.collect(gate_all)
    moe = comm.collect(total)
    mixed = (unpad(middle) + unpad(moe)).astype(BF)
    grad_tokens, grad_qkv, grad_out, grad_small = back(
        moe_grad, gate_grad, cot, x, middle, sent, flags, prob, attended, packed, normed_a, small, proj_qkv, proj_out
    )
    grad_tokens = unpad(grad_tokens)

    grad_small = jnp.pad(grad_small.T, ((0, 0), (0, 128 - TALL)))
    shares = jnp.concatenate((grad_qkv, grad_out, grad_small, jnp.zeros_like(grad_small)), 1)
    shares = comm.scatter_core(shares, 1)
    shares = comm.scatter_shard(shares, 0)
    shares = comm.scatter_heads(shares, 1)
    cut = shares.shape[0] // 4
    rolled = [
        lax.dynamic_slice_in_dim(shares, ((comm.tensor + 4 - k) % 4) * cut, cut, 0) for k in range(4)
    ]
    summed = comm.line_scatter(rolled).astype(BF)
    pieces = comm.line_gather(summed)
    whole = jnp.zeros(shares.shape, BF)
    for k in range(4):
        whole = lax.dynamic_update_slice_in_dim(whole, pieces[k], ((comm.tensor + 4 - k) % 4) * cut, 0)
    whole = comm.join(whole, comm.over_heads(whole), comm.head // 2, 1)
    whole = comm.join(whole, comm.over_core(whole), comm.pair, 1).astype(F32)
    small = whole[:, 4 * width : 4 * width + 128]

    grad_in, grad_outer = jnp.stack(inner_grads, 0), jnp.stack(outer_grads, 0)
    grad_in = comm.join(grad_in, comm.over_core(grad_in), comm.pair, 0).astype(F32)
    grad_outer = comm.join(grad_outer, comm.over_core(grad_outer), comm.pair, 0).astype(F32)
    return (
        mixed,
        grad_tokens,
        small[:, experts],
        small[:, experts + 1],
        whole[:, : 3 * width],
        whole[:, 3 * width : 4 * width],
        small[:, experts + 2],
        small[:, experts + 3],
        small[:, :experts],
        grad_in,
        grad_outer,
    )


def solution(mesh):
    split = P(AXES, None)
    vector, matrix = P("shard"), P("shard", None)
    inner, outer = P(None, "shard", "tensor"), P(None, "tensor", "shard")
    return jax.shard_map(
        local,
        mesh=mesh,
        in_specs=(
            split, vector, vector, matrix, matrix, vector, vector, matrix, inner, outer, split, split, split,
        ),
        out_specs=(
            split, split, vector, vector, matrix, matrix, vector, vector, matrix, inner, outer,
        ),
        check_vma=False,
    )
```

time: 766 us -> 631 us (0.82)
  waiting for transfers between devices: 349 us -> 135 us
  Pallas kernels: 113 us -> 208 us
  other arithmetic: 74.8 us -> 60.8 us
    ppermute x76 -> x64, waiting for transfers between devices: 349 us -> 135 us  [move(): return lax.ppermute(value, AXES, pairs)]
    pallas_call x1, Pallas kernels: 11 us -> 95.8 us  [head(): pl.pallas_call(head_kernel, out_shape=(shape((2, TALL, depth), BF), shape...]
    dynamic_slice x9 -> x12, local copies, waits for them, and re-layouts: 0.64 us -> 14.2 us  [halves(): other = lax.dynamic_slice_in_dim(value, (1 - index) * size, size, axis)]
    pallas_call x1, Pallas kernels: 75 us -> 86.2 us  [expert_pass(): pl.pallas_call(expert_kernel, out_shape=(shape((blocks, length, width), B...]
    ppermute x76 -> x64, starting transfers between devices: 141 us -> 145 us  [move(): return lax.ppermute(value, AXES, pairs)]
    unnamed x112 -> x141, local copies, waits for them, and re-layouts: 17.1 us -> 13.8 us
  transfers between devices with their start and end apart: 76 -> 64, of which waited for: 37 -> 27; matrix products, arithmetic and copies ran while one was open for 16% -> 17% of each run, Pallas kernels for 5% -> 4%
where the time goes in v3:
time: 631 us; the launch traced here: 623 us
  Pallas kernels  208 us (33%)
  starting transfers between devices  145 us (23%)
  waiting for transfers between devices  135 us (21%)
  local copies, waits for them, and re-layouts  71.8 us (11%)
  other arithmetic  60.8 us (10%)
    ppermute x64, starting transfers between devices, move(): return lax.ppermute(value, AXES, pairs)  145 us
    ppermute x64, waiting for transfers between devices, move(): return lax.ppermute(value, AXES, pairs)  135 us
    pallas_call x1, Pallas kernels, head(): pl.pallas_call(head_kernel, out_shape=(shape((2, TALL, depth), BF), shape...  95.8 us
    pallas_call x1, Pallas kernels, expert_pass(): pl.pallas_call(expert_kernel, out_shape=(shape((blocks, length, width), B...  86.2 us
    pallas_call x1, Pallas kernels, back(): pl.pallas_call(back_kernel, out_shape=(shape((rows, width), BF), shape((w...  26.4 us
    dynamic_update_slice x4, local copies, waits for them, and re-layouts, local(): lax.dynamic_update_slice_in_dim(whole, pieces[k], (comm.tensor + 4 - k) %...  14.2 us
    dynamic_slice x12, local copies, waits for them, and re-layouts, halves(): other = lax.dynamic_slice_in_dim(value, (1 - index) * size, size, axis)  14.2 us
    unnamed x141, local copies, waits for them, and re-layouts  13.8 us
  transfers between devices with their start and end apart: 64, of which 27 were waited for; matrix products, arithmetic and copies ran while one was open for 17% of the time, Pallas kernels for 4%

profile of v3, /device:TPU:17, one launch (start us, length us, event | category | flops | bytes accessed | tf_op | source)
XLA Modules:
  0.0 622.6 jit_solution(10615662507090975585)
XLA Ops:
  6.8 95.8 %head.1 = (bf16[2,16,384]{2,1,0:T(8,128)(2,1)}, bf16[768,2304]{1,0:T(8,128)(2,1)}, bf16[768,768]{1,0:T(8,128)(2,1)}, bf16[416,768]{1,0:T(8,128)(2,1)}, bf16[416,...) custom-call(bf16[416,768]{1,0:T(8,128)(2,1)} %bitcast.144, ...), custom_call_target="tpu_custom_call" | custom-call | flops 8000000000 | bytes 30000000 | tf_op jit(solution)/shard_map/head/pallas_call | solution.py:394
  102.6 86.2 %experts.1 = (bf16[8,416,768]{2,1,0:T(8,128)(2,1)}, bf16[8,416,768]{2,1,0:T(8,128)(2,1)}, bf16[8,16,416]{2,1,0:T(8,128)(2,1)}, bf16[4,768,768]{2,1,0:T(8,128)(2,1)}, bf16[4,768,768]{2,1,0:T(8,128)(2,1)}) custom-call(s32[2]{0:T(128)} %pad_add_fusion.place_ref, bf16[8,416,768]{2,1,0:T(8,128)(2,1)} %get-tuple-element.34.rows_ref, ...), custom_call_target="tpu_custom_call" | custom-call | flops 49999998976 | bytes 50000000 | tf_op jit(solution)/shard_map/experts/pallas_call | solution.py:563
  197.9 5.7 fusion.20
  214.5 16.2 %collective-permute-start.15 = (bf16[16,416]{1,0:T(8,128)(2,1)}, bf16[16,416]{1,0:T(8,128)(2,1)}, u32[]{:S(2)}, u32[]{:S(2)}) collective-permute-start(bf16[16,416]{1,0:T(8,128)(2,1)} %get-tuple-element.149), channel_id=1, source_target_pairs={{0,1},{1,2},{2,3},{4,5},{5,6},{6,7},{8,9},{9,10},{10,11},{12,13},{... | collective-permute-start | bytes 39944 | tf_op jit(solution)/shard_map/ppermute | solution.py:712
  266.2 8.6 %collective-permute-done.41 = bf16[384,768]{1,0:T(8,128)(2,1)S(1)} collective-permute-done((bf16[384,768]{1,0:T(8,128)(2,1)}, bf16[384,768]{1,0:T(8,128)(2,1)S(1)}, u32[]{:S(2)}, u32[]{:S(2)}) %collective-permute-start.41) | collective-permute-done | bytes 589856 | tf_op jit(solution)/shard_map/ppermute | solution.py:712
  276.2 11.3 %collective-permute-done.38 = bf16[384,768]{1,0:T(8,128)(2,1)S(1)} collective-permute-done((bf16[384,768]{1,0:T(8,128)(2,1)}, bf16[384,768]{1,0:T(8,128)(2,1)S(1)}, u32[]{:S(2)}, u32[]{:S(2)}) %collective-permute-start.38) | collective-permute-done | bytes 589856 | tf_op jit(solution)/shard_map/ppermute | solution.py:712
  292.0 8.1 %collective-permute-done.60 = bf16[768,384]{1,0:T(8,128)(2,1)S(1)} collective-permute-done((bf16[768,384]{1,0:T(8,128)(2,1)S(1)}, bf16[768,384]{1,0:T(8,128)(2,1)S(1)}, u32[]{:S(2)}, u32[]{:S(2)}) %collective-permute-start.60) | collective-permute-done | bytes 589856 | tf_op jit(solution)/shard_map/ppermute | solution.py:712
  304.1 8.6 %collective-permute-done.57 = bf16[768,384]{1,0:T(8,128)(2,1)S(1)} collective-permute-done((bf16[768,384]{1,0:T(8,128)(2,1)S(1)}, bf16[768,384]{1,0:T(8,128)(2,1)S(1)}, u32[]{:S(2)}, u32[]{:S(2)}) %collective-permute-start.57) | collective-permute-done | bytes 589856 | tf_op jit(solution)/shard_map/ppermute | solution.py:712
  320.9 4.5 collective-permute-done.54
  326.8 11.4 %collective-permute-done.51 = bf16[768,384]{1,0:T(8,128)(2,1)S(1)} collective-permute-done((bf16[768,384]{1,0:T(8,128)(2,1)S(1)}, bf16[768,384]{1,0:T(8,128)(2,1)S(1)}, u32[]{:S(2)}, u32[]{:S(2)}) %collective-permute-start.51) | collective-permute-done | bytes 589856 | tf_op jit(solution)/shard_map/ppermute | solution.py:712
  358.8 26.4 %back.1 = (bf16[416,768]{1,0:T(8,128)(2,1)}, bf16[768,2304]{1,0:T(8,128)(2,1)}, bf16[768,768]{1,0:T(8,128)(2,1)}, bf16[16,768]{1,0:T(8,128)(2,1)}) custom-call(f32[416,768]{1,0:T(8,128)} %fusion.8.moe_ref, f32[16,416]{1,0:T(8,128)} %fusion.19.gate_ref, bf16[416,768]{1,0:T(8,128)(2,1)} %bitcast.147, bf16[416,768]{1,0:T(8,128)(2,1)} %bitcast.145, ...), custom_call_target="tpu_custom_call" | custom-call | flops 16000000000 | bytes 20000000 | tf_op jit(solution)/shard_map/back/pallas_call | solution.py:679
  389.8 5.0 collective-permute-start.21
  403.8 6.0 collective-permute-done.55
  410.1 6.0 collective-permute-done.52
  416.4 6.0 collective-permute-done.49
  422.8 6.0 collective-permute-done.46
  429.1 6.0 collective-permute-done.43
  448.0 6.0 collective-permute-done.59
  457.5 4.6 collective-permute-done.22
  470.5 6.5 %collective-permute-done.23 = bf16[384,832]{0,1:T(8,128)(2,1)S(1)} collective-permute-done((bf16[384,832]{0,1:T(8,128)(2,1)}, bf16[384,832]{0,1:T(8,128)(2,1)S(1)}, u32[]{:S(2)}, u32[]{:S(2)}) %collective-permute-start.23) | collective-permute-done | bytes 639008 | tf_op jit(solution)/shard_map/ppermute | solution.py:712
  499.4 8.6 %collective-permute-start.63 = (bf16[4,768,384]{2,1,0:T(8,128)(2,1)}, bf16[4,768,384]{2,1,0:T(8,128)(2,1)}, u32[]{:S(2)}, u32[]{:S(2)}) collective-permute-start(bf16[4,768,384]{2,1,0:T(8,128)(2,1)} %pad_maximum_fusion.1), channel_id=1, source_target_pairs={{0,4},{1,5},{2,6},{3,7},{4,0},{5,1},{6,2},{7,3},{8,12},{9,13},{10,... | collective-permute-start | bytes 7077896 | tf_op jit(solution)/shard_map/ppermute | solution.py:712
  521.5 8.3 %collective-permute-done.29 = bf16[96,832]{1,0:T(8,128)(2,1)S(1)} collective-permute-done((bf16[96,832]{1,0:T(8,128)(2,1)S(1)}, bf16[96,832]{1,0:T(8,128)(2,1)S(1)}, u32[]{:S(2)}, u32[]{:S(2)}) %collective-permute-start.29) | collective-permute-done | bytes 159776 | tf_op jit(solution)/shard_map/ppermute | solution.py:712
  591.7 4.8 collective-permute-start.37
  615.7 5.2 copy.54
  (386 shorter events, 258.2 us)
Async XLA Ops:
  192.3 295.2 %collective-permute-start = (bf16[4,416,768]{2,1,0:T(8,128)(2,1)}, bf16[4,416,768]{2,1,0:T(8,128)(2,1)}, u32[]{:S(2)}, u32[]{:S(2)}) collective-permute-start(bf16[4,416,768]{2,1,0:T(8,128)(2,1)} %constant_dynamic-slice_fusion.3), channel_id=1, source_target_pairs={{0,4},{1,5},{2,6},{3,7},{4,0},{5,1},{6,2},{7,3},{8,12},{9,13},{10,... | collective-permute-start | bytes 7667720 | tf_op jit(solution)/shard_map/ppermute | solution.py:712
  196.8 58.6 %collective-permute-start.7 = (bf16[4,416,768]{2,1,0:T(8,128)(2,1)}, bf16[4,416,768]{2,1,0:T(8,128)(2,1)}, u32[]{:S(2)}, u32[]{:S(2)}) collective-permute-start(bf16[4,416,768]{2,1,0:T(8,128)(2,1)} %constant_dynamic-slice_fusion.2), channel_id=1, source_target_pairs={{0,4},{1,5},{2,6},{3,7},{4,0},{5,1},{6,2},{7,3},{8,12},{9,13},{10,... | collective-permute-start | bytes 7667720 | tf_op jit(solution)/shard_map/ppermute | solution.py:712
  205.5 48.3 %collective-permute-start.47 = (bf16[384,768]{1,0:T(8,128)(2,1)}, bf16[384,768]{1,0:T(8,128)(2,1)}, u32[]{:S(2)}, u32[]{:S(2)}) collective-permute-start(bf16[384,768]{1,0:T(8,128)(2,1)} %dynamic-slice_bitcast_fusion.5), channel_id=1, source_target_pairs={{0,16},{1,17},{2,18},{3,19},{4,20},{5,21},{6,22},{7,23},{8,24},{9,... | collective-permute-start | bytes 1769480 | tf_op jit(solution)/shard_map/ppermute | solution.py:712
  253.8 33.7 %collective-permute-start.38 = (bf16[384,768]{1,0:T(8,128)(2,1)}, bf16[384,768]{1,0:T(8,128)(2,1)S(1)}, u32[]{:S(2)}, u32[]{:S(2)}) collective-permute-start(bf16[384,768]{1,0:T(8,128)(2,1)} %dynamic-slice_bitcast_fusion.8), channel_id=1, source_target_pairs={{0,16},{1,17},{2,18},{3,19},{4,20},{5,21},{6,22},{7,23},{8,24},{9,... | collective-permute-start | bytes 1769480 | tf_op jit(solution)/shard_map/ppermute | solution.py:712
  255.4 44.7 %collective-permute-start.60 = (bf16[768,384]{1,0:T(8,128)(2,1)S(1)}, bf16[768,384]{1,0:T(8,128)(2,1)S(1)}, u32[]{:S(2)}, u32[]{:S(2)}) collective-permute-start(bf16[768,384]{1,0:T(8,128)(2,1)S(1)} %copy-done.48), channel_id=1, source_target_pairs={{0,16},{1,17},{2,18},{3,19},{4,20},{5,21},{6,22},{7,23},{8,24},{9,... | collective-permute-start | bytes 1769480 | tf_op jit(solution)/shard_map/ppermute | solution.py:712
  262.2 26.7 %collective-permute-start.8 = (bf16[416,768]{1,0:T(8,128)(2,1)S(1)}, bf16[416,768]{1,0:T(8,128)(2,1)S(1)}, u32[]{:S(2)}, u32[]{:S(2)}) collective-permute-start(bf16[416,768]{1,0:T(8,128)(2,1)S(1)} %get-tuple-element.105), channel_id=1, source_target_pairs={{0,1},{1,2},{2,3},{4,5},{5,6},{6,7},{8,9},{9,10},{10,11},{12,13},{... | collective-permute-start | bytes 1916936 | tf_op jit(solution)/shard_map/ppermute | solution.py:712
  274.8 37.9 %collective-permute-start.57 = (bf16[768,384]{1,0:T(8,128)(2,1)S(1)}, bf16[768,384]{1,0:T(8,128)(2,1)S(1)}, u32[]{:S(2)}, u32[]{:S(2)}) collective-permute-start(bf16[768,384]{1,0:T(8,128)(2,1)S(1)} %copy-done.49), channel_id=1, source_target_pairs={{0,16},{1,17},{2,18},{3,19},{4,20},{5,21},{6,22},{7,23},{8,24},{9,... | collective-permute-start | bytes 1769480 | tf_op jit(solution)/shard_map/ppermute | solution.py:712
  287.5 37.9 %collective-permute-start.54 = (bf16[768,384]{1,0:T(8,128)(2,1)S(1)}, bf16[768,384]{1,0:T(8,128)(2,1)S(1)}, u32[]{:S(2)}, u32[]{:S(2)}) collective-permute-start(bf16[768,384]{1,0:T(8,128)(2,1)S(1)} %copy-done.50), channel_id=1, source_target_pairs={{0,16},{1,17},{2,18},{3,19},{4,20},{5,21},{6,22},{7,23},{8,24},{9,... | collective-permute-start | bytes 1769480 | tf_op jit(solution)/shard_map/ppermute | solution.py:712
  288.9 26.8 %collective-permute-start.11 = (bf16[416,768]{1,0:T(8,128)(2,1)S(1)}, bf16[416,768]{1,0:T(8,128)(2,1)S(1)}, u32[]{:S(2)}, u32[]{:S(2)}) collective-permute-start(bf16[416,768]{1,0:T(8,128)(2,1)S(1)} %get-tuple-element.106), channel_id=1, source_target_pairs={{1,0},{2,1},{3,2},{5,4},{6,5},{7,6},{9,8},{10,9},{11,10},{13,12},{... | collective-permute-start | bytes 1916936 | tf_op jit(solution)/shard_map/ppermute | solution.py:712
  312.8 25.4 %collective-permute-start.51 = (bf16[768,384]{1,0:T(8,128)(2,1)S(1)}, bf16[768,384]{1,0:T(8,128)(2,1)S(1)}, u32[]{:S(2)}, u32[]{:S(2)}) collective-permute-start(bf16[768,384]{1,0:T(8,128)(2,1)S(1)} %copy-done.51), channel_id=1, source_target_pairs={{0,16},{1,17},{2,18},{3,19},{4,20},{5,21},{6,22},{7,23},{8,24},{9,... | collective-permute-start | bytes 1769480 | tf_op jit(solution)/shard_map/ppermute | solution.py:712
  315.7 32.0 %collective-permute-start.48 = (bf16[384,384]{1,0:T(8,128)(2,1)S(1)}, bf16[384,384]{1,0:T(8,128)(2,1)S(1)}, u32[]{:S(2)}, u32[]{:S(2)}) collective-permute-start(bf16[384,384]{1,0:T(8,128)(2,1)S(1)} %dynamic-slice_convert_fusion.6), channel_id=1, source_target_pairs={{0,8},{1,9},{2,10},{3,11},{4,12},{5,13},{6,14},{7,15},{8,0},{9,1},... | collective-permute-start | bytes 884744 | tf_op jit(solution)/shard_map/ppermute | solution.py:712
  317.3 24.8 %collective-permute-start.12 = (bf16[416,768]{1,0:T(8,128)(2,1)S(1)}, bf16[416,768]{1,0:T(8,128)(2,1)S(1)}, u32[]{:S(2)}, u32[]{:S(2)}) collective-permute-start(bf16[416,768]{1,0:T(8,128)(2,1)S(1)} %get-tuple-element.104), channel_id=1, source_target_pairs={{1,0},{2,1},{3,2},{5,4},{6,5},{7,6},{9,8},{10,9},{11,10},{13,12},{... | collective-permute-start | bytes 1916936 | tf_op jit(solution)/shard_map/ppermute | solution.py:712
  325.4 64.4 %collective-permute-start.45 = (bf16[384,384]{1,0:T(8,128)(2,1)}, bf16[384,384]{1,0:T(8,128)(2,1)}, u32[]{:S(2)}, u32[]{:S(2)}) collective-permute-start(bf16[384,384]{1,0:T(8,128)(2,1)} %dynamic-slice_convert_fusion.7), channel_id=1, source_target_pairs={{0,8},{1,9},{2,10},{3,11},{4,12},{5,13},{6,14},{7,15},{8,0},{9,1},... | collective-permute-start | bytes 884744 | tf_op jit(solution)/shard_map/ppermute | solution.py:712
  347.7 48.2 %collective-permute-start.42 = (bf16[384,384]{1,0:T(8,128)(2,1)}, bf16[384,384]{1,0:T(8,128)(2,1)}, u32[]{:S(2)}, u32[]{:S(2)}) collective-permute-start(bf16[384,384]{1,0:T(8,128)(2,1)} %dynamic-slice_convert_fusion.8), channel_id=1, source_target_pairs={{0,8},{1,9},{2,10},{3,11},{4,12},{5,13},{6,14},{7,15},{8,0},{9,1},... | collective-permute-start | bytes 884744 | tf_op jit(solution)/shard_map/ppermute | solution.py:712
  352.5 44.8 %collective-permute-start.39 = (bf16[384,384]{1,0:T(8,128)(2,1)}, bf16[384,384]{1,0:T(8,128)(2,1)}, u32[]{:S(2)}, u32[]{:S(2)}) collective-permute-start(bf16[384,384]{1,0:T(8,128)(2,1)} %dynamic-slice_convert_fusion.9), channel_id=1, source_target_pairs={{0,8},{1,9},{2,10},{3,11},{4,12},{5,13},{6,14},{7,15},{8,0},{9,1},... | collective-permute-start | bytes 884744 | tf_op jit(solution)/shard_map/ppermute | solution.py:712
  356.3 43.3 %collective-permute-start.61 = (bf16[384,384]{1,0:T(8,128)(2,1)}, bf16[384,384]{1,0:T(8,128)(2,1)}, u32[]{:S(2)}, u32[]{:S(2)}) collective-permute-start(bf16[384,384]{1,0:T(8,128)(2,1)} %dynamic-slice_convert_fusion.2), channel_id=1, source_target_pairs={{0,8},{1,9},{2,10},{3,11},{4,12},{5,13},{6,14},{7,15},{8,0},{9,1},... | collective-permute-start | bytes 884744 | tf_op jit(solution)/shard_map/ppermute | solution.py:712
  389.8 45.5 %collective-permute-start.21 = (bf16[768,1664]{1,0:T(8,128)(2,1)S(1)}, bf16[768,1664]{1,0:T(8,128)(2,1)S(1)}, u32[]{:S(2)}, u32[]{:S(2)}) collective-permute-start(bf16[768,1664]{1,0:T(8,128)(2,1)S(1)} %constant_dynamic-slice_fusion), channel_id=1, source_target_pairs={{0,4},{1,5},{2,6},{3,7},{4,0},{5,1},{6,2},{7,3},{8,12},{9,13},{10,... | collective-permute-start | bytes 7667720 | tf_op jit(solution)/shard_map/ppermute | solution.py:712
  436.1 26.1 %collective-permute-start.22 = (bf16[384,1664]{1,0:T(8,128)(2,1)S(1)}, bf16[384,1664]{1,0:T(8,128)(2,1)S(1)}, u32[]{:S(2)}, u32[]{:S(2)}) collective-permute-start(bf16[384,1664]{1,0:T(8,128)(2,1)S(1)} %dynamic-slice_convert_fusion), channel_id=1, source_target_pairs={{0,16},{1,17},{2,18},{3,19},{4,20},{5,21},{6,22},{7,23},{8,24},{9,... | collective-permute-start | bytes 3833864 | tf_op jit(solution)/shard_map/ppermute | solution.py:712
  441.4 25.2 %collective-permute-start.56 = (bf16[384,384]{1,0:T(8,128)(2,1)S(1)}, bf16[384,384]{1,0:T(8,128)(2,1)}, u32[]{:S(2)}, u32[]{:S(2)}) collective-permute-start(bf16[384,384]{1,0:T(8,128)(2,1)S(1)} %add_convert_fusion.2), channel_id=1, source_target_pairs={{0,8},{1,9},{2,10},{3,11},{4,12},{5,13},{6,14},{7,15},{8,0},{9,1},... | collective-permute-start | bytes 884744 | tf_op jit(solution)/shard_map/ppermute | solution.py:712
  454.1 78.0 %collective-permute-start.50 = (bf16[4,384,768]{2,1,0:T(8,128)(2,1)}, bf16[4,384,768]{2,1,0:T(8,128)(2,1)}, u32[]{:S(2)}, u32[]{:S(2)}) collective-permute-start(bf16[4,384,768]{2,1,0:T(8,128)(2,1)} %pad_maximum_fusion), channel_id=1, source_target_pairs={{0,4},{1,5},{2,6},{3,7},{4,0},{5,1},{6,2},{7,3},{8,12},{9,13},{10,... | collective-permute-start | bytes 7077896 | tf_op jit(solution)/shard_map/ppermute | solution.py:712
  499.4 78.5 %collective-permute-start.63 = (bf16[4,768,384]{2,1,0:T(8,128)(2,1)}, bf16[4,768,384]{2,1,0:T(8,128)(2,1)}, u32[]{:S(2)}, u32[]{:S(2)}) collective-permute-start(bf16[4,768,384]{2,1,0:T(8,128)(2,1)} %pad_maximum_fusion.1), channel_id=1, source_target_pairs={{0,4},{1,5},{2,6},{3,7},{4,0},{5,1},{6,2},{7,3},{8,12},{9,13},{10,... | collective-permute-start | bytes 7077896 | tf_op jit(solution)/shard_map/ppermute | solution.py:712
  508.0 36.7 %collective-permute-start.4 = (bf16[416,768]{1,0:T(8,128)(2,1)}, bf16[416,768]{1,0:T(8,128)(2,1)S(1)}, u32[]{:S(2)}, u32[]{:S(2)}) collective-permute-start(bf16[416,768]{1,0:T(8,128)(2,1)} %get-tuple-element.110), channel_id=1, source_target_pairs={{1,0},{2,1},{3,2},{5,4},{6,5},{7,6},{9,8},{10,9},{11,10},{13,12},{... | collective-permute-start | bytes 1916936 | tf_op jit(solution)/shard_map/ppermute | solution.py:712
  519.6 25.1 %collective-permute-start.2 = (bf16[416,768]{1,0:T(8,128)(2,1)S(1)}, bf16[416,768]{1,0:T(8,128)(2,1)S(1)}, u32[]{:S(2)}, u32[]{:S(2)}) collective-permute-start(bf16[416,768]{1,0:T(8,128)(2,1)S(1)} %fusion.10), channel_id=1, source_target_pairs={{0,1},{1,2},{2,3},{4,5},{5,6},{6,7},{8,9},{9,10},{10,11},{12,13},{... | collective-permute-start | bytes 1916936 | tf_op jit(solution)/shard_map/ppermute | solution.py:712
  546.1 37.2 %collective-permute-start.5 = (bf16[416,768]{1,0:T(8,128)(2,1)}, bf16[416,768]{1,0:T(8,128)(2,1)}, u32[]{:S(2)}, u32[]{:S(2)}) collective-permute-start(bf16[416,768]{1,0:T(8,128)(2,1)} %get-tuple-element.108), channel_id=1, source_target_pairs={{1,0},{2,1},{3,2},{5,4},{6,5},{7,6},{9,8},{10,9},{11,10},{13,12},{... | collective-permute-start | bytes 1916936 | tf_op jit(solution)/shard_map/ppermute | solution.py:712
  (110 other events, 1294.6 us)

commit v4 on v3

--- a/solution.py
+++ b/solution.py
@@ -169,11 +169,14 @@
         self.above = (shard, head, lax.rem(tensor + 1, 4))
         self.below = (shard, head, lax.rem(tensor + 3, 4))
 
-    def greet(self):
+    def greet(self, line=False):
         barrier = pltpu.get_barrier_semaphore()
-        for device in (self.across, self.beside, self.twin, self.above, self.below):
+        devices = [self.across, self.beside, self.twin, self.above, self.below]
+        if line:
+            devices.append((self.shard, self.head, lax.rem(self.tensor + 2, 4)))
+        for device in devices:
             pl.semaphore_signal(barrier, inc=1, device_id=device, device_id_type=MESH)
-        pl.semaphore_wait(barrier, 5)
+        pl.semaphore_wait(barrier, len(devices))
 
 
 class Links:
@@ -194,6 +197,9 @@
         copy.start()
         self.sent.append((None, copy))
         return copy
+
+    def skip(self, done):
+        self.sent = [(when, copy) for when, copy in self.sent if copy is not done]
 
     def finish(self):
         for when, copy in self.sent:
@@ -596,35 +602,6 @@
     )(place, rows, flags, cot, own_in, got_in, own_out, got_out)
 
 
-def back_attention(at, grad_proj, packed_ref, out_ref, stacked):
-    width = grad_proj.shape[1]
-    group = 3 * HEAD_DIM
-    scale = HEAD_DIM ** (-0.5)
-    lanes = lax.broadcasted_iota(jnp.int32, (PAD, group), 1) // HEAD_DIM
-    for double in range(width // group // 2):
-        made = []
-        packed = packed_ref[at, pl.ds(double * 6 * group, 6 * group)]
-        for side in range(2):
-            query, keys, values = (
-                packed[:, (3 * side + k) * group : (3 * side + k + 1) * group] for k in range(3)
-            )
-            index = double * 2 + side
-            grad_att = contract_cols(grad_proj, out_ref[pl.ds(index * group, group), :]).astype(BF)
-            outs = [jnp.zeros((PAD, group), F32) for _ in range(3)]
-            for head in range(3):
-                mask = lanes == head
-                probs = head_probs(jnp.where(mask, query, jnp.zeros_like(query)), keys, scale)
-                part = jnp.where(mask, grad_att, jnp.zeros_like(grad_att))
-                grad_weights = contract_cols(part, values)
-                inner_sum = jnp.sum(probs * grad_weights, -1, keepdims=True)
-                grad_scores = (probs * (grad_weights - inner_sum)).astype(BF)
-                outs[0] = jnp.where(mask, dot(grad_scores, keys), outs[0])
-                outs[1] = jnp.where(mask, contract_rows(grad_scores, query), outs[1])
-                outs[2] = jnp.where(mask, contract_rows(probs.astype(BF), grad_att), outs[2])
-            made += [outs[0] * scale, outs[1] * scale, outs[2]]
-        stacked[at, pl.ds(double * 6 * group, 6 * group)] = jnp.concatenate(made, 1).astype(BF)
-
-
 def back_middle(at, moe, gates, cot, middle, rows, probs, flags, small_ref, sums):
     experts = TALL // 2
     row = lax.broadcasted_iota(jnp.int32, flags.shape, 0)
@@ -640,6 +617,32 @@
     sums[2] = sums[2] + jnp.sum(grad * unit, 0, keepdims=True)
     sums[3] = sums[3] + jnp.sum(grad, 0, keepdims=True)
     return cot + norm_back(grad, unit, inverse, gain_row(small_ref, experts, 2))
+
+
+def back_heads(at, double, grad_proj, packed_ref, out_ref, stacked):
+    width = grad_proj.shape[1]
+    group = 3 * HEAD_DIM
+    scale = HEAD_DIM ** (-0.5)
+    lanes = lax.broadcasted_iota(jnp.int32, (PAD, group), 1) // HEAD_DIM
+    made = []
+    packed = packed_ref[at, pl.ds(double * 6 * group, 6 * group)]
+    for side in range(2):
+        query, keys, values = (packed[:, (3 * side + k) * group : (3 * side + k + 1) * group] for k in range(3))
+        index = double * 2 + side
+        grad_att = contract_cols(grad_proj, out_ref[pl.ds(index * group, group), :]).astype(BF)
+        outs = [jnp.zeros((PAD, group), F32) for _ in range(3)]
+        for head in range(3):
+            mask = lanes == head
+            probs = head_probs(jnp.where(mask, query, jnp.zeros_like(query)), keys, scale)
+            part = jnp.where(mask, grad_att, jnp.zeros_like(grad_att))
+            grad_weights = contract_cols(part, values)
+            inner_sum = jnp.sum(probs * grad_weights, -1, keepdims=True)
+            grad_scores = (probs * (grad_weights - inner_sum)).astype(BF)
+            outs[0] = jnp.where(mask, dot(grad_scores, keys), outs[0])
+            outs[1] = jnp.where(mask, contract_rows(grad_scores, query), outs[1])
+            outs[2] = jnp.where(mask, contract_rows(probs.astype(BF), grad_att), outs[2])
+        made += [outs[0] * scale, outs[1] * scale, outs[2]]
+    stacked[at, pl.ds(double * 6 * group, 6 * group)] = jnp.concatenate(made, 1).astype(BF)
 
 
 def back_kernel(
@@ -660,7 +663,8 @@
         )
         grad_proj = grad_middle.astype(BF)
         projected[at, :] = grad_proj
-        back_attention(at, grad_proj, packed_ref, out_ref, stacked)
+        for double in range(width // (6 * HEAD_DIM)):
+            back_heads(at, double, grad_proj, packed_ref, out_ref, stacked)
         grad = contract_cols(stacked[at, :], qkv_ref[...])
         unit, inverse = norm_parts(x_ref[at, :].astype(F32))
         sums[0] = sums[0] + jnp.sum(grad * unit, 0, keepdims=True)
@@ -691,6 +695,428 @@
     )(moe, gates, cot, x, middle, sent, flags, prob, attended, packed, normed, small, qkv, out)
 
 
+class LineScatter:
+    def __init__(self, links, place, sums, up, down):
+        self.links, self.place = links, place
+        self.sums, self.up, self.down = sums, up, down
+        self.copies = {}
+
+    def ways(self, step):
+        t = self.place.tensor
+        return (
+            ("up", self.up, t + 3 - step, t <= step, t >= 1, self.place.above),
+            ("down", self.down, t - 3 + step, t >= 3 - step, t <= 2, self.place.below),
+        )
+
+    def send(self, part, step):
+        for name, got, slot, sends, comes, device in self.ways(step):
+            slot = jnp.clip(slot, 0, 3)
+            if step > 0:
+                before = self.copies[name, part, step - 1]
+
+                @pl.when(sends & comes)
+                def _():
+                    before.wait_recv()
+                    ref = self.sums(slot, part)
+                    ref[...] = (ref[...].astype(F32) + got(step - 1, part)[...].astype(F32)).astype(BF)
+
+            copy = self.links.copy(self.sums(slot, part), got(step, part), device)
+            pl.when(sends)(copy.start)
+            self.links.sent.append((sends, copy))
+            self.copies[name, part, step] = copy
+
+    def finish(self, part, total):
+        total[...] = self.sums(self.place.tensor, part)[...].astype(F32)
+        for name, got, slot, sends, comes, device in self.ways(2):
+            copy = self.copies[name, part, 2]
+
+            @pl.when(comes)
+            def _():
+                copy.wait_recv()
+                total[...] += got(2, part)[...].astype(F32)
+
+
+def tail_kernel(
+    back_all, gate_all, total_all, grads_in, grads_out, rows_all, flags_all,
+    cot_ref, x_ref, middle_ref, prob_ref, attended_ref, packed_ref, normed_ref, small_ref, qkv_ref, out_ref,
+    mixed_ref, tokens_ref, dense_ref, grad_small, final_in, final_out, beside_in, beside_out,
+    back_sum, back_got, back_up, back_down, gate_sum, gate_got, gate_up, gate_down,
+    total_sum, total_got, total_up, total_down, moe, gates, rows_ref, flag_ref, projected, stacked,
+    chunks, core_got, across_sent, across_got, beside_sum, beside_sent, beside_got, line_sum, line_got, line_final,
+    own_in, own_out, across_in, across_out, read_in, read_out,
+    small_sent, small_core, small_half, small_across, small_side, small_beside, small_line_sent, small_line,
+    send, recv, local_sem,
+):
+    place = Place()
+    links = Links(send, recv)
+    rows, width = x_ref.shape
+    experts = TALL // 2
+    count = grads_in.shape[0]
+    depth = width // 2
+    shard, pair, side, tensor = place.shard, place.pair, place.side, place.tensor
+    mine = pair * 4 + tensor
+    place.greet(True)
+    ours, theirs = pl.ds(pair * 4, 4), pl.ds((1 - pair) * 4, 4)
+
+    locals_ = [
+        pltpu.make_async_copy(back_all.at[ours], back_sum, local_sem.at[0]),
+        pltpu.make_async_copy(gate_all.at[ours], gate_sum, local_sem.at[1]),
+        pltpu.make_async_copy(total_all.at[ours], total_sum, local_sem.at[2]),
+        pltpu.make_async_copy(rows_all.at[mine], rows_ref, local_sem.at[3]),
+        pltpu.make_async_copy(flags_all.at[mine], flag_ref, local_sem.at[4]),
+    ]
+    for copy in locals_:
+        copy.start()
+    from_twin = [
+        links.start(back_all.at[theirs], back_got, place.twin),
+        links.start(gate_all.at[theirs], gate_got, place.twin),
+        links.start(total_all.at[theirs], total_got, place.twin),
+    ]
+
+    here = pl.ds(pl.multiple_of(shard * depth, LANES), depth)
+    there = pl.ds(pl.multiple_of((1 - shard) * depth, LANES), depth)
+    items = []
+    for expert in range(count):
+        items.append((grads_in.at[expert, there, :], grads_in.at[expert, here, :], across_in.at[expert],
+                      beside_in.at[expert], final_in.at[pair * count + expert], own_in, read_in))
+        items.append((grads_out.at[expert, :, there], grads_out.at[expert, :, here], across_out.at[expert],
+                      beside_out.at[expert], final_out.at[pair * count + expert], own_out, read_out))
+    item_loads = [pltpu.make_async_copy(item[1], item[5], local_sem.at[8 + m]) for m, item in enumerate(items)]
+    item_across, item_beside, item_twin, item_keep = [], [], [], []
+    todo = {"across": 0, "x": 0, "y": 0}
+
+    def send_across():
+        m = todo["across"]
+        if m < len(items):
+            item_across.append(links.start(items[m][0], items[m][2], place.across))
+            todo["across"] += 1
+
+    def take_across():
+        m = todo["x"]
+        if m >= len(items):
+            return
+        todo["x"] += 1
+        item_across[m].wait_recv()
+        send_across()
+        item_loads[m].wait()
+        total, own = items[m][2], items[m][5]
+        total[...] = (total[...].astype(F32) + own[...].astype(F32)).astype(BF)
+        item_beside.append(links.start(total, items[m][3], place.beside))
+        if m + 2 < len(items):
+            item_loads[m + 2].start()
+
+    def take_beside():
+        m = todo["y"]
+        if m >= len(items):
+            return
+        todo["y"] += 1
+        item_beside[m].wait_recv()
+        total, got = items[m][2], items[m][6]
+        load = pltpu.make_async_copy(items[m][3], got, local_sem.at[5])
+        load.start()
+        item_beside[m].wait_send()
+        load.wait()
+        total[...] = (total[...].astype(F32) + got[...].astype(F32)).astype(BF)
+        item_twin.append(links.start(total, items[m][4], place.twin))
+        keep = pltpu.make_async_copy(total, items[m][4], local_sem.at[16 + m])
+        keep.start()
+        item_keep.append(keep)
+
+    send_across()
+    send_across()
+    item_loads[0].start()
+    item_loads[1].start()
+
+    share = depth // 2
+    piece = share // 4
+    half = width // 2
+    stage = {}
+
+    def dense_core(k):
+        stage["core", k] = []
+        for owner in range(2):
+            source = chunks.at[k, pl.ds(pl.multiple_of(owner * depth + (1 - pair) * share, TALL), share), :]
+            stage["core", k].append(links.start(source, core_got.at[k, owner], place.twin))
+
+    def core_sum(k, owner):
+        at = pl.ds(pl.multiple_of(owner * depth + pair * share, TALL), share)
+        return chunks[k, at, :].astype(F32) + core_got[k, owner].astype(F32)
+
+    def dense_across(k):
+        for copy in stage["core", k]:
+            copy.wait_recv()
+        across_sent[k] = core_sum(k, 1 - shard).astype(BF)
+        stage["across", k] = links.start(across_sent.at[k], across_got.at[k], place.across)
+
+    def dense_beside(k):
+        stage["across", k].wait_recv()
+        beside_sum[k] = core_sum(k, shard) + across_got[k].astype(F32)
+        other = pl.ds(pl.multiple_of((1 - side) * half, LANES), half)
+        beside_sent[k] = beside_sum[k, :, other].astype(BF)
+        stage["beside", k] = links.start(beside_sent.at[k], beside_got.at[k], place.beside)
+
+    def around(offset):
+        return (shard, place.head, lax.rem(tensor + offset, 4))
+
+    def dense_line(k):
+        stage["beside", k].wait_recv()
+        own = pl.ds(pl.multiple_of(side * half, LANES), half)
+        line_sum[k] = (beside_sum[k, :, own] + beside_got[k].astype(F32)).astype(BF)
+        stage["line", k] = []
+        for offset in (2, 1, 3):
+            at = pl.ds(pl.multiple_of(lax.rem(tensor + offset, 4) * piece, TALL), piece)
+            stage["line", k].append(links.start(line_sum.at[k, at, :], line_got.at[k, offset - 1], around(offset)))
+
+    def dense_spread(k):
+        for copy in stage["line", k]:
+            copy.wait_recv()
+        at = pl.ds(pl.multiple_of(tensor * piece, TALL), piece)
+        value = line_sum[k, at, :].astype(F32)
+        for offset in range(3):
+            value = value + line_got[k, offset].astype(F32)
+        line_final[k] = value.astype(BF)
+        target = dense_ref.at[
+            pl.ds(pl.multiple_of(pair * share + tensor * piece, TALL), piece),
+            pl.ds(pl.multiple_of(k * width + side * half, LANES), half),
+        ]
+        stage["spread", k] = [links.start(line_final.at[k], target, around(offset)) for offset in (2, 1, 3)]
+        stage["keep", k] = pltpu.make_async_copy(line_final.at[k], target, local_sem.at[24 + k])
+        stage["keep", k].start()
+
+    def dense_return(k):
+        for copy in stage["spread", k]:
+            copy.wait_recv()
+        stage["keep", k].wait()
+        block = dense_ref.at[
+            pl.ds(pl.multiple_of(pair * share, TALL), share),
+            pl.ds(pl.multiple_of(k * width + side * half, LANES), half),
+        ]
+        stage["return", k] = links.start(block, block, place.beside)
+
+    def dense_twin(k):
+        stage["return", k].wait_recv()
+        block = dense_ref.at[pl.ds(pl.multiple_of(pair * share, TALL), share), pl.ds(k * width, width)]
+        stage["twin", k] = links.start(block, block, place.twin)
+
+    def slots(array):
+        def view(slot, part):
+            return array.at[slot, pl.ds(part * PAD, PAD), :]
+
+        return view
+
+    back_line = LineScatter(links, place, slots(back_sum), slots(back_up), slots(back_down))
+    total_line = LineScatter(links, place, slots(total_sum), slots(total_up), slots(total_down))
+    gate_line = LineScatter(
+        links, place, lambda slot, part: gate_sum.at[slot], lambda step, part: gate_up.at[step],
+        lambda step, part: gate_down.at[step],
+    )
+
+    def add_twin(sums, got):
+        for slot in range(4):
+            sums[slot] = (sums[slot].astype(F32) + got[slot].astype(F32)).astype(BF)
+
+    for copy in (locals_[0], locals_[1]):
+        copy.wait()
+    from_twin[1].wait_recv()
+    from_twin[0].wait_recv()
+    add_twin(gate_sum, gate_got)
+    add_twin(back_sum, back_got)
+    gate_line.send(0, 0)
+    for part in range(2):
+        back_line.send(part, 0)
+    locals_[2].wait()
+    from_twin[2].wait_recv()
+    add_twin(total_sum, total_got)
+    gate_line.send(0, 1)
+    for part in range(2):
+        back_line.send(part, 1)
+    take_across()
+    gate_line.send(0, 2)
+    for part in range(2):
+        back_line.send(part, 2)
+    take_across()
+    take_beside()
+    for part in range(2):
+        total_line.send(part, 0)
+    gate_line.finish(0, gates)
+    locals_[3].wait()
+    locals_[4].wait()
+
+    sums = [jnp.zeros((1, width), F32) for _ in range(4)] + [jnp.zeros((TALL, width), F32)]
+    for image in range(2):
+        at = pl.ds(image * PAD, PAD)
+        cols = slice(image * PAD, (image + 1) * PAD)
+        back_line.finish(image, moe.at[at, :])
+        grad = back_middle(
+            at, moe[at, :], gates[:, cols], cot_ref[at, :].astype(F32), middle_ref[at, :], rows_ref[at, :],
+            prob_ref[:, cols], flag_ref[:, cols].astype(F32), small_ref, sums,
+        )
+        moe[at, :] = grad
+        projected[at, :] = grad.astype(BF)
+    chunks[0] = contract_rows(attended_ref[...], projected[...]).astype(BF)
+    dense_core(0)
+    take_across()
+    take_beside()
+    for image in range(2):
+        at = pl.ds(image * PAD, PAD)
+        back_heads(at, 0, projected[at, :], packed_ref, out_ref, stacked)
+    chunks[1] = contract_rows(normed_ref[...], stacked[:, pl.ds(0, width)]).astype(BF)
+    dense_core(1)
+    dense_across(0)
+    for part in range(2):
+        total_line.send(part, 1)
+    take_across()
+    dense_across(1)
+    take_beside()
+    for image in range(2):
+        at = pl.ds(image * PAD, PAD)
+        back_heads(at, 1, projected[at, :], packed_ref, out_ref, stacked)
+    for k in (2, 3):
+        chunks[k] = contract_rows(normed_ref[...], stacked[:, pl.ds((k - 1) * width, width)]).astype(BF)
+        dense_core(k)
+    dense_beside(0)
+    for k in (2, 3):
+        dense_across(k)
+    for part in range(2):
+        total_line.send(part, 2)
+    for image in range(2):
+        at = pl.ds(image * PAD, PAD)
+        grad = contract_cols(stacked[at, :], qkv_ref[...])
+        unit, inverse = norm_parts(x_ref[at, :].astype(F32))
+        sums[0] = sums[0] + jnp.sum(grad * unit, 0, keepdims=True)
+        sums[1] = sums[1] + jnp.sum(grad, 0, keepdims=True)
+        tokens_ref[at, :] = (
+            moe[at, :] + norm_back(grad, unit, inverse, gain_row(small_ref, experts, 0))
+        ).astype(BF)
+    small_sent[...] = jnp.concatenate([sums[4][0:experts]] + sums[:4] + [jnp.zeros((4, width), F32)], 0)
+    small_copies = [links.start(small_sent, small_core, place.twin)]
+    take_across()
+    take_beside()
+    dense_beside(1)
+    dense_line(0)
+    small_copies[0].wait_recv()
+    other = pl.ds(pl.multiple_of((1 - shard) * depth, LANES), depth)
+    small_half[...] = small_sent[:, other] + small_core[:, other]
+    small_copies.append(links.start(small_half, small_across, place.across))
+    take_across()
+    take_beside()
+    dense_line(1)
+    dense_spread(0)
+    dense_beside(2)
+    small_copies[1].wait_recv()
+    own = pl.ds(pl.multiple_of(shard * depth, LANES), depth)
+    small_side[...] = small_sent[:, own] + small_core[:, own] + small_across[...]
+    small_copies.append(links.start(small_side, small_beside, place.beside))
+    dense_beside(3)
+    dense_spread(1)
+    dense_return(0)
+    dense_line(2)
+    take_across()
+    take_beside()
+    small_copies[2].wait_recv()
+    small_line_sent[...] = small_side[...] + small_beside[...]
+    small_line_copies = [links.start(small_line_sent, small_line.at[offset - 1], around(offset)) for offset in (2, 1, 3)]
+    dense_line(3)
+    dense_spread(2)
+    dense_return(1)
+    dense_twin(0)
+    take_across()
+    take_beside()
+    dense_spread(3)
+    dense_return(2)
+    dense_twin(1)
+    take_beside()
+    dense_return(3)
+    dense_twin(2)
+    for copy in small_line_copies:
+        copy.wait_recv()
+    grad_small[...] = small_line_sent[...] + small_line[0] + small_line[1] + small_line[2]
+    for part in range(2):
+        at = pl.ds(part * PAD, PAD)
+        total_line.finish(part, moe.at[at, :])
+        mixed_ref[at, :] = (middle_ref[at, :] + moe[at, :]).astype(BF)
+    for _ in items:
+        take_across()
+        take_beside()
+    dense_twin(3)
+    for copy in item_twin + [stage["twin", k] for k in range(4)]:
+        copy.wait_recv()
+    for copy in item_keep:
+        copy.wait()
+    for copy in item_beside:
+        links.skip(copy)
+    links.finish()
+
+
+def tail(back_all, gate_all, total_all, grads_in, grads_out, rows_all, flags_all, cot, x, middle, prob, attended, packed, normed, small, qkv, out):
+    rows, width = x.shape
+    count, _, hidden = grads_in.shape
+    depth = width // 2
+    shape = jax.ShapeDtypeStruct
+    anywhere = pl.BlockSpec(memory_space=pl.ANY)
+    vmem = pl.BlockSpec(memory_space=pltpu.VMEM)
+    share, piece, half = depth // 2, depth // 8, width // 2
+
+    def scatter_buffers(tall, wide):
+        return [pltpu.VMEM((4, tall, wide), BF)] * 2 + [pltpu.VMEM((3, tall, wide), BF)] * 2
+
+    return pl.pallas_call(
+        tail_kernel,
+        out_shape=(
+            shape((rows, width), BF),
+            shape((rows, width), BF),
+            shape((depth, 4 * width), BF),
+            shape((TALL, depth), F32),
+            shape((2 * count, depth, hidden), BF),
+            shape((2 * count, hidden, depth), BF),
+            shape((count, depth, hidden), BF),
+            shape((count, hidden, depth), BF),
+        ),
+        in_specs=[anywhere] * 7 + [vmem] * 10,
+        out_specs=(vmem,) * 4 + (anywhere,) * 4,
+        scratch_shapes=scatter_buffers(rows, width)
+        + scatter_buffers(TALL, rows)
+        + scatter_buffers(rows, width)
+        + [
+            pltpu.VMEM((rows, width), F32),
+            pltpu.VMEM((TALL, rows), F32),
+            pltpu.VMEM((rows, width), BF),
+            pltpu.VMEM((TALL, rows), BF),
+            pltpu.VMEM((rows, width), BF),
+            pltpu.VMEM((rows, 3 * width), BF),
+            pltpu.VMEM((4, width, width), BF),
+            pltpu.VMEM((4, 2, share, width), BF),
+            pltpu.VMEM((4, share, width), BF),
+            pltpu.VMEM((4, share, width), BF),
+            pltpu.VMEM((4, share, width), F32),
+            pltpu.VMEM((4, share, half), BF),
+            pltpu.VMEM((4, share, half), BF),
+            pltpu.VMEM((4, share, half), BF),
+            pltpu.VMEM((4, 3, piece, half), BF),
+            pltpu.VMEM((4, piece, half), BF),
+        ]
+        + [pltpu.VMEM((depth, hidden), BF), pltpu.VMEM((hidden, depth), BF)]
+        + [pltpu.VMEM((count, depth, hidden), BF), pltpu.VMEM((count, hidden, depth), BF)]
+        + [pltpu.VMEM((depth, hidden), BF), pltpu.VMEM((hidden, depth), BF)]
+        + [
+            pltpu.VMEM((TALL, width), F32),
+            pltpu.VMEM((TALL, width), F32),
+            pltpu.VMEM((TALL, depth), F32),
+            pltpu.VMEM((TALL, depth), F32),
+            pltpu.VMEM((TALL, depth), F32),
+            pltpu.VMEM((TALL, depth), F32),
+            pltpu.VMEM((TALL, depth), F32),
+            pltpu.VMEM((3, TALL, depth), F32),
+            pltpu.SemaphoreType.DMA((160,)),
+            pltpu.SemaphoreType.DMA((160,)),
+            pltpu.SemaphoreType.DMA((28,)),
+        ],
+        compiler_params=pltpu.CompilerParams(vmem_limit_bytes=BIG, collective_id=2, has_side_effects=True),
+        cost_estimate=pl.CostEstimate(flops=16 * 10**9, bytes_accessed=5 * 10**7, transcendentals=10**6),
+        name="tail",
+    )(back_all, gate_all, total_all, grads_in, grads_out, rows_all, flags_all, cot, x, middle, prob, attended, packed, normed, small, qkv, out)
+
+
 class Comm:
     def __init__(self):
         self.sizes = tuple(lax.axis_size(axis) for axis in AXES)
@@ -832,9 +1258,6 @@
             rows_all, flags_all, grad_rows, got_in, got_out,
         ) = head(x, cot, small, qkv_weight, out_weight, expert_in, expert_out, noise, ids)
         weights = (expert_in, got_in, expert_out, got_out)
-        mine = comm.pair * 4 + comm.tensor
-        sent = lax.dynamic_index_in_dim(rows_all, mine, 0, False)
-        flags = lax.dynamic_index_in_dim(flags_all, mine, 0, False)
     else:
         small = lax.all_gather(small, "shard", axis=1, tiled=True)
         small = small.reshape(TALL, 2, width // 2).transpose(1, 0, 2)
@@ -854,6 +1277,26 @@
 
         grad_rows, rows_all, flags_all = gather(cot), gather(sent), gather(flags)
     total, back_all, gate_all, grads_in, grads_out = expert_pass(place, rows_all, flags_all, grad_rows, *weights)
+
+    if comm.sizes[0] == 2:
+        mixed, grad_tokens, dense, grad_small, grad_in, grad_outer, _, _ = tail(
+            back_all, gate_all, total, grads_in, grads_out, rows_all, flags_all,
+            cot, x, middle, prob, attended, packed, normed_a, small, proj_qkv, proj_out,
+        )
+        dense = dense.astype(F32)
+        return (
+            unpad(mixed),
+            unpad(grad_tokens),
+            grad_small[experts],
+            grad_small[experts + 1],
+            dense[:, width:],
+            dense[:, :width],
+            grad_small[experts + 2],
+            grad_small[experts + 3],
+            grad_small[:experts].T,
+            grad_in.astype(F32),
+            grad_outer.astype(F32),
+        )
 
     def reduce_expert(grad, axis, other):
         part = comm.scatter_shard(grad, axis)

time: 631 us -> 397 us (0.63)
  Pallas kernels: 208 us -> 358 us
  starting transfers between devices: 145 us -> 0 us
  waiting for transfers between devices: 135 us -> 0 us
  other arithmetic: 60.8 us -> 9.55 us
  local copies, waits for them, and re-layouts: 71.8 us -> 20.7 us
    pallas_call x1, Pallas kernels: 26.4 us -> 187 us  [tail(): pl.pallas_call(tail_kernel, out_shape=(shape((rows, width), BF), shape((r...]
    ppermute x64 -> x0, starting transfers between devices: 145 us -> none  [move(): return lax.ppermute(value, AXES, pairs)]
    ppermute x64 -> x0, waiting for transfers between devices: 135 us -> none  [move(): return lax.ppermute(value, AXES, pairs)]
    add x17 -> x0, other arithmetic: 14.7 us -> none  [the longest x3 6.87 us: collect(): mine = mine.astype(F32) + self.over_core(other).astype(F32)]
    dynamic_slice x12 -> x0, local copies, waits for them, and re-layouts: 14.2 us -> none  [halves(): other = lax.dynamic_slice_in_dim(value, (1 - index) * size, size, axis)]
    dynamic_update_slice x4 -> x0, local copies, waits for them, and re-layouts: 14.2 us -> none  [local(): lax.dynamic_update_slice_in_dim(whole, pieces[k], (comm.tensor + 4 - k) %...]
    select_n x15 -> x0, other arithmetic: 14.1 us -> none  [the longest x12 13.1 us: join(): first = jnp.where(index == 0, mine, other)]
    unnamed x141 -> x10, local copies, waits for them, and re-layouts: 13.8 us -> 0.91 us
  transfers between devices with their start and end apart: 64 -> 0, of which waited for: 27 -> 0; matrix products, arithmetic and copies ran while one was open for 17% -> 0% of each run, Pallas kernels for 4% -> 0%
where the time goes in v4:
time: 397 us; the launch traced here: 389 us
  Pallas kernels  358 us (90%)
  local copies, waits for them, and re-layouts  20.7 us (5%)
  other arithmetic  9.55 us (2%)
    pallas_call x1, Pallas kernels, tail(): pl.pallas_call(tail_kernel, out_shape=(shape((rows, width), BF), shape((r...  187 us
    pallas_call x1, Pallas kernels, head(): pl.pallas_call(head_kernel, out_shape=(shape((2, TALL, depth), BF), shape...  95.7 us
    pallas_call x1, Pallas kernels, expert_pass(): pl.pallas_call(expert_kernel, out_shape=(shape((blocks, length, width), B...  74.8 us

profile of v4, /device:TPU:17, one launch (start us, length us, event | category | flops | bytes accessed | tf_op | source)
XLA Modules:
  0.0 388.9 jit_solution(10001098779272116843)
XLA Ops:
  1.2 0.7 broadcast_in_dim.12
  1.9 0.7 broadcast_in_dim.13
  2.6 0.7 broadcast_in_dim.14
  4.0 0.8 reshape.64
  4.7 0.7 concatenate.3
  6.1 0.7 reshape.65.ids_ref
  6.8 0.8 reshape.62
  7.6 0.7 reshape.63.noise_ref
  8.3 1.2 reshape.58
  9.5 0.9 pad.19
  10.4 1.2 reshape.60
  11.6 0.9 pad.20
  12.4 95.7 %head.1 = (bf16[2,16,384]{2,1,0:T(8,128)(2,1)}, bf16[768,2304]{1,0:T(8,128)(2,1)}, bf16[768,768]{1,0:T(8,128)(2,1)}, bf16[416,768]{1,0:T(8,128)(2,1)}, bf16[416,...) custom-call(bf16[416,768]{1,0:T(8,128)(2,1)} %bitcast.17, ...), custom_call_target="tpu_custom_call" | custom-call | flops 8000000000 | bytes 30000000 | tf_op jit(solution)/shard_map/head/pallas_call | solution.py:400
  108.2 74.8 %experts.1 = (bf16[8,416,768]{2,1,0:T(8,128)(2,1)}, bf16[8,416,768]{2,1,0:T(8,128)(2,1)}, bf16[8,16,416]{2,1,0:T(8,128)(2,1)}, bf16[4,768,768]{2,1,0:T(8,128)(2,1)}, bf16[4,768,768]{2,1,0:T(8,128)(2,1)}) custom-call(s32[2]{0:T(128)} %pad_add_fusion.place_ref, bf16[8,416,768]{2,1,0:T(8,128)(2,1)} %get-tuple-element.35.rows_ref.rows_all, ...), custom_call_target="tpu_custom_call" | custom-call | flops 49999998976 | bytes 50000000 | tf_op jit(solution)/shard_map/experts/pallas_call | solution.py:569
  183.0 187.3 %tail.1 = (bf16[416,768]{1,0:T(8,128)(2,1)}, bf16[416,768]{1,0:T(8,128)(2,1)}, bf16[384,3072]{1,0:T(8,128)(2,1)}, f32[16,384]{1,0:T(8,128)}, bf16[8,384,768]{2,1...) custom-call(bf16[8,416,768]{2,1,0:T(8,128)(2,1)} %get-tuple-element.40.ba, ...), custom_call_target="tpu_custom_call" | custom-call | flops 16000000000 | bytes 50000000 | tf_op jit(solution)/shard_map/tail/pallas_call | solution.py:1063
  370.3 1.3 slice.36
  371.5 0.9 reshape.67
  372.5 1.1 slice.37
  373.6 0.9 reshape.69
  375.8 1.1 slice.39
  376.9 2.0 slice.38
  378.9 0.9 copy-done.1
  379.8 4.6 %convert_element_type.17 = f32[8,384,768]{2,1,0:T(8,128)} convert(bf16[8,384,768]{2,1,0:T(8,128)(2,1)S(1)} %copy-done.1) | non-fusion elementwise | flops 2359296 | bytes 14155776 | tf_op jit(solution)/shard_map/convert_element_type | solution.py:1297
  384.4 4.4 %convert_element_type.18 = f32[8,768,384]{2,1,0:T(8,128)} convert(bf16[8,768,384]{2,1,0:T(8,128)(2,1)S(1)} %bitcast.16) | non-fusion elementwise | flops 2359296 | bytes 14155776 | tf_op jit(solution)/shard_map/convert_element_type | solution.py:1298
  (17 shorter events, 3.1 us)
Async XLA Ops:
  370.2 4.3 %copy-start.2 = (f32[16,384]{1,0:T(8,128)S(1)}, f32[16,384]{1,0:T(8,128)}, u32[]{:S(2)}) copy-start(f32[16,384]{1,0:T(8,128)} %get-tuple-element.55) | copy-start | bytes 73732
  370.3 5.5 %copy-start = (bf16[384,3072]{1,0:T(8,128)(2,1)S(1)}, bf16[384,3072]{1,0:T(8,128)(2,1)}, u32[]{:S(2)}) copy-start(bf16[384,3072]{1,0:T(8,128)(2,1)} %get-tuple-element.56) | copy-start | bytes 7077892
  375.8 4.0 %copy-start.1 = (bf16[8,384,768]{2,1,0:T(8,128)(2,1)S(1)}, bf16[8,384,768]{2,1,0:T(8,128)(2,1)}, u32[]{:S(2)}) copy-start(bf16[8,384,768]{2,1,0:T(8,128)(2,1)} %get-tuple-element.57) | copy-start | bytes 14155780
  376.9 7.5 %slice-start = ((s8[4718592]{0:T(1024)(128)(4,1)}), s8[4194304]{0:T(1024)(128)(4,1)S(1)}, s32[]{:S(2)}) async-start(s8[4718592]{0:T(1024)(128)(4,1)} %bitcast.15), calls=%async_computation | async-start | bytes 8388608
  379.8 4.6 %slice-start.1 = ((s8[4718592]{0:T(1024)(128)(4,1)}), s8[524288]{0:T(1024)(128)(4,1)S(1)}, s32[]{:S(2)}) async-start(s8[4718592]{0:T(1024)(128)(4,1)} %bitcast.15), calls=%async_computation.1 | async-start | bytes 1048576
